TPU v7x, 32 devices: a whole 2x2x4 slice. The times are simulated.
32 devices in a mesh: rep: 4 (over y, x), fsdp: 8 (over z, core).
Axes of the slice: x: 2, y: 2, z: 4, core: 2. Of those that a mesh axis runs over, the one named last changes fastest.
Arguments:
- images: bfloat16 [32, 12, 16, 512], P(('rep', 'fsdp')), may hold values from -6 to 6
- enc_first: bfloat16 [4608, 512], P('fsdp'), may hold values from -0.09375 to 0.09375
- enc_second: bfloat16 [4608, 512], P('fsdp'), may hold values from -0.09375 to 0.09375
- dec_first: bfloat16 [4608, 512], P('fsdp'), may hold values from -0.09375 to 0.09375
- dec_second: bfloat16 [4608, 512], P('fsdp'), may hold values from -0.09375 to 0.09375
- head_conv: bfloat16 [4608, 64], P('fsdp'), may hold values from -0.09375 to 0.09375
- head_out: bfloat16 [64, 17], P('fsdp'), may hold values from -0.75 to 0.75
- norm_gain: float32 [4, 512], replicated, may hold values from 0.1 to 1.9
- norm_bias: float32 [4, 512], replicated, may hold values from -3 to 3
- head_bias: float32 [64], replicated, may hold values from -3 to 3
- out_bias: float32 [17], replicated, may hold values from -3 to 3
- task_weights: float32 [3], replicated, may hold values from 0.5 to 2
- pool_index: int32 [32, 48], P(('rep', 'fsdp')), may hold values from 0 to 3
- labels: int32 [32, 192], P(('rep', 'fsdp')), may hold values from 0 to 12
- task_masks: int32 [32, 3, 192], P(('rep', 'fsdp')), may hold values from 0 to 1, as said below
- targets: float32 [32, 4, 192], P(('rep', 'fsdp')), may hold values from -6 to 6
Outputs:
- grad_images: float32 [32, 12, 16, 512], P(('rep', 'fsdp'))
- grad_enc_first: float32 [4608, 512], P('fsdp')
- grad_enc_second: float32 [4608, 512], P('fsdp')
- grad_dec_first: float32 [4608, 512], P('fsdp')
- grad_dec_second: float32 [4608, 512], P('fsdp')
- grad_head_conv: float32 [4608, 64], P('fsdp')
- grad_head_out: float32 [64, 17], P('fsdp')
- grad_norm_gain: float32 [4, 512], replicated
- grad_norm_bias: float32 [4, 512], replicated
- grad_head_bias: float32 [64], replicated
- grad_out_bias: float32 [17], replicated
Inputs may be any that keep to these rules, and one draw needn't show every extreme that they name: `pool_index`: position of the pooled value in its 2x2 window, 2 times row plus column. `task_masks`: 1 where a pixel counts for a task; each image has its own share for each task, from about an eighth to all of its pixels; pixel 0 of every image counts for every task.
All inputs are finite; a program needn't handle non-finite values.
Results may differ from a plain program's by a relative error of at most 0.02.
Values may be sent and summed in bfloat16 or wider, within the bound.
A program may use at most 192 MiB of HBM per device.

v0:
```python
import math

import jax
import jax.numpy as jnp
from jax import lax
from jax.sharding import PartitionSpec as P

eps = 1e-05


def shifted_windows(source):
    height, breadth = (source.shape[1], source.shape[2])
    padded = jnp.pad(source, ((0, 0), (1, 1), (1, 1), (0, 0)))
    return [
        padded[:, position // 3 : position // 3 + height, position % 3 : position % 3 + breadth, :]
        for position in range(9)
    ]


def conv_forward(source, weight):
    channels = source.shape[3]
    summed = None
    for position, window in enumerate(shifted_windows(source)):
        partial_value = jnp.einsum(
            "nhwc,cd->nhwd",
            window,
            weight[position * channels : (position + 1) * channels],
            preferred_element_type=jnp.float32,
        )
        summed = partial_value if summed is None else summed + partial_value
    return summed


def conv_data_grad(grad_low, weight):
    images_n, height, breadth = (grad_low.shape[0], grad_low.shape[1], grad_low.shape[2])
    channels = weight.shape[0] // 9
    padded = jnp.zeros((images_n, height + 2, breadth + 2, channels), jnp.float32)
    for position in range(9):
        row_at, col_at = (position // 3, position % 3)
        backed = jnp.einsum(
            "nhwd,cd->nhwc",
            grad_low,
            weight[position * channels : (position + 1) * channels],
            preferred_element_type=jnp.float32,
        )
        padded = padded.at[:, row_at : row_at + height, col_at : col_at + breadth, :].add(backed)
    return padded[:, 1:-1, 1:-1, :]


def conv_weight_grad(source, grad_low):
    return jnp.concatenate(
        [
            jnp.einsum("nhwc,nhwd->cd", window, grad_low, preferred_element_type=jnp.float32)
            for window in shifted_windows(source)
        ],
        axis=0,
    )


def silu_slope(before):
    squashed = jax.nn.sigmoid(before)
    return squashed + before * squashed * (1.0 - squashed)


def moments(conv_out, population, rider):
    first_part = jnp.sum(conv_out, axis=(0, 1, 2))
    rider_sum = None
    if rider is None:
        first_sum = lax.psum(first_part, ("rep", "fsdp"))
    else:
        first_sum, rider_sum = lax.psum((first_part, rider), ("rep", "fsdp"))
    mean_val = first_sum / population
    centered = jnp.sum(jnp.square(conv_out - mean_val), axis=(0, 1, 2))
    spread = lax.psum(centered, ("rep", "fsdp")) / population
    return (mean_val, spread, rider_sum)


def per_device(
    images,
    enc_first,
    enc_second,
    dec_first,
    dec_second,
    head_conv,
    head_out,
    norm_gain,
    norm_bias,
    head_bias,
    out_bias,
    task_weights,
    pool_index,
    labels,
    task_masks,
    targets,
):
    images_n, height, breadth, channels = images.shape
    half_h, half_w = (height // 2, breadth // 2)
    population = float(images_n * height * breadth * lax.axis_size("rep") * lax.axis_size("fsdp"))
    root_pop = math.sqrt(population)
    classes = out_bias.shape[0] - 4
    enc_full = (
        lax.all_gather(enc_first, "fsdp", axis=0, tiled=True),
        lax.all_gather(enc_second, "fsdp", axis=0, tiled=True),
    )
    dec_full = (
        lax.all_gather(dec_first, "fsdp", axis=0, tiled=True),
        lax.all_gather(dec_second, "fsdp", axis=0, tiled=True),
        lax.all_gather(head_conv, "fsdp", axis=0, tiled=True),
        lax.all_gather(head_out, "fsdp", axis=0, tiled=True),
    )
    kernels = [enc_full[0], enc_full[1], dec_full[0], dec_full[1]]
    mask_float = task_masks.astype(jnp.float32)
    count_part = jnp.sum(mask_float, axis=(0, 2))
    picks = (
        pool_index.reshape(images_n, half_h, half_w, 1) == jnp.arange(4, dtype=jnp.int32)
    ).astype(jnp.float32)
    sources, normed_list, inverse_list, shaped_list = ([], [], [], [])
    source = images
    counts = None
    pooled = None
    for number in range(4):
        if number == 2:
            placed = pooled[:, :, :, None, :] * picks[:, :, :, :, None]
            placed = placed.reshape(images_n, half_h, half_w, 2, 2, channels)
            source = (
                jnp.transpose(placed, (0, 1, 3, 2, 4, 5))
                .reshape(images_n, height, breadth, channels)
                .astype(jnp.bfloat16)
            )
        conv_out = conv_forward(source, kernels[number])
        if number == 0:
            mean_val, spread, counts = moments(conv_out, population, count_part)
        else:
            mean_val, spread, ignored = moments(conv_out, population, None)
        inverse = lax.rsqrt(spread + eps)
        normed = (conv_out - mean_val) * inverse
        shaped = normed * norm_gain[number] + norm_bias[number]
        hidden = jax.nn.silu(shaped)
        sources.append(source)
        normed_list.append(normed)
        inverse_list.append(inverse)
        shaped_list.append(shaped)
        if number == 1:
            pooled = jnp.mean(hidden.reshape(images_n, half_h, 2, half_w, 2, channels), axis=(2, 4))
        else:
            source = hidden.astype(jnp.bfloat16)
    out_weight = dec_full[3].astype(jnp.float32)
    head_raw = conv_forward(source, dec_full[2]) + head_bias
    head_act = jax.nn.silu(head_raw)
    outputs = (
        jnp.einsum("nhwc,cd->nhwd", head_act, out_weight, precision=lax.Precision.HIGHEST)
        + out_bias
    )
    outputs = outputs.reshape(images_n, height * breadth, outputs.shape[3])
    factor = population * task_weights / counts
    logits = outputs[:, :, :classes]
    likely = jax.nn.softmax(logits, axis=-1)
    onehot = (labels[:, :, None] == jnp.arange(classes, dtype=jnp.int32)).astype(jnp.float32)
    grad_logits = (factor[0] * mask_float[:, 0])[:, :, None] * (likely - onehot)
    misfit = outputs[:, :, classes] - targets[:, 0]
    grad_depth = factor[1] * mask_float[:, 1] * misfit / jnp.sqrt(misfit * misfit + 1.0)
    predicted = outputs[:, :, classes + 1 :]
    wanted = jnp.transpose(targets[:, 1:], (0, 2, 1))
    radius = jnp.sqrt(jnp.sum(predicted * predicted, axis=-1) + 1.0)
    aligned = jnp.sum(predicted * wanted, axis=-1)
    grad_normal = -(factor[2] * mask_float[:, 2])[:, :, None] * (
        wanted / radius[:, :, None] - (aligned / (radius * radius * radius))[:, :, None] * predicted
    )
    grad_output = jnp.concatenate(
        [grad_logits, grad_depth[:, :, None], grad_normal], axis=-1
    ).reshape(images_n, height, breadth, out_bias.shape[0])
    back_enc = (
        lax.all_gather(enc_first, "fsdp", axis=0, tiled=True),
        lax.all_gather(enc_second, "fsdp", axis=0, tiled=True),
    )
    back_dec = (
        lax.all_gather(dec_first, "fsdp", axis=0, tiled=True),
        lax.all_gather(dec_second, "fsdp", axis=0, tiled=True),
        lax.all_gather(head_conv, "fsdp", axis=0, tiled=True),
        lax.all_gather(head_out, "fsdp", axis=0, tiled=True),
    )
    back_kernels = [back_enc[0], back_enc[1], back_dec[0], back_dec[1]]
    back_out = back_dec[3].astype(jnp.float32)
    out_bias_part = jnp.sum(grad_output, axis=(0, 1, 2))
    head_out_term = jnp.einsum(
        "nhwc,nhwd->cd", head_act, grad_output, precision=lax.Precision.HIGHEST
    )
    grad_head_act = jnp.einsum(
        "nhwd,cd->nhwc", grad_output, back_out, precision=lax.Precision.HIGHEST
    )
    grad_head_low = (grad_head_act * silu_slope(head_raw)).astype(jnp.bfloat16)
    head_bias_part = jnp.sum(grad_head_low.astype(jnp.float32), axis=(0, 1, 2))
    head_conv_term = conv_weight_grad(source, grad_head_low)
    grad_hidden = conv_data_grad(grad_head_low, back_dec[2])
    weight_terms = [None, None, None, None]
    gain_sums = [None, None, None, None]
    bias_sums = [None, None, None, None]
    head_bias_sum = None
    out_bias_sum = None
    dec_shards = None
    for number in (3, 2, 1, 0):
        grad_shaped = grad_hidden * silu_slope(shaped_list[number])
        part_bias = jnp.sum(grad_shaped, axis=(0, 1, 2))
        part_gain = jnp.sum(grad_shaped * normed_list[number], axis=(0, 1, 2))
        if number == 3:
            bias_sum, gain_sum, head_bias_sum, out_bias_sum = lax.psum(
                (part_bias, part_gain, head_bias_part, out_bias_part), ("rep", "fsdp")
            )
        else:
            bias_sum, gain_sum = lax.psum((part_bias, part_gain), ("rep", "fsdp"))
        bias_sums[number] = bias_sum
        gain_sums[number] = gain_sum
        grad_conv = (
            inverse_list[number]
            * norm_gain[number]
            * (grad_shaped - bias_sum / population - normed_list[number] * gain_sum / population)
        )
        grad_low = grad_conv.astype(jnp.bfloat16)
        weight_terms[number] = conv_weight_grad(sources[number], grad_low)
        if number == 2:
            dec_shards = (
                lax.psum_scatter(weight_terms[2], "fsdp", scatter_dimension=0, tiled=True),
                lax.psum_scatter(weight_terms[3], "fsdp", scatter_dimension=0, tiled=True),
                lax.psum_scatter(head_conv_term, "fsdp", scatter_dimension=0, tiled=True),
                lax.psum_scatter(head_out_term, "fsdp", scatter_dimension=0, tiled=True),
            )
        grad_source = conv_data_grad(grad_low, back_kernels[number])
        if number == 2:
            regroup = jnp.transpose(
                grad_source.reshape(images_n, half_h, 2, half_w, 2, channels), (0, 1, 3, 2, 4, 5)
            ).reshape(images_n, half_h, half_w, 4, channels)
            grad_pooled = jnp.sum(regroup * picks[:, :, :, :, None], axis=3)
            grad_hidden = jnp.broadcast_to(
                0.25 * grad_pooled[:, :, None, :, None, :],
                (images_n, half_h, 2, half_w, 2, channels),
            ).reshape(images_n, height, breadth, channels)
        else:
            grad_hidden = grad_source
    enc_shards = (
        lax.psum_scatter(weight_terms[0], "fsdp", scatter_dimension=0, tiled=True),
        lax.psum_scatter(weight_terms[1], "fsdp", scatter_dimension=0, tiled=True),
    )
    summed = (
        lax.psum(enc_shards[0].astype(jnp.bfloat16), "rep").astype(jnp.float32),
        lax.psum(enc_shards[1].astype(jnp.bfloat16), "rep").astype(jnp.float32),
        lax.psum(dec_shards[0].astype(jnp.bfloat16), "rep").astype(jnp.float32),
        lax.psum(dec_shards[1].astype(jnp.bfloat16), "rep").astype(jnp.float32),
        lax.psum(dec_shards[2].astype(jnp.bfloat16), "rep").astype(jnp.float32),
        lax.psum(dec_shards[3].astype(jnp.bfloat16), "rep").astype(jnp.float32),
    )
    return (
        grad_hidden,
        summed[0] / root_pop,
        summed[1] / root_pop,
        summed[2] / root_pop,
        summed[3] / root_pop,
        summed[4] / root_pop,
        summed[5] / root_pop,
        jnp.stack(gain_sums, axis=0) / root_pop,
        jnp.stack(bias_sums, axis=0) / root_pop,
        head_bias_sum / root_pop,
        out_bias_sum / root_pop,
    )


def solution(mesh):
    placed = (
        P(("rep", "fsdp"), None, None, None),
        P("fsdp", None),
        P("fsdp", None),
        P("fsdp", None),
        P("fsdp", None),
        P("fsdp", None),
        P("fsdp", None),
        P(),
        P(),
        P(),
        P(),
        P(),
        P(("rep", "fsdp"), None),
        P(("rep", "fsdp"), None),
        P(("rep", "fsdp"), None, None),
        P(("rep", "fsdp"), None, None),
    )
    return jax.shard_map(
        per_device,
        mesh=mesh,
        in_specs=placed,
        out_specs=(
            P(("rep", "fsdp"), None, None, None),
            P("fsdp", None),
            P("fsdp", None),
            P("fsdp", None),
            P("fsdp", None),
            P("fsdp", None),
            P("fsdp", None),
            P(),
            P(),
            P(),
            P(),
        ),
        check_vma=False,
    )
```

profile of v0, /device:TPU:0, one launch (start us, length us, event | category | flops | bytes accessed | tf_op | source)
XLA Modules:
  0.0 1290.7 jit_solution(3718472713178442489)
XLA Ops:
  16.6 14.8 %all_gather.29 = bf16[64,17]{1,0:T(8,128)(2,1)S(1)} all-gather(bf16[8,17]{1,0:T(8,128)(2,1)} %param.112), channel_id=1, replica_groups=mesh['rep'=4,'fsdp'=8] {'fsdp'}, dimensions={0}, use_global_device_ids=true | all-gather | bytes 2448 | tf_op jit(solution)/shard_map/all_gather | solution.py:109
  31.4 18.1 %all-gather = bf16[8,576,64]{1,2,0:T(8,128)(2,1)S(1)} all-gather(bf16[1,576,64]{1,2,0:T(8,128)(2,1)} %bitcast.984), channel_id=1, replica_groups=mesh['rep'=4,'fsdp'=8] {'fsdp'}, dimensions={0}, use_global_device_ids=true | all-gather | bytes 663552 | tf_op jit(solution)/shard_map/all_gather | solution.py:108
  51.1 18.2 %all-gather.6.cloned.1.call-done = bf16[4608,512]{1,0:T(8,128)(2,1)} async-done(((bf16[576,512]{1,0:T(8,128)(2,1)}), bf16[4608,512]{1,0:T(8,128)(2,1)}) %all-gather.6.cloned.1.call-update) | async-done | bytes 4718608 | tf_op jit(solution)/shard_map/all_gather | solution.py:102
  76.2 42.6 %psum.175 = f32[512]{0:T(512)S(1)} all-reduce(f32[512]{0:T(512)S(1)} %get-tuple-element.611), channel_id=1, replica_groups=mesh['rep'=4,'fsdp'=8] {'rep','fsdp'}, use_global_device_ids=true, to_apply=%region_1.2 | all-reduce | flops 512 | bytes 4096 | tf_op jit(solution)/shard_map/psum | solution.py:71
  118.9 41.1 %psum.176 = f32[512]{0:T(512)S(1)} all-reduce(f32[512]{0:T(512)S(1)} %multiply_reduce_fusion.4), channel_id=1, replica_groups=mesh['rep'=4,'fsdp'=8] {'rep','fsdp'}, use_global_device_ids=true, to_apply=%region_3.4 | all-reduce | flops 512 | bytes 4096 | tf_op jit(solution)/shard_map/psum | solution.py:74
  167.8 43.0 %psum.177 = f32[512]{0:T(512)S(1)} all-reduce(f32[512]{0:T(512)S(1)} %get-tuple-element.613), channel_id=1, replica_groups=mesh['rep'=4,'fsdp'=8] {'rep','fsdp'}, use_global_device_ids=true, to_apply=%region_5.6 | all-reduce | flops 512 | bytes 4096 | tf_op jit(solution)/shard_map/psum | solution.py:69
  210.8 39.3 %psum.178 = f32[512]{0:T(512)S(1)} all-reduce(f32[512]{0:T(512)S(1)} %multiply_reduce_fusion.3), channel_id=1, replica_groups=mesh['rep'=4,'fsdp'=8] {'rep','fsdp'}, use_global_device_ids=true, to_apply=%region_7.8 | all-reduce | flops 512 | bytes 4096 | tf_op jit(solution)/shard_map/psum | solution.py:74
  258.8 40.7 %psum.179 = f32[512]{0:T(512)S(1)} all-reduce(f32[512]{0:T(512)S(1)} %get-tuple-element.615), channel_id=1, replica_groups=mesh['rep'=4,'fsdp'=8] {'rep','fsdp'}, use_global_device_ids=true, to_apply=%region_10.11 | all-reduce | flops 512 | bytes 4096 | tf_op jit(solution)/shard_map/psum | solution.py:69
  299.6 40.0 %psum.180 = f32[512]{0:T(512)S(1)} all-reduce(f32[512]{0:T(512)S(1)} %multiply_reduce_fusion.2), channel_id=1, replica_groups=mesh['rep'=4,'fsdp'=8] {'rep','fsdp'}, use_global_device_ids=true, to_apply=%region_12.13 | all-reduce | flops 512 | bytes 4096 | tf_op jit(solution)/shard_map/psum | solution.py:74
  347.3 40.5 %psum.181 = f32[512]{0:T(512)S(1)} all-reduce(f32[512]{0:T(512)S(1)} %get-tuple-element.617), channel_id=1, replica_groups=mesh['rep'=4,'fsdp'=8] {'rep','fsdp'}, use_global_device_ids=true, to_apply=%region_14.15 | all-reduce | flops 512 | bytes 4096 | tf_op jit(solution)/shard_map/psum | solution.py:69
  387.9 39.5 %all-reduce.15 = (f32[512]{0:T(512)S(1)}, f32[3]{0:T(128)}) all-reduce(f32[512]{0:T(512)S(1)} %multiply_reduce_fusion.1, f32[3]{0:T(128)S(1)} %convert_reduce_fusion.1), channel_id=1, replica_groups=mesh['rep'=4,'fsdp'=8] {'rep','fsdp'}, use_global_device_ids=true, to_apply=%region_16.17 | all-reduce | flops 515 | bytes 4120 | tf_op jit(solution)/shard_map/psum | solution.py:74
  449.3 3.9 scatter-add.151
  453.2 3.6 fusion.38
  456.8 3.8 scatter-add.154
  480.9 40.8 %all-reduce.14 = (f32[512]{0:T(512)S(1)}, f32[512]{0:T(512)S(1)}) all-reduce(f32[512]{0:T(512)S(1)} %get-tuple-element.558, f32[512]{0:T(512)S(1)} %get-tuple-element.557), channel_id=1, replica_groups=mesh['rep'=4,'fsdp'=8] {'rep','fsdp'}, use_global_device_ids=true, to_apply=%region_27.28 | all-reduce | flops 1024 | bytes 8192 | tf_op jit(solution)/shard_map/psum | solution.py:206
  524.8 3.4 fusion.47
  528.3 3.9 scatter-add.166
  552.6 39.8 %all-reduce.13 = (f32[512]{0:T(512)S(1)}, f32[512]{0:T(512)S(1)}) all-reduce(f32[512]{0:T(512)} %get-tuple-element.556, f32[512]{0:T(512)} %get-tuple-element.555), channel_id=1, replica_groups=mesh['rep'=4,'fsdp'=8] {'rep','fsdp'}, use_global_device_ids=true, to_apply=%region_31.32 | all-reduce | flops 1024 | bytes 8192 | tf_op jit(solution)/shard_map/psum | solution.py:210
  595.2 3.4 fusion.58
  598.7 3.9 scatter-add.181
  602.6 3.9 fusion.60
  606.5 3.8 scatter-add.184
  635.4 40.7 %all-reduce.12 = (f32[512]{0:T(512)S(1)}, f32[512]{0:T(512)S(1)}) all-reduce(f32[512]{0:T(512)S(1)} %get-tuple-element.554, f32[512]{0:T(512)S(1)} %get-tuple-element.553), channel_id=1, replica_groups=mesh['rep'=4,'fsdp'=8] {'rep','fsdp'}, use_global_device_ids=true, to_apply=%region_36.37 | all-reduce | flops 1024 | bytes 8192 | tf_op jit(solution)/shard_map/psum | solution.py:210
  709.8 39.6 %all-reduce.11 = (f32[512]{0:T(512)S(1)}, f32[512]{0:T(512)S(1)}, f32[64]{0:T(128)S(1)}, f32[17]{0:T(128)S(1)}) all-reduce(f32[512]{0:T(512)S(1)} %get-tuple-element.552, f32[512]{0:T(512)S(1)} %get-tuple-element.551, f32[64]{0:T(128)S(1)} %copy-done.49, f32[17]{0:T(128)S(1)} %copy-done.48), channel_id=1, replica_groups=mesh['rep'=4,'fsdp'=8] {'rep','fsdp'}, use_global_device_ids=true, to_apply=%region_40.41 | all-reduce | flops 1105 | bytes 8840 | tf_op jit(solution)/shard_map/psum | solution.py:210
  816.5 3.2 fusion.82
  823.9 72.5 %reduce-scatter.8.cloned.1.call-done = f32[576,512]{1,0:T(8,128)} async-done(((f32[4608,512]{1,0:T(8,128)}), f32[576,512]{1,0:T(8,128)}) %reduce-scatter.8.cloned.1.call-update) | async-done | bytes 1179664 | tf_op jit(solution)/shard_map/reduce_scatter | solution.py:240
  898.6 98.0 %reduce-scatter.10.cloned.1.call-done = f32[576,512]{1,0:T(8,128)} async-done(((f32[4608,512]{1,0:T(8,128)}), f32[576,512]{1,0:T(8,128)}) %reduce-scatter.10.cloned.1.call-update) | async-done | bytes 1179664 | tf_op jit(solution)/shard_map/reduce_scatter | solution.py:241
  998.8 98.0 %reduce-scatter.12.cloned.1.call-done = f32[576,512]{1,0:T(8,128)} async-done(((f32[4608,512]{1,0:T(8,128)}), f32[576,512]{1,0:T(8,128)}) %reduce-scatter.12.cloned.1.call-update) | async-done | bytes 1179664 | tf_op jit(solution)/shard_map/reduce_scatter | solution.py:222
  1099.0 98.1 %reduce-scatter.14.cloned.1.call-done = f32[576,512]{1,0:T(8,128)} async-done(((f32[4608,512]{1,0:T(8,128)}), f32[576,512]{1,0:T(8,128)}) %reduce-scatter.14.cloned.1.call-update) | async-done | bytes 1179664 | tf_op jit(solution)/shard_map/reduce_scatter | solution.py:223
  1213.7 26.0 %all-reduce.10 = bf16[64,17]{1,0:T(8,128)(2,1)S(1)} all-reduce(f32[64,17]{1,0:T(8,128)S(1)} %convolution_bitcast_fusion.90), channel_id=7, replica_groups=mesh['rep'=4,'fsdp'=8] {'fsdp'}, use_global_device_ids=true, to_apply=%region_51.52.clone | all-reduce | flops 1088 | bytes 6528
  1239.6 10.1 psum.197
  1252.0 23.9 %all-reduce.19.cloned.1.call-done = (bf16[576,512]{1,0:T(8,128)(2,1)}, bf16[576,512]{1,0:T(8,128)(2,1)}, bf16[576,512]{1,0:T(8,128)(2,1)}, bf16[576,512]{1,0:T(8,128)(2,1)}, bf16[576,64]{0,1:T(8,128)(2,1)}) async-done(((bf16[576,512]{1,0:T(8,128)(2,1)}, bf16[576,512]{1,0:T(8,128)(2,1)}, bf16[576,512]{1,0:T(8,128)(2,1)}, bf16[576,512]{1,0:T(8,128)(2,1)}, bf16[576,64]{0,1:T(8,128)(2,1)}), ...) | async-done | bytes 2433040 | tf_op jit(solution)/shard_map/psum | solution.py:244
  (383 shorter events, 271.8 us)
Async XLA Ops:
  7.2 43.2 %copy-start.50 = (s32[4]{0:T(128)S(1)}, s32[4]{0:T(128)}, u32[]{:S(2)}) copy-start(s32[4]{0:T(128)} %constant.1079.clone.1) | copy-start | bytes 52
  7.2 62.1 %copy-start = (bf16[1,12,16,512]{3,2,1,0:T(8,128)(2,1)S(1)}, bf16[1,12,16,512]{3,2,1,0:T(8,128)(2,1)}, u32[]{:S(2)}) copy-start(bf16[1,12,16,512]{3,2,1,0:T(8,128)(2,1)} %param.106) | copy-start | bytes 589828
  7.2 62.1 %all-gather.6.cloned.1.call-start = ((), (), s32[]{:S(2)}) async-start(), calls=%async_computation.5 | async-start | bytes 5308416 | tf_op jit(solution)/shard_map/all_gather | solution.py:102
  7.9 152.8 %all-gather.8.cloned.1.call-start = ((), (), s32[]{:S(2)}) async-start(), calls=%async_computation.6 | async-start | bytes 5308416 | tf_op jit(solution)/shard_map/all_gather | solution.py:103
  8.7 243.1 %all-gather.10.cloned.1.call-start = ((), (), s32[]{:S(2)}) async-start(), calls=%async_computation.7 | async-start | bytes 5308416 | tf_op jit(solution)/shard_map/all_gather | solution.py:106
  9.4 330.9 %all-gather.12.cloned.1.call-start = ((), (), s32[]{:S(2)}) async-start(), calls=%async_computation.8 | async-start | bytes 5308416 | tf_op jit(solution)/shard_map/all_gather | solution.py:107
  10.0 812.2 %reduce-scatter.16.cloned.1.call-start = ((), (), s32[]{:S(2)}) async-start(), calls=%async_computation.13 | async-start | bytes 2654208
  15.6 150.7 %copy-start.28 = (f32[1,512]{1,0:T(1,128)}, f32[1,512]{1,0:T(1,128)S(1)}, u32[]{:S(2)}) copy-start(f32[1,512]{1,0:T(1,128)S(1)} %get-tuple-element.586) | copy-start | bytes 6148
  15.6 235.1 %copy-start.30 = (f32[1,512]{1,0:T(1,128)}, f32[1,512]{1,0:T(1,128)S(1)}, u32[]{:S(2)}) copy-start(f32[1,512]{1,0:T(1,128)S(1)} %get-tuple-element.585) | copy-start | bytes 6148
  15.6 330.2 %copy-start.26 = (f32[1,512]{1,0:T(1,128)}, f32[1,512]{1,0:T(1,128)S(1)}, u32[]{:S(2)}) copy-start(f32[1,512]{1,0:T(1,128)S(1)} %get-tuple-element.587) | copy-start | bytes 6148
  15.7 412.5 %copy-start.17 = (f32[1,512]{1,0:T(1,128)}, f32[1,512]{1,0:T(1,128)S(1)}, u32[]{:S(2)}) copy-start(f32[1,512]{1,0:T(1,128)S(1)} %get-tuple-element.584) | copy-start | bytes 6148
  16.5 149.8 %copy-start.34 = (f32[1,512]{1,0:T(1,128)}, f32[1,512]{1,0:T(1,128)S(1)}, u32[]{:S(2)}) copy-start(f32[1,512]{1,0:T(1,128)S(1)} %get-tuple-element.590) | copy-start | bytes 6148
  16.5 234.2 %copy-start.36 = (f32[1,512]{1,0:T(1,128)}, f32[1,512]{1,0:T(1,128)S(1)}, u32[]{:S(2)}) copy-start(f32[1,512]{1,0:T(1,128)S(1)} %get-tuple-element.589) | copy-start | bytes 6148
  16.6 329.3 %copy-start.32 = (f32[1,512]{1,0:T(1,128)}, f32[1,512]{1,0:T(1,128)S(1)}, u32[]{:S(2)}) copy-start(f32[1,512]{1,0:T(1,128)S(1)} %get-tuple-element.591) | copy-start | bytes 6148
  16.6 411.6 %copy-start.24 = (f32[1,512]{1,0:T(1,128)}, f32[1,512]{1,0:T(1,128)S(1)}, u32[]{:S(2)}) copy-start(f32[1,512]{1,0:T(1,128)S(1)} %get-tuple-element.588) | copy-start | bytes 6148
  31.4 399.4 %copy-start.37 = (bf16[64,17]{1,0:T(8,128)(2,1)}, bf16[64,17]{1,0:T(8,128)(2,1)S(1)}, u32[]{:S(2)}) copy-start(bf16[64,17]{1,0:T(8,128)(2,1)S(1)} %all_gather.29) | copy-start | bytes 6532
  50.4 394.7 %copy-start.5 = (bf16[4608,64]{0,1:T(8,128)(2,1)}, bf16[4608,64]{0,1:T(8,128)(2,1)S(1)}, u32[]{:S(2)}) copy-start(bf16[4608,64]{0,1:T(8,128)(2,1)S(1)} %reshape.2720) | copy-start | bytes 1769476
  346.8 90.5 %copy-start.31 = (f32[1,4,192]{2,1,0:T(4,128)S(1)}, f32[1,4,192]{2,1,0:T(4,128)}, u32[]{:S(2)}) copy-start(f32[1,4,192]{2,1,0:T(4,128)} %param.121) | copy-start | bytes 9220
  456.8 23.1 %copy-start.25 = (f32[1,512]{1,0:T(1,128)S(1)}, f32[1,512]{1,0:T(1,128)}, u32[]{:S(2)}) copy-start(f32[1,512]{1,0:T(1,128)} %copy-done.24) | copy-start | bytes 6148
  460.6 61.7 %copy-start.43 = (f32[512]{0:T(512)S(1)}, f32[512]{0:T(512)}, u32[]{:S(2)}) copy-start(f32[512]{0:T(512)} %get-tuple-element.600) | copy-start | bytes 6148
  695.5 56.5 %copy-start.7 = (bf16[12,16,512]{2,1,0:T(8,128)(2,1)S(1)}, bf16[12,16,512]{2,1,0:T(8,128)(2,1)}, u32[]{:S(2)}) copy-start(bf16[12,16,512]{2,1,0:T(8,128)(2,1)} %copy-done.6) | copy-start | bytes 589828
  709.8 49.5 %copy-start.8 = (f32[1,12,16,512]{3,2,1,0:T(8,128)S(1)}, f32[1,12,16,512]{3,2,1,0:T(8,128)}, u32[]{:S(2)}) copy-start(f32[1,12,16,512]{3,2,1,0:T(8,128)} %get-tuple-element.580) | copy-start | bytes 1179652
  709.8 49.5 %copy-start.42 = (f32[512]{0:T(512)S(1)}, f32[512]{0:T(512)}, u32[]{:S(2)}) copy-start(f32[512]{0:T(512)} %get-tuple-element.594) | copy-start | bytes 6148
  759.2 137.2 %reduce-scatter.8.cloned.1.call-start = ((), (), s32[]{:S(2)}) async-start(), calls=%async_computation.9 | async-start | bytes 10616832 | tf_op jit(solution)/shard_map/reduce_scatter | solution.py:240
  771.5 225.1 %reduce-scatter.10.cloned.1.call-start = ((), (), s32[]{:S(2)}) async-start(), calls=%async_computation.10 | async-start | bytes 10616832 | tf_op jit(solution)/shard_map/reduce_scatter | solution.py:241
  783.5 313.3 %reduce-scatter.12.cloned.1.call-start = ((), (), s32[]{:S(2)}) async-start(), calls=%async_computation.11 | async-start | bytes 10616832 | tf_op jit(solution)/shard_map/reduce_scatter | solution.py:222
  795.8 401.2 %reduce-scatter.14.cloned.1.call-start = ((), (), s32[]{:S(2)}) async-start(), calls=%async_computation.12 | async-start | bytes 10616832 | tf_op jit(solution)/shard_map/reduce_scatter | solution.py:223
  807.9 468.0 %all-reduce.19.cloned.1.call-start = ((), (), s32[]{:S(2)}) async-start(), calls=%async_computation.14 | async-start | bytes 4882432 | tf_op jit(solution)/shard_map/psum | solution.py:244
  1203.2 46.5 %copy-start.39 = (f32[512]{0:T(512)S(1)}, f32[512]{0:T(512)}, u32[]{:S(2)}) copy-start(f32[512]{0:T(512)} %copy-done.38) | copy-start | bytes 6148
  1203.2 46.5 %copy-start.41 = (f32[512]{0:T(512)S(1)}, f32[512]{0:T(512)}, u32[]{:S(2)}) copy-start(f32[512]{0:T(512)} %copy-done.40) | copy-start | bytes 6148
  1203.2 46.5 %copy-start.45 = (f32[512]{0:T(512)S(1)}, f32[512]{0:T(512)}, u32[]{:S(2)}) copy-start(f32[512]{0:T(512)} %copy-done.44) | copy-start | bytes 6148
  1203.3 46.5 %copy-start.47 = (f32[512]{0:T(512)S(1)}, f32[512]{0:T(512)}, u32[]{:S(2)}) copy-start(f32[512]{0:T(512)} %copy-done.46) | copy-start | bytes 6148
  (31 other events, 265.0 us)
Sparse Core Ops, SparseCore 0:
  9.7 59.6 all-gather.5
  71.0 51.4 all-gather.7
  124.1 51.5 all-gather.9
  177.2 51.0 all-gather.11
  759.3 36.1 reduce-scatter.15
  797.7 98.6 reduce-scatter.7
  898.7 97.8 reduce-scatter.9
  998.9 97.8 reduce-scatter.11
  1099.1 97.8 reduce-scatter.13
  1201.1 74.7 all-reduce.18
where the time goes:
time: 1300 us; the launch traced here: 1290 us
  blocking collectives  557 us (43%)
  waiting for transfers between devices  411 us (32%)
  matrix products  174 us (13%)
  local copies, waits for them, and re-layouts  92.6 us (7%)
  other arithmetic  38.8 us (3%)
  between operations  16.8 us (1%)
    psum x4, blocking collectives, moments(): spread = lax.psum(centered, ('rep', 'fsdp')) / population  160 us
    psum x3, blocking collectives, moments(): first_sum = lax.psum(first_part, ('rep', 'fsdp'))  124 us
    psum x3, blocking collectives, per_device(): bias_sum, gain_sum = lax.psum((part_bias, part_gain), ('rep', 'fsdp'))  120 us
    reduce_scatter x1, waiting for transfers between devices, per_device(): lax.psum_scatter(weight_terms[3], 'fsdp', scatter_dimension=0, tiled=True)  98.1 us
    reduce_scatter x1, waiting for transfers between devices, per_device(): lax.psum_scatter(weight_terms[2], 'fsdp', scatter_dimension=0, tiled=True)  98 us
    reduce_scatter x1, waiting for transfers between devices, per_device(): lax.psum_scatter(weight_terms[1], 'fsdp', scatter_dimension=0, tiled=True)  98 us
    dot_general x45, matrix products, conv_data_grad(): jnp.einsum('nhwd,cd->nhwc', grad_low, weight[position * channels:(positio...  85.3 us
    reduce_scatter x1, waiting for transfers between devices, per_device(): lax.psum_scatter(weight_terms[0], 'fsdp', scatter_dimension=0, tiled=True)  72.5 us
  transfers between devices with their start and end apart: 10, of which 6 were waited for; matrix products, arithmetic and copies ran while one was open for 9% of the time, Pallas kernels for 0%

commit v1 on v0

v1 whole, which is shorter than its diff:
```python
import functools
import math
import types

import jax
import jax.numpy as jnp
from jax import lax
from jax.experimental import pallas as pl
from jax.experimental.pallas import tpu as pltpu
from jax.sharding import PartitionSpec as P

MESH = pl.DeviceIdType.MESH
F32, BF16 = jnp.float32, jnp.bfloat16
EPS = 1e-05
LANES = 128
EXACT = lax.Precision.HIGHEST

GROUPS = (
    ["images", "start", "head_out", "a2a", "pool", "dh3", "rs3", "rs2", "rs1", "rs0", "norms", "small_rep", "small_all"]
    + [f"ag{i}" for i in (0, 2)]
    + [f"stat{i}" for i in range(8)]
    + [f"core{i}" for i in range(5)]
    + [f"z{i}" for i in range(5)]
    + [f"rows{i}" for i in range(5)]
    + [f"own{i}" for i in range(5)]
    + ["own_image"]
)
GROUP = {name: number for number, name in enumerate(GROUPS)}


def kernel(d, *refs):
    it = iter(refs)
    take = lambda count: [next(it) for _ in range(count)]
    images, w0, w1, w2, w3, hw, ho, gain, shift, hb, ob, tw, pidx, lab, msk, tgt = take(16)
    gi, gw0, gw1, gw2, gw3, ghc, gnorm, gsmall = take(8)
    (s, s4, wf, y, zb, zhat, d9, u_sel, ut_sel, a2a_s, a2a_r, rs_s, rs_r, pool_own, pool_all, ps_s, ps_r, gi_s, gi_r) = take(19)
    (gf, cr, zr, hr, hw_s, st_s, st_r, start_s, start_r, ho_s, ho_r, rep_s, rep_r, all_s, all_r, norm_s, feat) = take(17)
    ssem, rsem, wsz, wrz, wsf, wrf = take(6)
    w_in, gw = (w0, w1, w2, w3, hw_s), (gw0, gw1, gw2, gw3)
    R, F, Z, rows, C, CR, W, PIX, PD, M, PW = d.R, d.F, d.Z, d.rows, d.C, d.CR, d.W, d.PIX, d.PD, d.M, d.PW
    total = float(M * F)
    root = math.sqrt(total)

    r, f = lax.axis_index("rep"), lax.axis_index("fsdp")
    zc, core = f // 2, f % 2
    sib = (r, zc * 2 + (1 - core))
    rep_peer = lambda k: ((r + k) % R, f)
    z_peer = lambda k: (r, ((zc + k) % Z) * 2 + core)
    my_lanes = pl.ds(pl.multiple_of(r * CR, CR), CR)

    def block(owner):
        return pl.ds(pl.multiple_of(owner * rows, d.row_tile), rows)

    def send(src, dst, to, group):
        g = GROUP[group]
        pltpu.make_async_remote_copy(
            src_ref=src, dst_ref=dst, send_sem=ssem.at[g], recv_sem=rsem.at[g], device_id=to, device_id_type=MESH
        ).start()

    def wait_recv(ref, group):
        pltpu.make_async_copy(ref, ref, rsem.at[GROUP[group]]).wait()

    def wait_send(ref, group):
        pltpu.make_async_copy(ref, ref, ssem.at[GROUP[group]]).wait()

    def over(count, body, first=0):
        def step(i, carry):
            body(i)
            return carry

        lax.fori_loop(first, count, step, 0)

    barrier = pltpu.get_barrier_semaphore()
    over(R, lambda k: pl.semaphore_signal(barrier, inc=1, device_id=rep_peer(k), device_id_type=MESH), 1)
    over(F, lambda k: pl.semaphore_signal(barrier, inc=1, device_id=(r, (f + k) % F), device_id_type=MESH), 1)
    pl.semaphore_wait(barrier, R + F - 2)

    def w_copy(l, src, owner, to, send_sem, recv_sem):
        return pltpu.make_async_remote_copy(
            src_ref=src, dst_ref=wf.at[l, block(owner)], send_sem=send_sem, recv_sem=recv_sem, device_id=to, device_id_type=MESH
        )

    def w_push(l):
        src = w_in[l].at[:, my_lanes] if l < 4 else w_in[l]
        over(Z, lambda k: w_copy(l, src, f, z_peer(k), wsz.at[l, k], wrz.at[l, k]).start(), 1)
        w_copy(l, src, f, sib, wsf.at[l, 0], wrf.at[l, 0]).start()
        pltpu.make_async_copy(src, wf.at[l, block(f)], rsem.at[GROUP[f"own{l}"]]).start()

    def w_relay(l):
        def step(k):
            owner = ((zc + Z - k) % Z) * 2 + core
            here = wf.at[l, block(owner)]
            pltpu.make_async_copy(here, here, wrz.at[l, k]).wait()
            w_copy(l, here, owner, sib, wsf.at[l, k], wrf.at[l, k]).start()

        over(Z, step, 1)

    def w_finish(l):
        over(Z, lambda k: pltpu.make_async_copy(wf.at[l, block(f)], wf.at[l, block(f)], wrf.at[l, k]).wait())
        wait_recv(wf.at[l, block(f)], f"own{l}")

    w_push(0)
    over(R, lambda k: send(images, s.at[0, pl.ds(pl.multiple_of(r * PD, PD), PD)], rep_peer(k), "images"), 1)
    own_rows = s.at[0, pl.ds(pl.multiple_of(r * PD, PD), PD)]
    pltpu.make_async_copy(images, own_rows, rsem.at[GROUP["own_image"]]).start()

    start_s[...] = jnp.zeros_like(start_s)
    counted = jnp.sum(msk[...].astype(F32), axis=1, keepdims=True)
    lane = lax.broadcasted_iota(jnp.int32, (1, LANES), 1)
    start_s[0:1, :] = sum(jnp.where(lane == t, counted[t : t + 1, :], 0.0) for t in range(3))
    start_s[1:2, 0 : PW // R] = pidx[...].astype(F32)
    over(R, lambda k: send(start_s, start_r.at[r], rep_peer(k), "start"), 1)
    start_r[r] = start_s[...]
    ho_s[...] = jnp.zeros_like(ho_s)
    ho_s[0 : d.q, 0 : d.OC] = ho[...].astype(F32)
    over(F, lambda k: send(ho_s, ho_r.at[f], (r, (f + k) % F), "head_out"), 1)
    ho_r[f] = ho_s[...]
    hw_s[...] = jnp.zeros_like(hw_s)
    hw_s[:, 0 : d.HC] = hw[...]

    feat[...] = jnp.zeros_like(feat)
    feat[0:1, 0:PD] = lab[...].astype(F32)
    feat[1:4, 0:PD] = msk[...].astype(F32)
    feat[4:8, 0:PD] = tgt[...]
    columns = jnp.transpose(feat[...])[0:PD, :]

    wait_recv(start_r.at[pl.ds(0, R - 1)], "start")
    feat[...] = jnp.zeros_like(feat)
    for i in range(R):
        feat[0:1, i * (PW // R) : (i + 1) * (PW // R)] = start_r[i, 1:2, 0 : PW // R]
    picked_row = feat[0:1, 0:PW]
    picked_col = jnp.transpose(feat[...])[0:PW, 0:1]
    bits = W.bit_length() - 1

    def places(axis, shape):
        q = lax.broadcasted_iota(jnp.int32, shape, axis)
        image = jnp.zeros(shape, jnp.int32)
        for i in range(1, M // PIX):
            image = image + jnp.where(q >= i * PIX, 1, 0)
        q = q - image * PIX
        window = image * (PIX // 4) + (q >> (bits + 1)) * (W // 2) + ((q & (W - 1)) >> 1)
        position = 2 * ((q >> bits) & 1) + (q & 1)
        return window, position.astype(F32)

    def windows(rows_first):
        shape = (M, PW) if rows_first else (PW, M)
        window, position = places(0 if rows_first else 1, shape)
        other = lax.broadcasted_iota(jnp.int32, shape, 1 if rows_first else 0)
        return window == other, position

    inside, position = windows(True)
    u_sel[...] = jnp.where(inside & (position == picked_row), 1.0, 0.0).astype(BF16)
    inside, position = windows(False)
    ut_sel[...] = jnp.where(inside & (position == picked_col), 1.0, 0.0).astype(BF16)

    def image_rows(i):
        return pl.ds(pl.multiple_of(i * PIX, PIX), PIX)

    def per_image(count, body, init):
        return lax.fori_loop(0, count, body, init)

    def column_of(shape):
        return lax.broadcasted_iota(jnp.int32, shape, 0) & (W - 1)

    blank = jnp.zeros((W, CR), F32)

    def conv(src, count, l, out):
        height = count * PIX
        for kx in range(3):
            taps = [wf[l, (3 * ky + kx) * C : (3 * ky + kx + 1) * C, :].astype(BF16) for ky in range(3)]
            y[0:height, kx * 3 * CR : (kx + 1) * 3 * CR] = jnp.dot(
                src[...], jnp.concatenate(taps, axis=1), preferred_element_type=F32
            )

        def body(i, summed):
            at = image_rows(i)
            col = column_of((PIX, CR))
            parts = []
            for kx in range(3):
                up, mid, down = (y[at, (kx * 3 + ky) * CR : (kx * 3 + ky + 1) * CR] for ky in range(3))
                parts.append(
                    mid
                    + jnp.concatenate([blank, up[: PIX - W]], axis=0)
                    + jnp.concatenate([down[W:], blank], axis=0)
                )
            z = (
                parts[1]
                + jnp.where(col > 0, pltpu.roll(parts[0], 1, 0), 0.0)
                + jnp.where(col < W - 1, pltpu.roll(parts[2], PIX - 1, 0), 0.0)
            )
            out[at, :] = z
            return summed + jnp.sum(z, axis=0, keepdims=True)

        return per_image(count, body, jnp.zeros((1, CR), F32))

    def spread_taps(i, grad):
        at = image_rows(i)
        col = column_of((PIX, CR))
        moved = (
            jnp.where(col < W - 1, pltpu.roll(grad, PIX - 1, 0), 0.0),
            grad,
            jnp.where(col > 0, pltpu.roll(grad, 1, 0), 0.0),
        )
        low_blank = blank.astype(BF16)
        for kx in range(3):
            low = moved[kx].astype(BF16)
            nine = (
                jnp.concatenate([low[W:], low_blank], axis=0),
                low,
                jnp.concatenate([low_blank, low[: PIX - W]], axis=0),
            )
            for ky in range(3):
                d9[at, (kx * 3 + ky) * CR : (kx * 3 + ky + 1) * CR] = nine[ky]

    def data_grad(l, height, write):
        step = 2 * CR
        for half in range(C // step):
            taps = [
                wf[l, t * C + half * step : t * C + (half + 1) * step, :].astype(BF16)
                for t in (3 * ky + kx for kx in range(3) for ky in range(3))
            ]
            part = lax.dot_general(
                d9[0:height, :],
                jnp.concatenate(taps, axis=1),
                (((1,), (1,)), ((), ())),
                preferred_element_type=F32,
            )
            write(half, part)

    def weight_grad(l, src, height):
        for kx in range(3):
            part = lax.dot_general(
                src[...],
                d9[0:height, kx * 3 * CR : (kx + 1) * 3 * CR],
                (((0,), (0,)), ((), ())),
                preferred_element_type=F32,
            )
            for ky in range(3):
                t = 3 * ky + kx
                gf[l, t * C : (t + 1) * C, :] = part[:, ky * CR : (ky + 1) * CR].astype(gf.dtype)
        over(Z, lambda k: send(gf.at[l, block(2 * k + 1 - core)], cr.at[l, k], sib, f"core{l}"))

    def core_sum(l):
        wait_recv(cr.at[l], f"core{l}")

        def step(k):
            to = (zc + k) % Z
            at = block(2 * to + core)
            gf[l, at, :] = (gf[l, at, :].astype(F32) + cr[l, to].astype(F32)).astype(gf.dtype)

        def push(k):
            to = (zc + k) % Z
            step(k)
            send(gf.at[l, block(2 * to + core)], zr.at[l, zc], (r, 2 * to + core), f"z{l}")

        over(Z, push, 1)
        step(0)

    def z_sum(l):
        wait_recv(zr.at[l, pl.ds(0, Z - 1)], f"z{l}")
        summed = lax.fori_loop(
            1, Z, lambda k, so_far: so_far + zr[l, (zc + k) % Z].astype(F32), gf[l, block(f), :].astype(F32)
        )
        summed = summed * (1.0 / root)
        if l < 4:
            gw[l][:, my_lanes] = summed.astype(gw[l].dtype)
            here = gw[l].at[:, my_lanes]
            over(R, lambda k: send(here, here, rep_peer(k), f"rows{l}"), 1)
        else:
            hr[r] = summed.astype(hr.dtype)
            over(R, lambda k: send(hr.at[r], hr.at[r], rep_peer(k), "rows4"), 1)

    def rows_done(l):
        if l < 4:
            wait_recv(gw[l].at[:, pl.ds(0, (R - 1) * CR)], f"rows{l}")
        else:
            wait_recv(hr.at[pl.ds(0, R - 1)], "rows4")
            ghc[...] = sum(hr[i].astype(F32) for i in range(R))

    def exchange(e):
        over(F, lambda k: send(st_s.at[e], st_r.at[e, f], (r, (f + k) % F), f"stat{e}"), 1)
        st_r[e, f] = st_s[e]

    def exchanged(e):
        wait_recv(st_r.at[e, pl.ds(0, F - 1)], f"stat{e}")
        return st_r[e]

    st_s[...] = jnp.zeros_like(st_s)
    w_relay(0)
    w_push(1)
    wait_recv(s.at[0, pl.ds(0, (R - 1) * PD)], "images")
    wait_recv(own_rows, "own_image")

    inverse_of, counts = [], None
    for l in range(4):
        w_finish(l)
        if l == 2:
            wait_recv(pool_all.at[:, pl.ds(0, (R - 1) * CR)], "pool")
            s[2] = jnp.dot(u_sel[...], pool_all[...], preferred_element_type=F32).astype(BF16)
        elif l:
            wait_recv(s.at[l, :, pl.ds(0, (R - 1) * CR)], f"ag{l - 1}")
        first = conv(s.at[l], M // PIX, l, zb)
        mean_here = first * (1.0 / M)

        def squares(i, so_far):
            return so_far + jnp.sum(jnp.square(zb[image_rows(i), :] - mean_here), axis=0, keepdims=True)

        st_s[l, 0:1, :] = first
        st_s[l, 1:2, :] = per_image(M // PIX, squares, jnp.zeros((1, CR), F32))
        if l == 0:
            st_s[l, 2:3, :] = sum(start_r[i, 0:1, :] for i in range(R))
        exchange(l)
        parts = exchanged(l)
        tot = jnp.sum(parts, axis=0)
        mean = tot[0:1] * (1.0 / total)
        apart = jnp.sum(jnp.square(parts * (1.0 / M) - mean[None]), axis=0)[0:1] * float(M)
        inverse = lax.rsqrt((tot[1:2] + apart) * (1.0 / total) + EPS)
        inverse_of.append(inverse)
        if l == 0:
            counts = tot[2:3]
        g_row, b_row = gain[l : l + 1, my_lanes], shift[l : l + 1, my_lanes]

        def activate(i, carry):
            at = image_rows(i)
            normed = (zb[at, :] - mean) * inverse
            zhat[l, at, :] = normed
            shaped = normed * g_row + b_row
            hidden = shaped * jax.nn.sigmoid(shaped)
            if l == 1:
                zb[at, :] = hidden
            elif l == 3:
                a2a_s[i] = hidden.astype(BF16)
            else:
                s[l + 1, at, my_lanes] = hidden.astype(BF16)
            return carry

        per_image(M // PIX, activate, 0)
        if l == 1:
            inside, unused = windows(False)
            pooled = jnp.dot(
                jnp.where(inside, 0.25, 0.0), zb[...], precision=EXACT, preferred_element_type=F32
            )
            pool_own[...] = pooled.astype(BF16)
            pool_all[:, my_lanes] = pooled.astype(BF16)
            over(R, lambda k: send(pool_own, pool_all.at[:, my_lanes], rep_peer(k), "pool"), 1)
        elif l == 3:
            over(R, lambda k: send(a2a_s.at[(r + k) % R], s4.at[:, my_lanes], rep_peer(k), "a2a"), 1)
            s4[:, my_lanes] = a2a_s[r]
        else:
            here = s.at[l + 1, :, my_lanes]
            over(R, lambda k: send(here, here, rep_peer(k), f"ag{l}"), 1)
        w_relay(l + 1)
        if l < 3:
            w_push(l + 2)

    w_finish(4)
    wait_recv(s4.at[:, pl.ds(0, (R - 1) * CR)], "a2a")
    wait_recv(ho_r.at[pl.ds(0, F - 1)], "head_out")
    conv(s4, PD // PIX, 4, zb)
    head_bias = jnp.concatenate([hb[...], jnp.zeros((1, CR - d.HC), F32)], axis=1)
    out_bias = jnp.concatenate([ob[...], jnp.zeros((1, CR - d.OC), F32)], axis=1)
    head_raw = zb[0:PD, :] + head_bias
    squashed = jax.nn.sigmoid(head_raw)
    head_act = head_raw * squashed
    project = jnp.concatenate([ho_r[i][0 : d.q] for i in range(F)] + [jnp.zeros((LANES - d.HC, LANES), F32)], axis=0)
    out = jnp.dot(head_act, project, precision=EXACT, preferred_element_type=F32) + out_bias
    lane = lax.broadcasted_iota(jnp.int32, (PD, LANES), 1)
    classes = d.OC - 4
    factor = total * jnp.concatenate([tw[...], jnp.zeros((1, LANES - 3), F32)], axis=1) / jnp.maximum(counts, 1.0)
    pixel = [columns[:, i : i + 1] for i in range(8)]
    is_class = lane < classes
    top = jnp.max(jnp.where(is_class, out, -jnp.inf), axis=1, keepdims=True)
    grown = jnp.where(is_class, jnp.exp(jnp.where(is_class, out - top, 0.0)), 0.0)
    likely = grown / jnp.sum(grown, axis=1, keepdims=True)
    onehot = jnp.where(lane.astype(F32) == pixel[0], 1.0, 0.0)
    grad_class = factor[:, 0:1] * pixel[1] * (likely - onehot)
    misfit = out - pixel[4]
    grad_depth = factor[:, 1:2] * pixel[2] * misfit / jnp.sqrt(misfit * misfit + 1.0)
    is_normal = (lane > classes) & (lane < d.OC)
    predicted = jnp.where(is_normal, out, 0.0)
    wanted = sum(jnp.where(lane == classes + 1 + i, pixel[5 + i], 0.0) for i in range(3))
    radius = jnp.sqrt(jnp.sum(predicted * predicted, axis=1, keepdims=True) + 1.0)
    aligned = jnp.sum(predicted * wanted, axis=1, keepdims=True)
    grad_normal = -(factor[:, 2:3] * pixel[3]) * (wanted / radius - aligned / (radius * radius * radius) * predicted)
    grad_out = jnp.where(
        is_class, grad_class, jnp.where(lane == classes, grad_depth, jnp.where(is_normal, grad_normal, 0.0))
    )
    grad_act = lax.dot_general(
        grad_out, project, (((1,), (1,)), ((), ())), precision=EXACT, preferred_element_type=F32
    )
    grad_head = (grad_act * (squashed + head_raw * squashed * (1.0 - squashed))).astype(BF16).astype(F32)
    zb[0:PD, :] = grad_head
    y[0:PD, 0:CR] = head_act
    y[0:PD, CR : 2 * CR] = grad_out

    def spread_head(i, carry):
        spread_taps(i, zb[image_rows(i), :])
        return carry

    per_image(PD // PIX, spread_head, 0)

    def write_dh3(half, part):
        a2a_s[2 * half] = part[:, 0:CR].astype(BF16)
        a2a_s[2 * half + 1] = part[:, CR : 2 * CR].astype(BF16)

    wait_send(a2a_r.at[pl.ds(0, R - 1)], "a2a")
    data_grad(4, PD, write_dh3)
    over(R, lambda k: send(a2a_s.at[(r + k) % R], a2a_r.at[r], rep_peer(k), "dh3"), 1)
    a2a_r[r] = a2a_s[r]
    weight_grad(4, s4, PD)
    head_act, grad_out = y[0:PD, 0:CR], y[0:PD, CR : 2 * CR]
    pad = jnp.zeros((2 * LANES - PD, LANES), F32)
    act_t = jnp.transpose(jnp.concatenate([head_act, pad], axis=0))[:, 0:PD]
    rep_s[0 : d.HC, :] = jnp.dot(act_t, grad_out, precision=EXACT, preferred_element_type=F32)[0 : d.HC]
    rep_s[d.HC : d.HC + 8, :] = jnp.zeros((8, LANES), F32)
    rep_s[d.HC : d.HC + 1, :] = jnp.sum(zb[0:PD, :], axis=0, keepdims=True)
    rep_s[d.HC + 1 : d.HC + 2, :] = jnp.sum(grad_out, axis=0, keepdims=True)
    over(R, lambda k: send(rep_s, rep_r.at[r], rep_peer(k), "small_rep"), 1)
    rep_r[r] = rep_s[...]

    def head_small():
        wait_recv(rep_r.at[pl.ds(0, R - 1)], "small_rep")
        summed = sum(rep_r[i] for i in range(R))
        for i in range(F):
            all_s[i, 0 : d.q, :] = summed[i * d.q : (i + 1) * d.q]
            if d.q < 8:
                all_s[i, d.q : 8, :] = jnp.zeros((8 - d.q, LANES), F32)
            all_s[i, 8:16, :] = summed[d.HC : d.HC + 8]
        over(F, lambda k: send(all_s.at[(f + k) % F], all_r.at[f], (r, (f + k) % F), "small_all"), 1)
        all_r[f] = all_s[f]

    for l in (3, 2, 1, 0):
        e = 7 - l
        g_row, b_row = gain[l : l + 1, my_lanes], shift[l : l + 1, my_lanes]
        if l == 3:
            wait_recv(a2a_r.at[pl.ds(0, R - 1)], "dh3")
            entering = lambda i, at: a2a_r[i].astype(F32)
        elif l == 1:
            wait_recv(ps_r.at[pl.ds(0, R - 1)], "rs2")
            pooled = sum(ps_r[i].astype(F32) for i in range(R))
            inside, unused = windows(True)
            zb[...] = jnp.dot(jnp.where(inside, 0.25, 0.0), pooled, precision=EXACT, preferred_element_type=F32)
            entering = lambda i, at: zb[at, :]
        else:
            slot = 0 if l == 2 else 1
            wait_recv(rs_r.at[slot, pl.ds(0, R - 1)], f"rs{l + 1}")
            entering = lambda i, at: sum(rs_r[slot, j, at, :].astype(F32) for j in range(R))

        def slopes(i, so_far):
            at = image_rows(i)
            normed = zhat[l, at, :]
            shaped = normed * g_row + b_row
            squashed = jax.nn.sigmoid(shaped)
            grad = entering(i, at) * (squashed + shaped * squashed * (1.0 - squashed))
            zb[at, :] = grad
            return (
                so_far[0] + jnp.sum(grad, axis=0, keepdims=True),
                so_far[1] + jnp.sum(grad * normed, axis=0, keepdims=True),
            )

        none = jnp.zeros((1, CR), F32)
        part_bias, part_gain = per_image(M // PIX, slopes, (none, none))
        st_s[e, 0:1, :] = part_bias
        st_s[e, 1:2, :] = part_gain
        exchange(e)
        if l == 3:
            core_sum(4)
            head_small()
        else:
            z_sum(l + 2)
        tot = jnp.sum(exchanged(e), axis=0)
        bias_sum, gain_sum = tot[0:1], tot[1:2]
        norm_s[l : l + 1, :] = gain_sum * (1.0 / root)
        norm_s[4 + l : 5 + l, :] = bias_sum * (1.0 / root)
        scale = inverse_of[l] * g_row

        def through_norm(i, carry):
            at = image_rows(i)
            spread_taps(
                i, scale * (zb[at, :] - bias_sum * (1.0 / total) - zhat[l, at, :] * (gain_sum * (1.0 / total)))
            )
            return carry

        per_image(M // PIX, through_norm, 0)
        if l == 2:

            def write(half, part):
                chosen = jnp.dot(ut_sel[...], part.astype(BF16), preferred_element_type=F32).astype(BF16)
                ps_s[2 * half] = chosen[:, 0:CR]
                ps_s[2 * half + 1] = chosen[:, CR : 2 * CR]

            data_grad(l, M, write)
            over(R, lambda k: send(ps_s.at[(r + k) % R], ps_r.at[r], rep_peer(k), "rs2"), 1)
            ps_r[r] = ps_s[r]
            weight_grad(l, s.at[l], M)
            core_sum(l)
        elif l == 0:
            weight_grad(l, s.at[l], M)

            def write(half, part):
                for i in range(R):
                    gi_s[i, :, half * 2 * CR : (half + 1) * 2 * CR] = part[i * PD : (i + 1) * PD].astype(BF16)

            data_grad(l, M, write)
            over(R, lambda k: send(gi_s.at[(r + k) % R], gi_r.at[r], rep_peer(k), "rs0"), 1)
            gi_r[r] = gi_s[r]
            core_sum(l)
        else:
            slot = 0 if l == 3 else 1

            def write(half, part):
                rs_s[slot, 2 * half] = part[:, 0:CR].astype(BF16)
                rs_s[slot, 2 * half + 1] = part[:, CR : 2 * CR].astype(BF16)

            data_grad(l, M, write)
            over(R, lambda k: send(rs_s.at[slot, (r + k) % R], rs_r.at[slot, r], rep_peer(k), f"rs{l}"), 1)
            rs_r[slot, r] = rs_s[slot, r]
            weight_grad(l, s.at[l], M)
            core_sum(l)

    gnorm[:, my_lanes] = norm_s[...]
    over(R, lambda k: send(norm_s, gnorm.at[:, my_lanes], rep_peer(k), "norms"), 1)
    z_sum(1)
    wait_recv(all_r.at[pl.ds(0, F - 1)], "small_all")
    gsmall[...] = jnp.sum(all_r[...], axis=0) * (1.0 / root)
    rows_done(4)
    rows_done(3)
    rows_done(2)
    wait_recv(gi_r.at[pl.ds(0, R - 1)], "rs0")
    gi[...] = sum(gi_r[i].astype(F32) for i in range(R))
    z_sum(0)
    wait_recv(gnorm.at[:, pl.ds(0, (R - 1) * CR)], "norms")
    rows_done(1)
    rows_done(0)

    wait_send(s.at[0, pl.ds(0, (R - 1) * PD)], "images")
    wait_send(start_r.at[pl.ds(0, R - 1)], "start")
    wait_send(ho_r.at[pl.ds(0, F - 1)], "head_out")
    wait_send(pool_all.at[:, pl.ds(0, (R - 1) * CR)], "pool")
    for i in (0, 2):
        wait_send(s.at[i + 1, :, pl.ds(0, (R - 1) * CR)], f"ag{i}")
    wait_send(a2a_r.at[pl.ds(0, R - 1)], "dh3")
    wait_send(rs_r.at[0, pl.ds(0, R - 1)], "rs3")
    wait_send(ps_r.at[pl.ds(0, R - 1)], "rs2")
    wait_send(rs_r.at[1, pl.ds(0, R - 1)], "rs1")
    wait_send(gi_r.at[pl.ds(0, R - 1)], "rs0")
    wait_send(gnorm.at[:, pl.ds(0, (R - 1) * CR)], "norms")
    wait_send(rep_r.at[pl.ds(0, R - 1)], "small_rep")
    wait_send(all_r.at[pl.ds(0, F - 1)], "small_all")
    for e in range(8):
        wait_send(st_r.at[e, pl.ds(0, F - 1)], f"stat{e}")
    for l in range(5):
        wait_send(cr.at[l], f"core{l}")
        wait_send(zr.at[l, pl.ds(0, Z - 1)], f"z{l}")
        wait_send(gw[l].at[:, pl.ds(0, (R - 1) * CR)] if l < 4 else hr.at[pl.ds(0, R - 1)], f"rows{l}")
        one = wf.at[l, block(f)]
        over(Z, lambda k: pltpu.make_async_copy(one, one, wsf.at[l, k]).wait())
        over(Z, lambda k: pltpu.make_async_copy(one, one, wsz.at[l, k]).wait(), 1)


def per_device(
    R, F,
    images, enc_first, enc_second, dec_first, dec_second, head_conv, head_out, norm_gain, norm_bias, head_bias, out_bias,
    task_weights, pool_index, labels, task_masks, targets,
):
    n, height, breadth, channels = images.shape
    rows, hidden = head_conv.shape
    q, out_ch = head_out.shape
    d = types.SimpleNamespace(
        R=R, F=F, Z=F // 2, rows=rows, C=channels, CR=channels // R, W=breadth, PIX=height * breadth,
        PD=n * height * breadth, HC=hidden, OC=out_ch, q=q,
    )
    d.M = R * d.PD
    d.PW = d.M // 4
    wire = BF16 if rows % 16 == 0 else F32
    d.row_tile = 16 if rows % 16 == 0 else 8
    vm = pltpu.VMEM
    patch = 9 * channels
    scratch = [
        vm((4, d.M, d.C), BF16),
        vm((d.PD, d.C), BF16),
        vm((5, patch, d.CR), wire),
        vm((d.M, 9 * d.CR), F32),
        vm((d.M, d.CR), F32),
        vm((4, d.M, d.CR), F32),
        vm((d.M, 9 * d.CR), BF16),
        vm((d.M, d.PW), BF16),
        vm((d.PW, d.M), BF16),
        vm((R, d.PD, d.CR), BF16),
        vm((R, d.PD, d.CR), BF16),
        vm((2, R, d.M, d.CR), BF16),
        vm((2, R, d.M, d.CR), BF16),
        vm((d.PW, d.CR), BF16),
        vm((d.PW, d.C), BF16),
        vm((R, d.PW, d.CR), BF16),
        vm((R, d.PW, d.CR), BF16),
        vm((R, d.PD, d.C), BF16),
        vm((R, d.PD, d.C), BF16),
        vm((5, patch, d.CR), wire),
        vm((5, d.Z, rows, d.CR), wire),
        vm((5, d.Z, rows, d.CR), wire),
        vm((R, rows, d.CR), wire),
        vm((rows, LANES), wire),
        vm((8, 8, LANES), F32),
        vm((8, F, 8, LANES), F32),
        vm((8, LANES), F32),
        vm((R, 8, LANES), F32),
        vm((8, LANES), F32),
        vm((F, 8, LANES), F32),
        vm((hidden + 8, LANES), F32),
        vm((R, hidden + 8, LANES), F32),
        vm((F, 16, LANES), F32),
        vm((F, 16, LANES), F32),
        vm((8, LANES), F32),
        vm((LANES, 2 * LANES), F32),
        pltpu.SemaphoreType.DMA((len(GROUPS),)),
        pltpu.SemaphoreType.DMA((len(GROUPS),)),
        pltpu.SemaphoreType.DMA((5, d.Z)),
        pltpu.SemaphoreType.DMA((5, d.Z)),
        pltpu.SemaphoreType.DMA((5, d.Z)),
        pltpu.SemaphoreType.DMA((5, d.Z)),
    ]
    here, there = pl.BlockSpec(memory_space=pltpu.VMEM), pl.BlockSpec(memory_space=pl.ANY)
    row_type = BF16 if rows % 16 == 0 else F32
    shape = jax.ShapeDtypeStruct
    gi, gw0, gw1, gw2, gw3, ghc, gnorm, gsmall = pl.pallas_call(
        functools.partial(kernel, d),
        out_shape=[shape((d.PD, d.C), F32)]
        + [shape((rows, d.C), row_type)] * 4
        + [shape((rows, LANES), F32), shape((8, d.C), F32), shape((16, LANES), F32)],
        in_specs=[there] * 5 + [here] * 11,
        out_specs=[here] * 8,
        scratch_shapes=scratch,
        compiler_params=pltpu.CompilerParams(collective_id=0, has_side_effects=True, vmem_limit_bytes=60 * 2**20),
    )(
        images.reshape(d.PD, channels),
        *(w.astype(wire) for w in (enc_first, enc_second, dec_first, dec_second, head_conv)),
        head_out, norm_gain, norm_bias, head_bias.reshape(1, hidden), out_bias.reshape(1, out_ch),
        task_weights.reshape(1, 3), pool_index.reshape(1, -1), labels.reshape(1, -1),
        jnp.transpose(task_masks, (1, 0, 2)).reshape(3, -1), jnp.transpose(targets, (1, 0, 2)).reshape(4, -1),
    )
    return (
        gi.reshape(images.shape), gw0.astype(F32), gw1.astype(F32), gw2.astype(F32), gw3.astype(F32), ghc[:, :hidden],
        gsmall[:q, :out_ch], gnorm[0:4], gnorm[4:8], gsmall[8, :hidden], gsmall[9, :out_ch],
    )


def solution(mesh):
    split = ("rep", "fsdp")
    rows = P("fsdp", None)
    return jax.shard_map(
        functools.partial(per_device, mesh.shape["rep"], mesh.shape["fsdp"]),
        mesh=mesh,
        in_specs=(P(split, None, None, None),)
        + (rows,) * 6
        + (P(),) * 5
        + (P(split, None), P(split, None), P(split, None, None), P(split, None, None)),
        out_specs=(P(split, None, None, None),) + (rows,) * 6 + (P(),) * 4,
        check_vma=False,
    )
```

time: 1300 us -> 214 us (0.16)
  blocking collectives: 557 us -> 0 us
  waiting for transfers between devices: 411 us -> 0 us
  Pallas kernels: 0 us -> 197 us
  matrix products: 174 us -> 0 us
  local copies, waits for them, and re-layouts: 92.6 us -> 10.6 us
  other arithmetic: 38.8 us -> 5.73 us
  between operations: 16.8 us -> 0.67 us
    psum x13 -> x0, blocking collectives: 498 us -> none  [the longest x4 160 us: moments(): spread = lax.psum(centered, ('rep', 'fsdp')) / population]
    reduce_scatter x4 -> x0, waiting for transfers between devices: 367 us -> none  [the longest x1 98.1 us: per_device(): lax.psum_scatter(weight_terms[3], 'fsdp', scatter_dimension=0, tiled=True)]
    pallas_call x0 -> x1, Pallas kernels: none -> 197 us  [per_device(): pl.pallas_call(functools.partial(kernel, d), out_shape=[shape((d.PD, d.C)...]
    dot_general x138 -> x0, matrix products: 174 us -> none  [the longest x45 85.3 us: conv_data_grad(): jnp.einsum('nhwd,cd->nhwc', grad_low, weight[position * channels:(positio...]
    scatter-add x35 -> x0, local copies, waits for them, and re-layouts: 71.2 us -> none  [conv_data_grad(): padded.at[:, row_at:row_at + height, col_at:col_at + breadth, :].add(backed)]
    all_gather x2 -> x0, blocking collectives: 33 us -> none  [the longest x1 18.1 us: per_device(): lax.all_gather(head_conv, 'fsdp', axis=0, tiled=True)]
    unnamed x1 -> x0, blocking collectives: 26 us -> none
    psum x1 -> x0, waiting for transfers between devices: 23.9 us -> none  [per_device(): lax.psum(enc_shards[0].astype(jnp.bfloat16), 'rep').astype(jnp.float32)]
  transfers between devices with their start and end apart: 10 -> 0, of which waited for: 6 -> 0; matrix products, arithmetic and copies ran while one was open for 9% -> 0% of each run, Pallas kernels for 0% -> 0%
where the time goes in v1:
time: 214 us
  Pallas kernels  197 us (92%)
  local copies, waits for them, and re-layouts  10.6 us (5%)
  other arithmetic  5.73 us (3%)
    pallas_call x1, Pallas kernels, per_device(): pl.pallas_call(functools.partial(kernel, d), out_shape=[shape((d.PD, d.C)...  197 us
    unnamed x12, local copies, waits for them, and re-layouts  5.48 us

profile of v1, /device:TPU:0, one launch (start us, length us, event | category | flops | bytes accessed | tf_op | source)
XLA Modules:
  0.0 213.8 jit_solution(8142306779345827989)
XLA Ops:
  0.6 1.3 copy.31
  1.9 1.7 copy.27.refs_5_
  3.6 196.8 %shard_map.239 = (f32[192,512]{1,0:T(8,128)}, bf16[576,512]{1,0:T(8,128)(2,1)}, bf16[576,512]{1,0:T(8,128)(2,1)}, bf16[576,512]{1,0:T(8,128)(2,1)}, bf16[576,512...) custom-call(bf16[192,512]{1,0:T(8,128)(2,1)} %bitcast.16, bf16[576,512]{1,0:T(8,128)(2,1)} %refs_1_.1, ...), custom_call_target="tpu_custom_call" | custom-call | tf_op jit(solution)/shard_map/pallas_call | solution.py:626
  200.4 0.0 copy-start.2
  200.4 1.2 slice_bitcast_fusion
  201.7 1.2 slice_bitcast_fusion.1
  202.8 1.3 slice.19
  204.1 1.4 fusion
  205.5 1.8 copy.28
  207.3 2.2 %convert_element_type.12 = f32[576,512]{1,0:T(8,128)} convert(bf16[576,512]{1,0:T(8,128)(2,1)} %get-tuple-element.20) | non-fusion elementwise | flops 294912 | bytes 1769472 | tf_op jit(solution)/shard_map/convert_element_type | solution.py:643
  209.5 0.0 copy-done.2
  209.5 0.0 copy-start.1
  209.5 1.2 convert_element_type.13
  210.7 0.0 copy-done.1
  210.7 0.0 copy-start
  210.7 1.2 convert_element_type.14
  211.9 0.0 copy-done
  211.9 0.0 copy-start.3
  211.9 1.2 convert_element_type.15
  213.0 0.0 copy-done.3
  213.0 0.7 copy.33
Async XLA Ops:
  200.4 9.1 %copy-start.2 = (bf16[576,512]{1,0:T(8,128)(2,1)S(1)}, bf16[576,512]{1,0:T(8,128)(2,1)}, u32[]{:S(2)}) copy-start(bf16[576,512]{1,0:T(8,128)(2,1)} %get-tuple-element.21) | copy-start | bytes 1769476
  209.5 1.2 copy-start.1
  210.7 1.2 copy-start
  211.9 1.2 copy-start.3

commit v2 on v1

--- a/solution.py
+++ b/solution.py
@@ -21,6 +21,7 @@
     + [f"stat{i}" for i in range(8)]
     + [f"core{i}" for i in range(5)]
     + [f"z{i}" for i in range(5)]
+    + [f"mid{i}" for i in range(5)]
     + [f"rows{i}" for i in range(5)]
     + [f"own{i}" for i in range(5)]
     + ["own_image"]
@@ -34,10 +35,10 @@
     images, w0, w1, w2, w3, hw, ho, gain, shift, hb, ob, tw, pidx, lab, msk, tgt = take(16)
     gi, gw0, gw1, gw2, gw3, ghc, gnorm, gsmall = take(8)
     (s, s4, wf, y, zb, zhat, d9, u_sel, ut_sel, a2a_s, a2a_r, rs_s, rs_r, pool_own, pool_all, ps_s, ps_r, gi_s, gi_r) = take(19)
-    (gf, cr, zr, hr, hw_s, st_s, st_r, start_s, start_r, ho_s, ho_r, rep_s, rep_r, all_s, all_r, norm_s, feat) = take(17)
+    (gf, cr, zr, hw_s, hp, hg, hcr, hzr, hr, st_s, st_r, start_s, start_r, ho_s, ho_r, rep_s, rep_r, all_s, all_r, norm_s, feat) = take(21)
     ssem, rsem, wsz, wrz, wsf, wrf = take(6)
     w_in, gw = (w0, w1, w2, w3, hw_s), (gw0, gw1, gw2, gw3)
-    R, F, Z, rows, C, CR, W, PIX, PD, M, PW = d.R, d.F, d.Z, d.rows, d.C, d.CR, d.W, d.PIX, d.PD, d.M, d.PW
+    R, F, Z, rows, half, C, CR, W, PIX, PD, M, PW = d.R, d.F, d.Z, d.rows, d.half, d.C, d.CR, d.W, d.PIX, d.PD, d.M, d.PW
     total = float(M * F)
     root = math.sqrt(total)
 
@@ -46,85 +47,215 @@
     sib = (r, zc * 2 + (1 - core))
     rep_peer = lambda k: ((r + k) % R, f)
     z_peer = lambda k: (r, ((zc + k) % Z) * 2 + core)
+    line = Z == 4
+    is_end = (zc == 0) | (zc == Z - 1)
+    is_far = lambda k: (zc + k) % Z - zc == Z - 1
+    is_far_back = lambda k: zc - (zc + k) % Z == Z - 1
+    ends_apart = lambda k: is_far(k) | is_far_back(k)
     my_lanes = pl.ds(pl.multiple_of(r * CR, CR), CR)
 
     def block(owner):
         return pl.ds(pl.multiple_of(owner * rows, d.row_tile), rows)
 
+    arriving, leaving = {}, {}
+
+    def first_of(ref, count):
+        return lambda: ref.at[pl.ds(0, count)]
+
+    volume = {
+        "images": first_of(s.at[0], (R - 1) * PD),
+        "own_image": first_of(s.at[0], PD),
+        "start": first_of(start_r, R - 1),
+        "head_out": first_of(ho_r, F - 1),
+        "a2a": lambda: s4.at[:, pl.ds(0, (R - 1) * CR)],
+        "pool": lambda: pool_all.at[:, pl.ds(0, (R - 1) * CR)],
+        "dh3": first_of(a2a_r, R - 1),
+        "rs3": first_of(rs_r.at[0], R - 1),
+        "rs2": first_of(ps_r, R - 1),
+        "rs1": first_of(rs_r.at[1], R - 1),
+        "rs0": first_of(gi_r, R - 1),
+        "norms": lambda: gnorm.at[:, pl.ds(0, (R - 1) * CR)],
+        "small_rep": first_of(rep_r, R - 1),
+        "small_all": first_of(all_r, F - 1),
+        "rows4": first_of(hr, R - 1),
+        "core4": lambda: hcr,
+        "mid4": lambda: hzr.at[0],
+    }
+    for l in (0, 2):
+        volume[f"ag{l}"] = lambda l=l: s.at[l + 1, :, pl.ds(0, (R - 1) * CR)]
+    for e in range(8):
+        volume[f"stat{e}"] = first_of(st_r.at[e], F - 1)
+    for l in range(4):
+        volume[f"core{l}"] = lambda l=l: cr.at[l]
+        volume[f"mid{l}"] = lambda l=l: zr.at[l, 0]
+        volume[f"rows{l}"] = lambda l=l: gw[l].at[:, pl.ds(0, (R - 1) * CR)]
+
+    def wait_for(ref, sem):
+        pltpu.make_async_copy(ref, ref, sem).wait()
+
+    def wait_recv(group):
+        arriving.pop(group)()
+
+    def wait_send(group):
+        leaving.pop(group)()
+
+    def copy_here(src, dst, group):
+        g = GROUP[group]
+        arriving[group] = lambda: wait_for(dst, rsem.at[g])
+        pltpu.make_async_copy(src, dst, rsem.at[g]).start()
+
     def send(src, dst, to, group):
         g = GROUP[group]
+        if group in volume:
+            arriving[group] = lambda: wait_for(volume[group](), rsem.at[g])
+            leaving[group] = lambda: wait_for(volume[group](), ssem.at[g])
         pltpu.make_async_remote_copy(
             src_ref=src, dst_ref=dst, send_sem=ssem.at[g], recv_sem=rsem.at[g], device_id=to, device_id_type=MESH
         ).start()
 
-    def wait_recv(ref, group):
-        pltpu.make_async_copy(ref, ref, rsem.at[GROUP[group]]).wait()
-
-    def wait_send(ref, group):
-        pltpu.make_async_copy(ref, ref, ssem.at[GROUP[group]]).wait()
-
     def over(count, body, first=0):
+        if count <= 8:
+            for i in range(first, count):
+                body(i)
+            return
+
         def step(i, carry):
             body(i)
             return carry
 
         lax.fori_loop(first, count, step, 0)
+
+    def when(condition, body):
+        pl.when(condition)(body)
+
+    def direct(k, body):
+        if line and k in (1, Z - 1):
+            when(jnp.logical_not(ends_apart(k)), body)
+        else:
+            body()
+
+    def drain():
+        for waits in (arriving, leaving):
+            for wait in list(waits.values()):
+                wait()
 
     barrier = pltpu.get_barrier_semaphore()
     over(R, lambda k: pl.semaphore_signal(barrier, inc=1, device_id=rep_peer(k), device_id_type=MESH), 1)
     over(F, lambda k: pl.semaphore_signal(barrier, inc=1, device_id=(r, (f + k) % F), device_id_type=MESH), 1)
     pl.semaphore_wait(barrier, R + F - 2)
 
+    def w_block(l, owner):
+        return wf.at[l, block(owner)] if l < 4 else hp.at[owner]
+
     def w_copy(l, src, owner, to, send_sem, recv_sem):
         return pltpu.make_async_remote_copy(
-            src_ref=src, dst_ref=wf.at[l, block(owner)], send_sem=send_sem, recv_sem=recv_sem, device_id=to, device_id_type=MESH
+            src_ref=src, dst_ref=w_block(l, owner), send_sem=send_sem, recv_sem=recv_sem, device_id=to, device_id_type=MESH
         )
 
-    def w_push(l):
-        src = w_in[l].at[:, my_lanes] if l < 4 else w_in[l]
-        over(Z, lambda k: w_copy(l, src, f, z_peer(k), wsz.at[l, k], wrz.at[l, k]).start(), 1)
-        w_copy(l, src, f, sib, wsf.at[l, 0], wrf.at[l, 0]).start()
-        pltpu.make_async_copy(src, wf.at[l, block(f)], rsem.at[GROUP[f"own{l}"]]).start()
-
-    def w_relay(l):
-        def step(k):
-            owner = ((zc + Z - k) % Z) * 2 + core
-            here = wf.at[l, block(owner)]
-            pltpu.make_async_copy(here, here, wrz.at[l, k]).wait()
-            w_copy(l, here, owner, sib, wsf.at[l, k], wrf.at[l, k]).start()
-
-        over(Z, step, 1)
+    def w_src(l):
+        return w_in[l].at[:, my_lanes] if l < 4 else hw_s
+
+    def w_send(l, k):
+        arriving["near" if k in (1, Z - 1) else "rest", l, k] = lambda: direct(Z - k, lambda: w_wait(l, wrz.at[l, k]))
+        leaving["w", l, k] = lambda: direct(k, lambda: w_wait(l, wsz.at[l, k]))
+        direct(k, lambda: w_copy(l, w_src(l), f, z_peer(k), wsz.at[l, k], wrz.at[l, k]).start())
+
+    def w_push_near(l):
+        for k in sorted({1, Z - 1}):
+            w_send(l, k)
+        w_copy(l, w_src(l), f, sib, wsf.at[l, 0], wrf.at[l, 0]).start()
+        arriving["core", l, 0] = lambda: w_wait(l, wrf.at[l, 0])
+        leaving["core", l, 0] = lambda: w_wait(l, wsf.at[l, 0])
+        copy_here(w_src(l), w_block(l, f), f"own{l}")
+
+    def w_push_rest(l):
+        for k in range(2, Z - 1):
+            w_send(l, k)
+
+    def w_wait(l, sem):
+        pltpu.make_async_copy(w_block(l, f), w_block(l, f), sem).wait()
+
+    def w_arrived(l, k):
+        owner = ((zc + Z - k) % Z) * 2 + core
+        w_wait(l, wrz.at[l, k])
+        w_copy(l, w_block(l, owner), owner, sib, wsf.at[l, k], wrf.at[l, k]).start()
+
+    def w_relayed(l, k):
+        arriving["core", l, k] = lambda: w_wait(l, wrf.at[l, k])
+        leaving["core", l, k] = lambda: w_wait(l, wsf.at[l, k])
+
+    def w_relay_rest(l):
+        for k in range(2, Z - 1):
+            arriving.pop(("rest", l, k))
+            w_arrived(l, k)
+            w_relayed(l, k)
+        if line:
+
+            def hand_on():
+                to = (Z - 1) * (zc - 1)
+                owner = (Z - 1 - to) * 2 + core
+                slot = jnp.where(zc == 1, 1, Z - 1)
+                w_copy(l, w_block(l, owner), owner, (r, to * 2 + core), wsz.at[l, 0], wrz.at[l, slot]).start()
+
+            when(jnp.logical_not(is_end), hand_on)
+            leaving["far", l] = lambda: when(jnp.logical_not(is_end), lambda: w_wait(l, wsz.at[l, 0]))
+
+    def w_relay_near(l):
+        for k in sorted({1, Z - 1}):
+            arriving.pop(("near", l, k))
+            direct(Z - k, lambda: w_arrived(l, k))
+            if not line:
+                w_relayed(l, k)
+
+    def w_far(l):
+        if line:
+            for k in (1, Z - 1):
+                w_relayed(l, k)
+            when(zc == 0, lambda: w_arrived(l, 1))
+            when(zc == Z - 1, lambda: w_arrived(l, Z - 1))
 
     def w_finish(l):
-        over(Z, lambda k: pltpu.make_async_copy(wf.at[l, block(f)], wf.at[l, block(f)], wrf.at[l, k]).wait())
-        wait_recv(wf.at[l, block(f)], f"own{l}")
-
-    w_push(0)
+        for k in range(Z):
+            wait_recv(("core", l, k))
+        wait_recv(f"own{l}")
+
+    w_push_rest(0)
+    w_push_near(0)
     over(R, lambda k: send(images, s.at[0, pl.ds(pl.multiple_of(r * PD, PD), PD)], rep_peer(k), "images"), 1)
     own_rows = s.at[0, pl.ds(pl.multiple_of(r * PD, PD), PD)]
-    pltpu.make_async_copy(images, own_rows, rsem.at[GROUP["own_image"]]).start()
+    copy_here(images, own_rows, "own_image")
 
     start_s[...] = jnp.zeros_like(start_s)
-    counted = jnp.sum(msk[...].astype(F32), axis=1, keepdims=True)
+    masks = jnp.concatenate([msk[:, i, :] for i in range(d.n)], axis=1).astype(F32)
+    labels = jnp.concatenate([lab[i : i + 1, :] for i in range(d.n)], axis=1).astype(F32)
+    wanted = jnp.concatenate([tgt[i] for i in range(d.n)], axis=1)
+    pools = jnp.concatenate([pidx[i : i + 1, :] for i in range(d.n)], axis=1).astype(F32)
+    counted = jnp.sum(masks, axis=1, keepdims=True)
     lane = lax.broadcasted_iota(jnp.int32, (1, LANES), 1)
     start_s[0:1, :] = sum(jnp.where(lane == t, counted[t : t + 1, :], 0.0) for t in range(3))
-    start_s[1:2, 0 : PW // R] = pidx[...].astype(F32)
+    start_s[1:2, 0 : PW // R] = pools
     over(R, lambda k: send(start_s, start_r.at[r], rep_peer(k), "start"), 1)
     start_r[r] = start_s[...]
     ho_s[...] = jnp.zeros_like(ho_s)
     ho_s[0 : d.q, 0 : d.OC] = ho[...].astype(F32)
     over(F, lambda k: send(ho_s, ho_r.at[f], (r, (f + k) % F), "head_out"), 1)
     ho_r[f] = ho_s[...]
-    hw_s[...] = jnp.zeros_like(hw_s)
-    hw_s[:, 0 : d.HC] = hw[...]
+    wide = -(-rows // LANES) * LANES
+    tall = jnp.concatenate([hw[...].astype(F32), jnp.zeros((LANES - d.HC, rows), F32)], axis=0)
+    if wide > rows:
+        tall = jnp.concatenate([tall, jnp.zeros((LANES, wide - rows), F32)], axis=1)
+    tall = jnp.transpose(tall)
+    if wide < 2 * half:
+        tall = jnp.concatenate([tall, jnp.zeros((2 * half - wide, LANES), F32)], axis=0)
+    hw_s[...] = (tall[0:half] + pltpu.roll(tall[half : 2 * half], d.HC, 1)).astype(hw_s.dtype)
 
     feat[...] = jnp.zeros_like(feat)
-    feat[0:1, 0:PD] = lab[...].astype(F32)
-    feat[1:4, 0:PD] = msk[...].astype(F32)
-    feat[4:8, 0:PD] = tgt[...]
+    feat[0:1, 0:PD] = labels
+    feat[1:4, 0:PD] = masks
+    feat[4:8, 0:PD] = wanted
     columns = jnp.transpose(feat[...])[0:PD, :]
 
-    wait_recv(start_r.at[pl.ds(0, R - 1)], "start")
+    wait_recv("start")
     feat[...] = jnp.zeros_like(feat)
     for i in range(R):
         feat[0:1, i * (PW // R) : (i + 1) * (PW // R)] = start_r[i, 1:2, 0 : PW // R]
@@ -227,6 +358,15 @@
             )
             write(half, part)
 
+    def g_block(l, owner):
+        return gf.at[l, block(owner)] if l < 4 else hg.at[owner]
+
+    def from_core(l):
+        return cr.at[l] if l < 4 else hcr
+
+    def from_z(l):
+        return zr.at[l] if l < 4 else hzr
+
     def weight_grad(l, src, height):
         for kx in range(3):
             part = lax.dot_general(
@@ -237,30 +377,86 @@
             )
             for ky in range(3):
                 t = 3 * ky + kx
-                gf[l, t * C : (t + 1) * C, :] = part[:, ky * CR : (ky + 1) * CR].astype(gf.dtype)
-        over(Z, lambda k: send(gf.at[l, block(2 * k + 1 - core)], cr.at[l, k], sib, f"core{l}"))
+                gf[l % 4, t * C : (t + 1) * C, :] = part[:, ky * CR : (ky + 1) * CR].astype(gf.dtype)
+        if l == 4:
+
+            def pack(i, carry):
+                at = i * rows
+                low = gf[0, pl.ds(pl.multiple_of(at, d.row_tile), half), :].astype(F32)
+                high = gf[0, pl.ds(pl.multiple_of(at + half, d.row_tile), rows - half), :].astype(F32)
+                if rows < 2 * half:
+                    high = jnp.concatenate([high, jnp.zeros((2 * half - rows, CR), F32)], axis=0)
+                hg[i] = (low + pltpu.roll(high, d.HC, 1)).astype(hg.dtype)
+                return carry
+
+            lax.fori_loop(0, F, pack, 0)
+        over(Z, lambda k: send(g_block(l, 2 * k + 1 - core), from_core(l).at[k], sib, f"core{l}"))
 
     def core_sum(l):
-        wait_recv(cr.at[l], f"core{l}")
+        wait_recv(f"core{l}")
 
         def step(k):
-            to = (zc + k) % Z
-            at = block(2 * to + core)
-            gf[l, at, :] = (gf[l, at, :].astype(F32) + cr[l, to].astype(F32)).astype(gf.dtype)
-
+            ref = g_block(l, 2 * k + core)
+            ref[...] = (ref[...].astype(F32) + from_core(l)[k].astype(F32)).astype(ref.dtype)
+
+        over(Z, step)
+
+    def z_push(l):
         def push(k):
             to = (zc + k) % Z
-            step(k)
-            send(gf.at[l, block(2 * to + core)], zr.at[l, zc], (r, 2 * to + core), f"z{l}")
-
-        over(Z, push, 1)
-        step(0)
+            send(g_block(l, 2 * to + core), from_z(l).at[zc], (r, 2 * to + core), f"z{l}")
+
+        if line:
+
+            def to_middle():
+                through, owner = jnp.where(zc == 0, 1, Z - 2), Z - 1 - zc
+                send(g_block(l, 2 * owner + core), from_z(l).at[through], (r, 2 * through + core), f"mid{l}")
+
+            when(is_end, to_middle)
+            middle, outside = arriving.pop(f"mid{l}"), leaving.pop(f"mid{l}")
+            arriving[f"mid{l}"] = lambda: when(jnp.logical_not(is_end), middle)
+            leaving[f"mid{l}"] = lambda: when(is_end, outside)
+        for k in range(1, Z) if Z <= 8 else ():
+            if line and k == 2:
+                when(is_end, lambda: push(2))
+            else:
+                direct(k, lambda: push(k))
+        if Z > 8:
+            over(Z, push, 1)
+        arriving[f"z{l}"] = lambda: z_wait(l, rsem.at[GROUP[f"z{l}"]])
+        leaving[f"z{l}"] = lambda: z_wait(l, ssem.at[GROUP[f"z{l}"]])
+
+    def z_middle(l):
+        if line:
+            wait_recv(f"mid{l}")
+
+            def hand_on():
+                owner = (Z - 1) * (Z - 2 - zc)
+                ref = g_block(l, 2 * owner + core)
+                ref[...] = (ref[...].astype(F32) + from_z(l)[zc].astype(F32)).astype(ref.dtype)
+                send(ref, from_z(l).at[zc], (r, 2 * owner + core), f"z{l}")
+
+            when(jnp.logical_not(is_end), hand_on)
+
+    def z_wait(l, sem):
+        if line:
+            when(is_end, lambda: wait_for(from_z(l).at[pl.ds(0, Z - 2)], sem))
+            when(jnp.logical_not(is_end), lambda: wait_for(from_z(l).at[pl.ds(0, Z - 1)], sem))
+        else:
+            wait_for(from_z(l).at[pl.ds(0, Z - 1)], sem)
 
     def z_sum(l):
-        wait_recv(zr.at[l, pl.ds(0, Z - 1)], f"z{l}")
-        summed = lax.fori_loop(
-            1, Z, lambda k, so_far: so_far + zr[l, (zc + k) % Z].astype(F32), gf[l, block(f), :].astype(F32)
-        )
+        wait_recv(f"z{l}")
+        summed = g_block(l, f)[...].astype(F32)
+        if line:
+            one_side = jnp.where(zc == 0, 1, jnp.where(zc == Z - 1, Z - 2, zc - 1))
+            other_side = jnp.where(zc == 0, 2, jnp.where(zc == Z - 1, 1, zc + 1))
+            summed = summed + from_z(l)[one_side].astype(F32) + from_z(l)[other_side].astype(F32)
+            opposite = jnp.where(zc == 1, Z - 1, 0)
+            third = from_z(l)[opposite].astype(F32)
+            summed = summed + jnp.where(is_end, 0.0, third)
+        else:
+            summed = lax.fori_loop(1, Z, lambda k, so_far: so_far + from_z(l)[(zc + k) % Z].astype(F32), summed)
         summed = summed * (1.0 / root)
         if l < 4:
             gw[l][:, my_lanes] = summed.astype(gw[l].dtype)
@@ -272,33 +468,40 @@
 
     def rows_done(l):
         if l < 4:
-            wait_recv(gw[l].at[:, pl.ds(0, (R - 1) * CR)], f"rows{l}")
+            wait_recv(f"rows{l}")
         else:
-            wait_recv(hr.at[pl.ds(0, R - 1)], "rows4")
-            ghc[...] = sum(hr[i].astype(F32) for i in range(R))
+            wait_recv("rows4")
+            summed = sum(hr[i].astype(F32) for i in range(R))
+            wide = -(-half // LANES) * LANES
+            if wide > half:
+                summed = jnp.concatenate([summed, jnp.zeros((wide - half, LANES), F32)], axis=0)
+            summed = jnp.transpose(summed)
+            ghc[:, 0:half] = summed[0 : d.HC, 0:half]
+            ghc[:, half:rows] = summed[d.HC : 2 * d.HC, 0 : rows - half]
 
     def exchange(e):
         over(F, lambda k: send(st_s.at[e], st_r.at[e, f], (r, (f + k) % F), f"stat{e}"), 1)
         st_r[e, f] = st_s[e]
 
     def exchanged(e):
-        wait_recv(st_r.at[e, pl.ds(0, F - 1)], f"stat{e}")
+        wait_recv(f"stat{e}")
         return st_r[e]
 
     st_s[...] = jnp.zeros_like(st_s)
-    w_relay(0)
-    w_push(1)
-    wait_recv(s.at[0, pl.ds(0, (R - 1) * PD)], "images")
-    wait_recv(own_rows, "own_image")
+    w_relay_rest(0)
+    w_relay_near(0)
+    w_far(0)
+    wait_recv("images")
+    wait_recv("own_image")
 
     inverse_of, counts = [], None
     for l in range(4):
         w_finish(l)
         if l == 2:
-            wait_recv(pool_all.at[:, pl.ds(0, (R - 1) * CR)], "pool")
+            wait_recv("pool")
             s[2] = jnp.dot(u_sel[...], pool_all[...], preferred_element_type=F32).astype(BF16)
         elif l:
-            wait_recv(s.at[l, :, pl.ds(0, (R - 1) * CR)], f"ag{l - 1}")
+            wait_recv(f"ag{l - 1}")
         first = conv(s.at[l], M // PIX, l, zb)
         mean_here = first * (1.0 / M)
 
@@ -310,6 +513,9 @@
         if l == 0:
             st_s[l, 2:3, :] = sum(start_r[i, 0:1, :] for i in range(R))
         exchange(l)
+        if l != 1:
+            w_push_rest(l + 1)
+        w_push_near(l + 1)
         parts = exchanged(l)
         tot = jnp.sum(parts, axis=0)
         mean = tot[0:1] * (1.0 / total)
@@ -349,13 +555,26 @@
         else:
             here = s.at[l + 1, :, my_lanes]
             over(R, lambda k: send(here, here, rep_peer(k), f"ag{l}"), 1)
-        w_relay(l + 1)
-        if l < 3:
-            w_push(l + 2)
+        w_relay_rest(l + 1)
+        w_relay_near(l + 1)
+        if l == 0:
+            w_push_rest(2)
+        w_far(l + 1)
 
     w_finish(4)
-    wait_recv(s4.at[:, pl.ds(0, (R - 1) * CR)], "a2a")
-    wait_recv(ho_r.at[pl.ds(0, F - 1)], "head_out")
+    low_lanes = lax.broadcasted_iota(jnp.int32, (half, LANES), 1) < d.HC
+
+    def unpack(i, carry):
+        both = hp[i].astype(F32)
+        at = i * rows
+        wf[4, pl.ds(pl.multiple_of(at, d.row_tile), half), :] = jnp.where(low_lanes, both, 0.0).astype(wf.dtype)
+        high = jnp.where(low_lanes, pltpu.roll(both, d.HC, 1), 0.0).astype(wf.dtype)
+        wf[4, pl.ds(pl.multiple_of(at + half, d.row_tile), rows - half), :] = high[0 : rows - half]
+        return carry
+
+    lax.fori_loop(0, F, unpack, 0)
+    wait_recv("a2a")
+    wait_recv("head_out")
     conv(s4, PD // PIX, 4, zb)
     head_bias = jnp.concatenate([hb[...], jnp.zeros((1, CR - d.HC), F32)], axis=1)
     out_bias = jnp.concatenate([ob[...], jnp.zeros((1, CR - d.OC), F32)], axis=1)
@@ -403,7 +622,7 @@
         a2a_s[2 * half] = part[:, 0:CR].astype(BF16)
         a2a_s[2 * half + 1] = part[:, CR : 2 * CR].astype(BF16)
 
-    wait_send(a2a_r.at[pl.ds(0, R - 1)], "a2a")
+    wait_send("a2a")
     data_grad(4, PD, write_dh3)
     over(R, lambda k: send(a2a_s.at[(r + k) % R], a2a_r.at[r], rep_peer(k), "dh3"), 1)
     a2a_r[r] = a2a_s[r]
@@ -419,7 +638,7 @@
     rep_r[r] = rep_s[...]
 
     def head_small():
-        wait_recv(rep_r.at[pl.ds(0, R - 1)], "small_rep")
+        wait_recv("small_rep")
         summed = sum(rep_r[i] for i in range(R))
         for i in range(F):
             all_s[i, 0 : d.q, :] = summed[i * d.q : (i + 1) * d.q]
@@ -433,17 +652,17 @@
         e = 7 - l
         g_row, b_row = gain[l : l + 1, my_lanes], shift[l : l + 1, my_lanes]
         if l == 3:
-            wait_recv(a2a_r.at[pl.ds(0, R - 1)], "dh3")
+            wait_recv("dh3")
             entering = lambda i, at: a2a_r[i].astype(F32)
         elif l == 1:
-            wait_recv(ps_r.at[pl.ds(0, R - 1)], "rs2")
+            wait_recv("rs2")
             pooled = sum(ps_r[i].astype(F32) for i in range(R))
             inside, unused = windows(True)
             zb[...] = jnp.dot(jnp.where(inside, 0.25, 0.0), pooled, precision=EXACT, preferred_element_type=F32)
             entering = lambda i, at: zb[at, :]
         else:
             slot = 0 if l == 2 else 1
-            wait_recv(rs_r.at[slot, pl.ds(0, R - 1)], f"rs{l + 1}")
+            wait_recv(f"rs{l + 1}")
             entering = lambda i, at: sum(rs_r[slot, j, at, :].astype(F32) for j in range(R))
 
         def slopes(i, so_far):
@@ -463,8 +682,9 @@
         st_s[e, 0:1, :] = part_bias
         st_s[e, 1:2, :] = part_gain
         exchange(e)
+        core_sum(l + 1)
+        z_push(l + 1)
         if l == 3:
-            core_sum(4)
             head_small()
         else:
             z_sum(l + 2)
@@ -493,7 +713,7 @@
             over(R, lambda k: send(ps_s.at[(r + k) % R], ps_r.at[r], rep_peer(k), "rs2"), 1)
             ps_r[r] = ps_s[r]
             weight_grad(l, s.at[l], M)
-            core_sum(l)
+            z_middle(l + 1)
         elif l == 0:
             weight_grad(l, s.at[l], M)
 
@@ -504,7 +724,9 @@
             data_grad(l, M, write)
             over(R, lambda k: send(gi_s.at[(r + k) % R], gi_r.at[r], rep_peer(k), "rs0"), 1)
             gi_r[r] = gi_s[r]
-            core_sum(l)
+            z_middle(1)
+            core_sum(0)
+            z_push(0)
         else:
             slot = 0 if l == 3 else 1
 
@@ -516,46 +738,41 @@
             over(R, lambda k: send(rs_s.at[slot, (r + k) % R], rs_r.at[slot, r], rep_peer(k), f"rs{l}"), 1)
             rs_r[slot, r] = rs_s[slot, r]
             weight_grad(l, s.at[l], M)
-            core_sum(l)
+            z_middle(l + 1)
 
     gnorm[:, my_lanes] = norm_s[...]
     over(R, lambda k: send(norm_s, gnorm.at[:, my_lanes], rep_peer(k), "norms"), 1)
+    z_middle(0)
     z_sum(1)
-    wait_recv(all_r.at[pl.ds(0, F - 1)], "small_all")
+    wait_recv("small_all")
     gsmall[...] = jnp.sum(all_r[...], axis=0) * (1.0 / root)
     rows_done(4)
     rows_done(3)
     rows_done(2)
-    wait_recv(gi_r.at[pl.ds(0, R - 1)], "rs0")
+    wait_recv("rs0")
     gi[...] = sum(gi_r[i].astype(F32) for i in range(R))
     z_sum(0)
-    wait_recv(gnorm.at[:, pl.ds(0, (R - 1) * CR)], "norms")
+    wait_recv("norms")
     rows_done(1)
     rows_done(0)
 
-    wait_send(s.at[0, pl.ds(0, (R - 1) * PD)], "images")
-    wait_send(start_r.at[pl.ds(0, R - 1)], "start")
-    wait_send(ho_r.at[pl.ds(0, F - 1)], "head_out")
-    wait_send(pool_all.at[:, pl.ds(0, (R - 1) * CR)], "pool")
-    for i in (0, 2):
-        wait_send(s.at[i + 1, :, pl.ds(0, (R - 1) * CR)], f"ag{i}")
-    wait_send(a2a_r.at[pl.ds(0, R - 1)], "dh3")
-    wait_send(rs_r.at[0, pl.ds(0, R - 1)], "rs3")
-    wait_send(ps_r.at[pl.ds(0, R - 1)], "rs2")
-    wait_send(rs_r.at[1, pl.ds(0, R - 1)], "rs1")
-    wait_send(gi_r.at[pl.ds(0, R - 1)], "rs0")
-    wait_send(gnorm.at[:, pl.ds(0, (R - 1) * CR)], "norms")
-    wait_send(rep_r.at[pl.ds(0, R - 1)], "small_rep")
-    wait_send(all_r.at[pl.ds(0, F - 1)], "small_all")
-    for e in range(8):
-        wait_send(st_r.at[e, pl.ds(0, F - 1)], f"stat{e}")
-    for l in range(5):
-        wait_send(cr.at[l], f"core{l}")
-        wait_send(zr.at[l, pl.ds(0, Z - 1)], f"z{l}")
-        wait_send(gw[l].at[:, pl.ds(0, (R - 1) * CR)] if l < 4 else hr.at[pl.ds(0, R - 1)], f"rows{l}")
-        one = wf.at[l, block(f)]
-        over(Z, lambda k: pltpu.make_async_copy(one, one, wsf.at[l, k]).wait())
-        over(Z, lambda k: pltpu.make_async_copy(one, one, wsz.at[l, k]).wait(), 1)
+    drain()
+
+
+def finish(gi, gw0, gw1, gw2, gw3, ghc, gnorm, gsmall, *outs):
+    out_gi, out0, out1, out2, out3, out_hc, out_ho, out_gain, out_bias, out_hb, out_ob = outs
+    out_gi[...] = gi[...]
+    for src, dst in ((gw0, out0), (gw1, out1), (gw2, out2), (gw3, out3)):
+        dst[...] = src[...].astype(F32)
+
+    @pl.when(pl.program_id(0) == 0)
+    def _():
+        out_hc[...] = ghc[...]
+        out_ho[...] = gsmall[0 : out_ho.shape[0], 0 : out_ho.shape[1]]
+        out_gain[...] = gnorm[0:4, :]
+        out_bias[...] = gnorm[4:8, :]
+        out_hb[...] = gsmall[8:9, 0 : out_hb.shape[1]]
+        out_ob[...] = gsmall[9:10, 0 : out_ob.shape[1]]
 
 
 def per_device(
@@ -567,13 +784,14 @@
     rows, hidden = head_conv.shape
     q, out_ch = head_out.shape
     d = types.SimpleNamespace(
-        R=R, F=F, Z=F // 2, rows=rows, C=channels, CR=channels // R, W=breadth, PIX=height * breadth,
+        n=n, R=R, F=F, Z=F // 2, rows=rows, C=channels, CR=channels // R, W=breadth, PIX=height * breadth,
         PD=n * height * breadth, HC=hidden, OC=out_ch, q=q,
     )
     d.M = R * d.PD
     d.PW = d.M // 4
     wire = BF16 if rows % 16 == 0 else F32
     d.row_tile = 16 if rows % 16 == 0 else 8
+    d.half = -(-rows // (2 * d.row_tile)) * d.row_tile
     vm = pltpu.VMEM
     patch = 9 * channels
     scratch = [
@@ -596,11 +814,15 @@
         vm((R, d.PW, d.CR), BF16),
         vm((R, d.PD, d.C), BF16),
         vm((R, d.PD, d.C), BF16),
-        vm((5, patch, d.CR), wire),
-        vm((5, d.Z, rows, d.CR), wire),
-        vm((5, d.Z, rows, d.CR), wire),
-        vm((R, rows, d.CR), wire),
-        vm((rows, LANES), wire),
+        vm((4, patch, d.CR), wire),
+        vm((4, d.Z, rows, d.CR), wire),
+        vm((4, d.Z, rows, d.CR), wire),
+        vm((d.half, LANES), wire),
+        vm((F, d.half, LANES), wire),
+        vm((F, d.half, LANES), wire),
+        vm((d.Z, d.half, LANES), wire),
+        vm((d.Z, d.half, LANES), wire),
+        vm((R, d.half, LANES), wire),
         vm((8, 8, LANES), F32),
         vm((8, F, 8, LANES), F32),
         vm((8, LANES), F32),
@@ -621,27 +843,43 @@
         pltpu.SemaphoreType.DMA((5, d.Z)),
     ]
     here, there = pl.BlockSpec(memory_space=pltpu.VMEM), pl.BlockSpec(memory_space=pl.ANY)
-    row_type = BF16 if rows % 16 == 0 else F32
     shape = jax.ShapeDtypeStruct
-    gi, gw0, gw1, gw2, gw3, ghc, gnorm, gsmall = pl.pallas_call(
+    kept = pl.pallas_call(
         functools.partial(kernel, d),
         out_shape=[shape((d.PD, d.C), F32)]
-        + [shape((rows, d.C), row_type)] * 4
-        + [shape((rows, LANES), F32), shape((8, d.C), F32), shape((16, LANES), F32)],
+        + [shape((rows, d.C), wire)] * 4
+        + [shape((hidden, rows), F32), shape((8, d.C), F32), shape((16, LANES), F32)],
         in_specs=[there] * 5 + [here] * 11,
         out_specs=[here] * 8,
         scratch_shapes=scratch,
         compiler_params=pltpu.CompilerParams(collective_id=0, has_side_effects=True, vmem_limit_bytes=60 * 2**20),
     )(
         images.reshape(d.PD, channels),
-        *(w.astype(wire) for w in (enc_first, enc_second, dec_first, dec_second, head_conv)),
-        head_out, norm_gain, norm_bias, head_bias.reshape(1, hidden), out_bias.reshape(1, out_ch),
-        task_weights.reshape(1, 3), pool_index.reshape(1, -1), labels.reshape(1, -1),
-        jnp.transpose(task_masks, (1, 0, 2)).reshape(3, -1), jnp.transpose(targets, (1, 0, 2)).reshape(4, -1),
+        *(w.astype(wire) for w in (enc_first, enc_second, dec_first, dec_second)),
+        head_conv.T, head_out, norm_gain, norm_bias, head_bias.reshape(1, hidden), out_bias.reshape(1, out_ch),
+        task_weights.reshape(1, 3), pool_index, labels, jnp.transpose(task_masks, (1, 0, 2)), targets,
     )
+    steps = next(count for count in (4, 3, 2, 1) if rows % (count * d.row_tile) == 0 and d.PD % (count * 8) == 0)
+    part = lambda height, width: pl.BlockSpec((height // steps, width), lambda i: (i, 0))
+    all_of = lambda height, width: pl.BlockSpec((height, width), lambda i: (0, 0))
+    rest = ((q, out_ch), (4, channels), (4, channels), (1, hidden), (1, out_ch))
+    gi, gw0, gw1, gw2, gw3, ghc, gq, gain, bias, ghb, gob = pl.pallas_call(
+        finish,
+        grid=(steps,),
+        out_shape=[shape((d.PD, channels), F32)]
+        + [shape((rows, channels), F32)] * 4
+        + [shape((hidden, rows), F32)]
+        + [shape(size, F32) for size in rest],
+        in_specs=[part(d.PD, channels)]
+        + [part(rows, channels)] * 4
+        + [all_of(hidden, rows), all_of(8, channels), all_of(16, LANES)],
+        out_specs=[part(d.PD, channels)]
+        + [part(rows, channels)] * 4
+        + [all_of(hidden, rows)]
+        + [all_of(*size) for size in rest],
+    )(*kept)
     return (
-        gi.reshape(images.shape), gw0.astype(F32), gw1.astype(F32), gw2.astype(F32), gw3.astype(F32), ghc[:, :hidden],
-        gsmall[:q, :out_ch], gnorm[0:4], gnorm[4:8], gsmall[8, :hidden], gsmall[9, :out_ch],
+        gi.reshape(images.shape), gw0, gw1, gw2, gw3, ghc.T, gq, gain, bias, ghb.reshape(hidden), gob.reshape(out_ch),
     )
 
 

time: 214 us -> 175 us (0.82)
  Pallas kernels: 197 us -> 174 us
  local copies, waits for them, and re-layouts: 10.6 us -> 0 us
  other arithmetic: 5.73 us -> 0 us
    pallas_call x1, Pallas kernels: 197 us -> 169 us  [per_device(): pl.pallas_call(functools.partial(kernel, d), out_shape=[shape((d.PD, d.C)...]
    convert_element_type x4 -> x0, other arithmetic: 5.73 us -> none  [the longest x1 2.23 us: per_device(): gw0.astype(F32)]
    unnamed x12 -> x0, local copies, waits for them, and re-layouts: 5.48 us -> none
    pallas_call x0 -> x1, Pallas kernels: none -> 5.1 us  [per_device(): pl.pallas_call(finish, grid=(steps,), out_shape=[shape((d.PD, channels),...]
    slice x2 -> x0, local copies, waits for them, and re-layouts: 2.66 us -> none  [the longest x1 1.4 us: per_device(): gnorm[4:8]]
    squeeze x2 -> x0, local copies, waits for them, and re-layouts: 2.43 us -> none  [the longest x1 1.25 us: per_device(): gsmall[9, :out_ch]]
where the time goes in v2:
time: 175 us
  Pallas kernels  174 us (99%)
    pallas_call x1, Pallas kernels, per_device(): pl.pallas_call(functools.partial(kernel, d), out_shape=[shape((d.PD, d.C)...  169 us
    pallas_call x1, Pallas kernels, per_device(): pl.pallas_call(finish, grid=(steps,), out_shape=[shape((d.PD, channels),...  5.1 us

profile of v2, /device:TPU:0, one launch (start us, length us, event | category | flops | bytes accessed | tf_op | source)
XLA Modules:
  0.0 175.0 jit_solution(13129846614288594658)
XLA Ops:
  0.7 169.1 %shard_map.239 = (f32[192,512]{1,0:T(8,128)}, bf16[576,512]{1,0:T(8,128)(2,1)}, bf16[576,512]{1,0:T(8,128)(2,1)}, bf16[576,512]{1,0:T(8,128)(2,1)}, bf16[576,512...) custom-call(bf16[192,512]{1,0:T(8,128)(2,1)} %bitcast.10, bf16[576,512]{1,0:T(8,128)(2,1)} %refs_1_.1, ...), custom_call_target="tpu_custom_call" | custom-call | tf_op jit(solution)/shard_map/pallas_call | solution.py:847
  169.7 5.1 %shard_map.240 = (f32[192,512]{1,0:T(8,128)}, f32[576,512]{1,0:T(8,128)}, f32[576,512]{1,0:T(8,128)}, f32[576,512]{1,0:T(8,128)}, f32[576,512]{1,0:T(8,128)}, /*...) custom-call(f32[192,512]{1,0:T(8,128)} %get-tuple-element.30.gi, ...), custom_call_target="tpu_custom_call" | custom-call | tf_op jit(solution)/shard_map/pallas_call | solution.py:866

commit v3 on v2

--- a/solution.py
+++ b/solution.py
@@ -16,14 +16,21 @@
 EXACT = lax.Precision.HIGHEST
 
 GROUPS = (
-    ["images", "start", "head_out", "a2a", "pool", "dh3", "rs3", "rs2", "rs1", "rs0", "norms", "small_rep", "small_all"]
-    + [f"ag{i}" for i in (0, 2)]
+    ["images", "start", "head_out", "a2a", "pool", "dh3", "rs2", "norms", "small_rep", "small_all"]
+    + [f"sums{i}" for i in range(2)]
+    + [f"norm{i}" for i in range(2)]
+    + [
+        f"{name}{way}"
+        for name in ("ag0", "ag2", "rs3", "rs1", "rs0", "rows0", "rows1", "rows2", "rows3")
+        for way in ("x0", "x1", "y0", "y1", "f0", "f1")
+    ]
     + [f"stat{i}" for i in range(8)]
     + [f"core{i}" for i in range(5)]
     + [f"z{i}" for i in range(5)]
     + [f"mid{i}" for i in range(5)]
-    + [f"rows{i}" for i in range(5)]
+    + ["rows4"]
     + [f"own{i}" for i in range(5)]
+    + [f"out{i}" for i in range(4)]
     + ["own_image"]
 )
 GROUP = {name: number for number, name in enumerate(GROUPS)}
@@ -34,7 +41,9 @@
     take = lambda count: [next(it) for _ in range(count)]
     images, w0, w1, w2, w3, hw, ho, gain, shift, hb, ob, tw, pidx, lab, msk, tgt = take(16)
     gi, gw0, gw1, gw2, gw3, ghc, gnorm, gsmall = take(8)
-    (s, s4, wf, y, zb, zhat, d9, u_sel, ut_sel, a2a_s, a2a_r, rs_s, rs_r, pool_own, pool_all, ps_s, ps_r, gi_s, gi_r) = take(19)
+    gather, columns_s = take(2)
+    (s, s4, wf, y, zb, zhat, d9, u_sel, ut_sel, a2a_s, a2a_r, rs_s, rs_l, pool_own, pool_all, ps_s, ps_r, gi_s, gi_l) = take(19)
+    (zg, slope, slope_z, nrm_s, nrm_r, sums_s, sums_r) = take(7)
     (gf, cr, zr, hw_s, hp, hg, hcr, hzr, hr, st_s, st_r, start_s, start_r, ho_s, ho_r, rep_s, rep_r, all_s, all_r, norm_s, feat) = take(21)
     ssem, rsem, wsz, wrz, wsf, wrf = take(6)
     w_in, gw = (w0, w1, w2, w3, hw_s), (gw0, gw1, gw2, gw3)
@@ -46,6 +55,9 @@
     zc, core = f // 2, f % 2
     sib = (r, zc * 2 + (1 - core))
     rep_peer = lambda k: ((r + k) % R, f)
+    one, two = r + 1 - 2 * (r % 2), (r + 2) % R
+    both = (one + 2) % R
+    at_one, at_two = (one, f), (two, f)
     z_peer = lambda k: (r, ((zc + k) % Z) * 2 + core)
     line = Z == 4
     is_end = (zc == 0) | (zc == Z - 1)
@@ -70,10 +82,7 @@
         "a2a": lambda: s4.at[:, pl.ds(0, (R - 1) * CR)],
         "pool": lambda: pool_all.at[:, pl.ds(0, (R - 1) * CR)],
         "dh3": first_of(a2a_r, R - 1),
-        "rs3": first_of(rs_r.at[0], R - 1),
         "rs2": first_of(ps_r, R - 1),
-        "rs1": first_of(rs_r.at[1], R - 1),
-        "rs0": first_of(gi_r, R - 1),
         "norms": lambda: gnorm.at[:, pl.ds(0, (R - 1) * CR)],
         "small_rep": first_of(rep_r, R - 1),
         "small_all": first_of(all_r, F - 1),
@@ -81,14 +90,23 @@
         "core4": lambda: hcr,
         "mid4": lambda: hzr.at[0],
     }
-    for l in (0, 2):
-        volume[f"ag{l}"] = lambda l=l: s.at[l + 1, :, pl.ds(0, (R - 1) * CR)]
+    for way in ("x", "y", "f"):
+        for h in range(2):
+            for j in range(2):
+                volume[f"ag{2 * j}{way}{h}"] = lambda j=j: zg.at[j, pl.ds(0, M // 2), pl.ds(0, CR)]
+                volume[f"rs{2 * j + 1}{way}{h}"] = lambda j=j: rs_l.at[j, 0]
+            volume[f"rs0{way}{h}"] = lambda: gi_l.at[0]
+            size = half if h == 0 else rows - half
+            for l in range(4):
+                volume[f"rows{l}{way}{h}"] = lambda l=l, size=size: gather.at[l, pl.ds(0, size), pl.ds(0, CR)]
+    for j in range(2):
+        volume[f"sums{j}"] = first_of(sums_r.at[j], R - 1)
+        volume[f"norm{j}"] = first_of(nrm_r.at[j], R - 1)
     for e in range(8):
         volume[f"stat{e}"] = first_of(st_r.at[e], F - 1)
     for l in range(4):
         volume[f"core{l}"] = lambda l=l: cr.at[l]
         volume[f"mid{l}"] = lambda l=l: zr.at[l, 0]
-        volume[f"rows{l}"] = lambda l=l: gw[l].at[:, pl.ds(0, (R - 1) * CR)]
 
     def wait_for(ref, sem):
         pltpu.make_async_copy(ref, ref, sem).wait()
@@ -240,27 +258,16 @@
     ho_s[0 : d.q, 0 : d.OC] = ho[...].astype(F32)
     over(F, lambda k: send(ho_s, ho_r.at[f], (r, (f + k) % F), "head_out"), 1)
     ho_r[f] = ho_s[...]
-    wide = -(-rows // LANES) * LANES
-    tall = jnp.concatenate([hw[...].astype(F32), jnp.zeros((LANES - d.HC, rows), F32)], axis=0)
-    if wide > rows:
-        tall = jnp.concatenate([tall, jnp.zeros((LANES, wide - rows), F32)], axis=1)
-    tall = jnp.transpose(tall)
-    if wide < 2 * half:
-        tall = jnp.concatenate([tall, jnp.zeros((2 * half - wide, LANES), F32)], axis=0)
-    hw_s[...] = (tall[0:half] + pltpu.roll(tall[half : 2 * half], d.HC, 1)).astype(hw_s.dtype)
-
-    feat[...] = jnp.zeros_like(feat)
-    feat[0:1, 0:PD] = labels
-    feat[1:4, 0:PD] = masks
-    feat[4:8, 0:PD] = wanted
-    columns = jnp.transpose(feat[...])[0:PD, :]
-
-    wait_recv("start")
-    feat[...] = jnp.zeros_like(feat)
-    for i in range(R):
-        feat[0:1, i * (PW // R) : (i + 1) * (PW // R)] = start_r[i, 1:2, 0 : PW // R]
-    picked_row = feat[0:1, 0:PW]
-    picked_col = jnp.transpose(feat[...])[0:PW, 0:1]
+    def pack_head():
+        wide = -(-rows // LANES) * LANES
+        tall = jnp.concatenate([hw[...].astype(F32), jnp.zeros((LANES - d.HC, rows), F32)], axis=0)
+        if wide > rows:
+            tall = jnp.concatenate([tall, jnp.zeros((LANES, wide - rows), F32)], axis=1)
+        tall = jnp.transpose(tall)
+        if wide < 2 * half:
+            tall = jnp.concatenate([tall, jnp.zeros((2 * half - wide, LANES), F32)], axis=0)
+        hw_s[...] = (tall[0:half] + pltpu.roll(tall[half : 2 * half], d.HC, 1)).astype(hw_s.dtype)
+
     bits = W.bit_length() - 1
 
     def places(axis, shape):
@@ -279,10 +286,23 @@
         other = lax.broadcasted_iota(jnp.int32, shape, 1 if rows_first else 0)
         return window == other, position
 
-    inside, position = windows(True)
-    u_sel[...] = jnp.where(inside & (position == picked_row), 1.0, 0.0).astype(BF16)
-    inside, position = windows(False)
-    ut_sel[...] = jnp.where(inside & (position == picked_col), 1.0, 0.0).astype(BF16)
+    def pixel_columns():
+        feat[...] = jnp.zeros_like(feat)
+        feat[0:1, 0:PD] = labels
+        feat[1:4, 0:PD] = masks
+        feat[4:8, 0:PD] = wanted
+        columns_s[...] = jnp.transpose(feat[...])[0:PD, 0:LANES]
+
+    def pool_matrices():
+        feat[...] = jnp.zeros_like(feat)
+        for i in range(R):
+            feat[0:1, i * (PW // R) : (i + 1) * (PW // R)] = start_r[i, 1:2, 0 : PW // R]
+        picked_row = feat[0:1, 0:PW]
+        picked_col = jnp.transpose(feat[...])[0:PW, 0:1]
+        inside, position = windows(True)
+        u_sel[...] = jnp.where(inside & (position == picked_row), 1.0, 0.0).astype(BF16)
+        inside, position = windows(False)
+        ut_sel[...] = jnp.where(inside & (position == picked_col), 1.0, 0.0).astype(BF16)
 
     def image_rows(i):
         return pl.ds(pl.multiple_of(i * PIX, PIX), PIX)
@@ -358,6 +378,61 @@
             )
             write(half, part)
 
+    def lanes_of(owner):
+        return pl.ds(pl.multiple_of(owner * CR, CR), CR)
+
+    def gather_start(name, piece):
+        send(piece(r, 0), piece(r, 0), at_one, f"{name}x0")
+        send(piece(r, 1), piece(r, 1), at_two, f"{name}y1")
+        send(piece(r, 1), piece(r, 1), at_one, f"{name}x1")
+        send(piece(r, 0), piece(r, 0), at_two, f"{name}y0")
+
+    def gather_forward(name, piece):
+        wait_recv(f"{name}x0")
+        send(piece(one, 0), piece(one, 0), at_two, f"{name}f0")
+        wait_recv(f"{name}y1")
+        send(piece(two, 1), piece(two, 1), at_one, f"{name}f1")
+
+    def await_rest(name):
+        for way in ("x1", "y0", "f0", "f1"):
+            wait_recv(f"{name}{way}")
+
+    def scatter_start(name, piece, land):
+        send(piece(both, 0), land(0), at_one, f"{name}x0")
+        send(piece(both, 1), land(2), at_two, f"{name}y1")
+        send(piece(one, 0), land(1), at_one, f"{name}x1")
+        send(piece(two, 1), land(3), at_two, f"{name}y0")
+
+    def scatter_forward(name, piece, land):
+        for way, ref, came, dst, to, group in (
+            ("x0", piece(two, 0), land(0), land(4), at_two, "f0"),
+            ("y1", piece(one, 1), land(2), land(5), at_one, "f1"),
+        ):
+            wait_recv(f"{name}{way}")
+            ref[...] = (ref[...].astype(F32) + came[...].astype(F32)).astype(ref.dtype)
+            send(ref, dst, to, f"{name}{group}")
+
+    def ag_piece(j):
+        return lambda owner, h: zg.at[j, pl.ds(h * (M // 2), M // 2), lanes_of(owner)]
+
+    def rows_piece(l):
+        return lambda owner, h: gather.at[l, pl.ds(h * half, half if h == 0 else rows - half), lanes_of(owner)]
+
+    def rs_piece(j):
+        return lambda owner, h: rs_s.at[j, owner, pl.ds(h * (M // 2), M // 2)]
+
+    def rs_land(j):
+        return lambda i: rs_l.at[j, i]
+
+    def gi_piece(owner, h):
+        return gi_s.at[owner, pl.ds(h * (PD // 2), PD // 2)]
+
+    def gi_land(i):
+        return gi_l.at[i]
+
+    def sigmoid(v):
+        return 0.5 * jnp.tanh(0.5 * v) + 0.5
+
     def g_block(l, owner):
         return gf.at[l, block(owner)] if l < 4 else hg.at[owner]
 
@@ -459,16 +534,16 @@
             summed = lax.fori_loop(1, Z, lambda k, so_far: so_far + from_z(l)[(zc + k) % Z].astype(F32), summed)
         summed = summed * (1.0 / root)
         if l < 4:
-            gw[l][:, my_lanes] = summed.astype(gw[l].dtype)
-            here = gw[l].at[:, my_lanes]
-            over(R, lambda k: send(here, here, rep_peer(k), f"rows{l}"), 1)
+            gather[l, :, my_lanes] = summed.astype(gather.dtype)
+            gather_start(f"rows{l}", rows_piece(l))
         else:
             hr[r] = summed.astype(hr.dtype)
             over(R, lambda k: send(hr.at[r], hr.at[r], rep_peer(k), "rows4"), 1)
 
     def rows_done(l):
         if l < 4:
-            wait_recv(f"rows{l}")
+            await_rest(f"rows{l}")
+            copy_here(gather.at[l], gw[l], f"out{l}")
         else:
             wait_recv("rows4")
             summed = sum(hr[i].astype(F32) for i in range(R))
@@ -493,29 +568,66 @@
     w_far(0)
     wait_recv("images")
     wait_recv("own_image")
-
+    wait_recv("start")
+
+    rep_all = lambda src, dst, group: over(R, lambda k: send(src, dst, rep_peer(k), group), 1)
+    images_here = M // PIX
     inverse_of, counts = [], None
+
+    def w_relay(l):
+        w_relay_rest(l)
+        w_relay_near(l)
+
+    def widened(j, i, b):
+        value = zg[j, image_rows(i), b * CR : (b + 1) * CR].astype(F32)
+        return value, [nrm_r[j, b, k : k + 1, :] for k in range(4)]
+
+    def slopes_of(j):
+        def body(i, carry):
+            for b in range(R):
+                value, (a, o, inverse, off) = widened(j, i, b)
+                shaped = value * a + o
+                squashed = sigmoid(shaped)
+                steep = squashed + shaped * squashed * (1.0 - squashed)
+                slope[j, image_rows(i), b * CR : (b + 1) * CR] = steep.astype(BF16)
+                slope_z[j, image_rows(i), b * CR : (b + 1) * CR] = (steep * (value * inverse + off)).astype(BF16)
+            return carry
+
+        per_image(images_here, body, 0)
+
     for l in range(4):
         w_finish(l)
         if l == 2:
             wait_recv("pool")
             s[2] = jnp.dot(u_sel[...], pool_all[...], preferred_element_type=F32).astype(BF16)
-        elif l:
-            wait_recv(f"ag{l - 1}")
-        first = conv(s.at[l], M // PIX, l, zb)
+        first = conv(s.at[l], images_here, l, zb)
         mean_here = first * (1.0 / M)
+        j = l // 2
+        gathers = l in (0, 2)
 
         def squares(i, so_far):
-            return so_far + jnp.sum(jnp.square(zb[image_rows(i), :] - mean_here), axis=0, keepdims=True)
-
+            apart = zb[image_rows(i), :] - mean_here
+            if gathers:
+                zg[j, image_rows(i), my_lanes] = apart.astype(BF16)
+            return so_far + jnp.sum(jnp.square(apart), axis=0, keepdims=True)
+
+        squared = per_image(images_here, squares, jnp.zeros((1, CR), F32))
+        if gathers:
+            gather_start(f"ag{l}", ag_piece(j))
         st_s[l, 0:1, :] = first
-        st_s[l, 1:2, :] = per_image(M // PIX, squares, jnp.zeros((1, CR), F32))
+        st_s[l, 1:2, :] = squared
         if l == 0:
             st_s[l, 2:3, :] = sum(start_r[i, 0:1, :] for i in range(R))
         exchange(l)
         if l != 1:
             w_push_rest(l + 1)
         w_push_near(l + 1)
+        if gathers:
+            gather_forward(f"ag{l}", ag_piece(j))
+        elif l == 1:
+            pixel_columns()
+        else:
+            slopes_of(1)
         parts = exchanged(l)
         tot = jnp.sum(parts, axis=0)
         mean = tot[0:1] * (1.0 / total)
@@ -525,22 +637,39 @@
         if l == 0:
             counts = tot[2:3]
         g_row, b_row = gain[l : l + 1, my_lanes], shift[l : l + 1, my_lanes]
+        if gathers:
+            off = (mean_here - mean) * inverse
+            nrm_s[j, 0:1, :] = inverse * g_row
+            nrm_s[j, 1:2, :] = off * g_row + b_row
+            nrm_s[j, 2:3, :] = inverse
+            nrm_s[j, 3:4, :] = off
+            rep_all(nrm_s.at[j], nrm_r.at[j, r], f"norm{j}")
+            nrm_r[j, r] = nrm_s[j]
 
         def activate(i, carry):
             at = image_rows(i)
             normed = (zb[at, :] - mean) * inverse
             zhat[l, at, :] = normed
             shaped = normed * g_row + b_row
-            hidden = shaped * jax.nn.sigmoid(shaped)
+            hidden = shaped * sigmoid(shaped)
             if l == 1:
                 zb[at, :] = hidden
-            elif l == 3:
+            else:
                 a2a_s[i] = hidden.astype(BF16)
-            else:
-                s[l + 1, at, my_lanes] = hidden.astype(BF16)
             return carry
 
-        per_image(M // PIX, activate, 0)
+        def keep_normed(i, carry):
+            zhat[l, image_rows(i), :] = (zb[image_rows(i), :] - mean) * inverse
+            return carry
+
+        def activate_all(i, carry):
+            for b in range(R):
+                value, (a, o, unused, also) = widened(j, i, b)
+                shaped = value * a + o
+                s[l + 1, image_rows(i), b * CR : (b + 1) * CR] = (shaped * sigmoid(shaped)).astype(BF16)
+            return carry
+
+        per_image(images_here, keep_normed if gathers else activate, 0)
         if l == 1:
             inside, unused = windows(False)
             pooled = jnp.dot(
@@ -548,17 +677,22 @@
             )
             pool_own[...] = pooled.astype(BF16)
             pool_all[:, my_lanes] = pooled.astype(BF16)
-            over(R, lambda k: send(pool_own, pool_all.at[:, my_lanes], rep_peer(k), "pool"), 1)
+            rep_all(pool_own, pool_all.at[:, my_lanes], "pool")
+            slopes_of(0)
         elif l == 3:
             over(R, lambda k: send(a2a_s.at[(r + k) % R], s4.at[:, my_lanes], rep_peer(k), "a2a"), 1)
             s4[:, my_lanes] = a2a_s[r]
+        elif l == 0:
+            pool_matrices()
         else:
-            here = s.at[l + 1, :, my_lanes]
-            over(R, lambda k: send(here, here, rep_peer(k), f"ag{l}"), 1)
-        w_relay_rest(l + 1)
-        w_relay_near(l + 1)
+            pack_head()
+        w_relay(l + 1)
         if l == 0:
             w_push_rest(2)
+        if gathers:
+            wait_recv(f"norm{j}")
+            await_rest(f"ag{l}")
+            per_image(images_here, activate_all, 0)
         w_far(l + 1)
 
     w_finish(4)
@@ -579,14 +713,14 @@
     head_bias = jnp.concatenate([hb[...], jnp.zeros((1, CR - d.HC), F32)], axis=1)
     out_bias = jnp.concatenate([ob[...], jnp.zeros((1, CR - d.OC), F32)], axis=1)
     head_raw = zb[0:PD, :] + head_bias
-    squashed = jax.nn.sigmoid(head_raw)
+    squashed = sigmoid(head_raw)
     head_act = head_raw * squashed
     project = jnp.concatenate([ho_r[i][0 : d.q] for i in range(F)] + [jnp.zeros((LANES - d.HC, LANES), F32)], axis=0)
     out = jnp.dot(head_act, project, precision=EXACT, preferred_element_type=F32) + out_bias
     lane = lax.broadcasted_iota(jnp.int32, (PD, LANES), 1)
     classes = d.OC - 4
     factor = total * jnp.concatenate([tw[...], jnp.zeros((1, LANES - 3), F32)], axis=1) / jnp.maximum(counts, 1.0)
-    pixel = [columns[:, i : i + 1] for i in range(8)]
+    pixel = [columns_s[:, i : i + 1] for i in range(8)]
     is_class = lane < classes
     top = jnp.max(jnp.where(is_class, out, -jnp.inf), axis=1, keepdims=True)
     grown = jnp.where(is_class, jnp.exp(jnp.where(is_class, out - top, 0.0)), 0.0)
@@ -648,29 +782,21 @@
         over(F, lambda k: send(all_s.at[(f + k) % F], all_r.at[f], (r, (f + k) % F), "small_all"), 1)
         all_r[f] = all_s[f]
 
-    for l in (3, 2, 1, 0):
-        e = 7 - l
-        g_row, b_row = gain[l : l + 1, my_lanes], shift[l : l + 1, my_lanes]
-        if l == 3:
-            wait_recv("dh3")
-            entering = lambda i, at: a2a_r[i].astype(F32)
-        elif l == 1:
-            wait_recv("rs2")
-            pooled = sum(ps_r[i].astype(F32) for i in range(R))
-            inside, unused = windows(True)
-            zb[...] = jnp.dot(jnp.where(inside, 0.25, 0.0), pooled, precision=EXACT, preferred_element_type=F32)
-            entering = lambda i, at: zb[at, :]
-        else:
-            slot = 0 if l == 2 else 1
-            wait_recv(f"rs{l + 1}")
-            entering = lambda i, at: sum(rs_r[slot, j, at, :].astype(F32) for j in range(R))
-
-        def slopes(i, so_far):
+    def rows_of(l):
+        return gain[l : l + 1, my_lanes], shift[l : l + 1, my_lanes]
+
+    def slope_here(l, at):
+        g_row, b_row = rows_of(l)
+        normed = zhat[l, at, :]
+        shaped = normed * g_row + b_row
+        squashed = sigmoid(shaped)
+        return normed, squashed + shaped * squashed * (1.0 - squashed)
+
+    def enter(l, entering):
+        def body(i, so_far):
             at = image_rows(i)
-            normed = zhat[l, at, :]
-            shaped = normed * g_row + b_row
-            squashed = jax.nn.sigmoid(shaped)
-            grad = entering(i, at) * (squashed + shaped * squashed * (1.0 - squashed))
+            normed, steep = slope_here(l, at)
+            grad = entering(i, at) * steep
             zb[at, :] = grad
             return (
                 so_far[0] + jnp.sum(grad, axis=0, keepdims=True),
@@ -678,82 +804,144 @@
             )
 
         none = jnp.zeros((1, CR), F32)
-        part_bias, part_gain = per_image(M // PIX, slopes, (none, none))
-        st_s[e, 0:1, :] = part_bias
-        st_s[e, 1:2, :] = part_gain
-        exchange(e)
-        core_sum(l + 1)
-        z_push(l + 1)
-        if l == 3:
-            head_small()
-        else:
-            z_sum(l + 2)
-        tot = jnp.sum(exchanged(e), axis=0)
+        part_bias, part_gain = per_image(images_here, body, (none, none))
+        st_s[7 - l, 0:1, :] = part_bias
+        st_s[7 - l, 1:2, :] = part_gain
+        exchange(7 - l)
+
+    def through_norm(l, grad_of):
+        tot = jnp.sum(exchanged(7 - l), axis=0)
         bias_sum, gain_sum = tot[0:1], tot[1:2]
         norm_s[l : l + 1, :] = gain_sum * (1.0 / root)
         norm_s[4 + l : 5 + l, :] = bias_sum * (1.0 / root)
-        scale = inverse_of[l] * g_row
-
-        def through_norm(i, carry):
+        scale = inverse_of[l] * rows_of(l)[0]
+        if l in (0, 2):
+            await_rest(f"rs{l + 1}")
+
+        def body(i, carry):
             at = image_rows(i)
-            spread_taps(
-                i, scale * (zb[at, :] - bias_sum * (1.0 / total) - zhat[l, at, :] * (gain_sum * (1.0 / total)))
+            normed, grad = grad_of(i, at)
+            spread_taps(i, scale * (grad - bias_sum * (1.0 / total) - normed * (gain_sum * (1.0 / total))))
+            return carry
+
+        per_image(images_here, body, 0)
+
+    def from_zb(l):
+        return lambda i, at: (zhat[l, at, :], zb[at, :])
+
+    def from_scatter(l):
+        j = l // 2
+        here = images_here // 2
+
+        def grad_of(i, at):
+            normed, steep = slope_here(l, at)
+            h = i // here
+            local = image_rows(i - h * here)
+            grad = (
+                rs_s[j, r, at, :].astype(F32)
+                + rs_l[j, 1 + 2 * h, local, :].astype(F32)
+                + rs_l[j, 4 + h, local, :].astype(F32)
             )
-            return carry
-
-        per_image(M // PIX, through_norm, 0)
-        if l == 2:
-
-            def write(half, part):
-                chosen = jnp.dot(ut_sel[...], part.astype(BF16), preferred_element_type=F32).astype(BF16)
-                ps_s[2 * half] = chosen[:, 0:CR]
-                ps_s[2 * half + 1] = chosen[:, CR : 2 * CR]
-
-            data_grad(l, M, write)
-            over(R, lambda k: send(ps_s.at[(r + k) % R], ps_r.at[r], rep_peer(k), "rs2"), 1)
-            ps_r[r] = ps_s[r]
-            weight_grad(l, s.at[l], M)
-            z_middle(l + 1)
-        elif l == 0:
-            weight_grad(l, s.at[l], M)
-
-            def write(half, part):
-                for i in range(R):
-                    gi_s[i, :, half * 2 * CR : (half + 1) * 2 * CR] = part[i * PD : (i + 1) * PD].astype(BF16)
-
-            data_grad(l, M, write)
-            over(R, lambda k: send(gi_s.at[(r + k) % R], gi_r.at[r], rep_peer(k), "rs0"), 1)
-            gi_r[r] = gi_s[r]
-            z_middle(1)
-            core_sum(0)
-            z_push(0)
-        else:
-            slot = 0 if l == 3 else 1
-
-            def write(half, part):
-                rs_s[slot, 2 * half] = part[:, 0:CR].astype(BF16)
-                rs_s[slot, 2 * half + 1] = part[:, CR : 2 * CR].astype(BF16)
-
-            data_grad(l, M, write)
-            over(R, lambda k: send(rs_s.at[slot, (r + k) % R], rs_r.at[slot, r], rep_peer(k), f"rs{l}"), 1)
-            rs_r[slot, r] = rs_s[slot, r]
-            weight_grad(l, s.at[l], M)
-            z_middle(l + 1)
+            return normed, grad * steep
+
+        return grad_of
+
+    def layer_down(l):
+        j = (l - 1) // 2
+
+        def write(part_at, part):
+            for b in range(2):
+                n = 2 * part_at + b
+                grad = part[:, b * CR : (b + 1) * CR]
+                rs_s[j, n] = grad.astype(BF16)
+                cols = slice(n * CR, (n + 1) * CR)
+                sums_s[j, n, 0:1, :] = jnp.sum(grad * slope[j, :, cols].astype(F32), axis=0, keepdims=True)
+                sums_s[j, n, 1:2, :] = jnp.sum(grad * slope_z[j, :, cols].astype(F32), axis=0, keepdims=True)
+
+        data_grad(l, M, write)
+        over(R, lambda k: send(sums_s.at[j, (r + k) % R], sums_r.at[j, r], rep_peer(k), f"sums{j}"), 1)
+        scatter_start(f"rs{l}", rs_piece(j), rs_land(j))
+        sums_r[j, r] = sums_s[j, r]
+        weight_grad(l, s.at[l], M)
+        wait_recv(f"sums{j}")
+        e = 7 - (l - 1)
+        st_s[e, 0:2, :] = sum(sums_r[j, i, 0:2, :] for i in range(R))
+        exchange(e)
+        scatter_forward(f"rs{l}", rs_piece(j), rs_land(j))
+
+    wait_recv("dh3")
+    enter(3, lambda i, at: a2a_r[i].astype(F32))
+    core_sum(4)
+    z_push(4)
+    head_small()
+    through_norm(3, from_zb(3))
+    layer_down(3)
+    z_middle(4)
+    core_sum(3)
+    z_push(3)
+
+    through_norm(2, from_scatter(2))
+
+    def write_pooled(part_at, part):
+        chosen = jnp.dot(ut_sel[...], part.astype(BF16), preferred_element_type=F32).astype(BF16)
+        ps_s[2 * part_at] = chosen[:, 0:CR]
+        ps_s[2 * part_at + 1] = chosen[:, CR : 2 * CR]
+
+    data_grad(2, M, write_pooled)
+    over(R, lambda k: send(ps_s.at[(r + k) % R], ps_r.at[r], rep_peer(k), "rs2"), 1)
+    ps_r[r] = ps_s[r]
+    weight_grad(2, s.at[2], M)
+    z_middle(3)
+    wait_recv("rs2")
+    pooled = sum(ps_r[i].astype(F32) for i in range(R))
+    inside, unused = windows(True)
+    zb[...] = jnp.dot(jnp.where(inside, 0.25, 0.0), pooled, precision=EXACT, preferred_element_type=F32)
+    enter(1, lambda i, at: zb[at, :])
+    core_sum(2)
+    z_push(2)
+    z_sum(4)
+    z_sum(3)
+    through_norm(1, from_zb(1))
+    gather_forward("rows3", rows_piece(3))
+    layer_down(1)
+    z_middle(2)
+    core_sum(1)
+    z_push(1)
+
+    through_norm(0, from_scatter(0))
+    weight_grad(0, s.at[0], M)
+    z_sum(2)
+
+    def write_images(part_at, part):
+        for i in range(R):
+            gi_s[i, :, part_at * 2 * CR : (part_at + 1) * 2 * CR] = part[i * PD : (i + 1) * PD].astype(BF16)
+
+    data_grad(0, M, write_images)
+    scatter_start("rs0", gi_piece, gi_land)
+    gather_forward("rows2", rows_piece(2))
+    z_middle(1)
+    core_sum(0)
+    z_push(0)
 
     gnorm[:, my_lanes] = norm_s[...]
-    over(R, lambda k: send(norm_s, gnorm.at[:, my_lanes], rep_peer(k), "norms"), 1)
+    rep_all(norm_s, gnorm.at[:, my_lanes], "norms")
     z_middle(0)
+    scatter_forward("rs0", gi_piece, gi_land)
     z_sum(1)
     wait_recv("small_all")
     gsmall[...] = jnp.sum(all_r[...], axis=0) * (1.0 / root)
     rows_done(4)
     rows_done(3)
+    gather_forward("rows1", rows_piece(1))
     rows_done(2)
-    wait_recv("rs0")
-    gi[...] = sum(gi_r[i].astype(F32) for i in range(R))
+    await_rest("rs0")
+    for h in range(2):
+        at = slice(h * (PD // 2), (h + 1) * (PD // 2))
+        gi[at, :] = gi_s[r, at, :].astype(F32) + gi_l[1 + 2 * h].astype(F32) + gi_l[4 + h].astype(F32)
     z_sum(0)
     wait_recv("norms")
     rows_done(1)
+    gather_forward("rows0", rows_piece(0))
     rows_done(0)
 
     drain()
@@ -795,6 +983,8 @@
     vm = pltpu.VMEM
     patch = 9 * channels
     scratch = [
+        vm((4, rows, d.C), wire),
+        vm((d.PD, LANES), F32),
         vm((4, d.M, d.C), BF16),
         vm((d.PD, d.C), BF16),
         vm((5, patch, d.CR), wire),
@@ -807,13 +997,20 @@
         vm((R, d.PD, d.CR), BF16),
         vm((R, d.PD, d.CR), BF16),
         vm((2, R, d.M, d.CR), BF16),
-        vm((2, R, d.M, d.CR), BF16),
+        vm((2, 6, d.M // 2, d.CR), BF16),
         vm((d.PW, d.CR), BF16),
         vm((d.PW, d.C), BF16),
         vm((R, d.PW, d.CR), BF16),
         vm((R, d.PW, d.CR), BF16),
         vm((R, d.PD, d.C), BF16),
-        vm((R, d.PD, d.C), BF16),
+        vm((6, d.PD // 2, d.C), BF16),
+        vm((2, d.M, d.C), BF16),
+        vm((2, d.M, d.C), BF16),
+        vm((2, d.M, d.C), BF16),
+        vm((2, 8, LANES), F32),
+        vm((2, R, 8, LANES), F32),
+        vm((2, R, 8, LANES), F32),
+        vm((2, R, 8, LANES), F32),
         vm((4, patch, d.CR), wire),
         vm((4, d.Z, rows, d.CR), wire),
         vm((4, d.Z, rows, d.CR), wire),
@@ -850,7 +1047,7 @@
         + [shape((rows, d.C), wire)] * 4
         + [shape((hidden, rows), F32), shape((8, d.C), F32), shape((16, LANES), F32)],
         in_specs=[there] * 5 + [here] * 11,
-        out_specs=[here] * 8,
+        out_specs=[here] + [there] * 4 + [here] * 3,
         scratch_shapes=scratch,
         compiler_params=pltpu.CompilerParams(collective_id=0, has_side_effects=True, vmem_limit_bytes=60 * 2**20),
     )(
@@ -859,7 +1056,7 @@
         head_conv.T, head_out, norm_gain, norm_bias, head_bias.reshape(1, hidden), out_bias.reshape(1, out_ch),
         task_weights.reshape(1, 3), pool_index, labels, jnp.transpose(task_masks, (1, 0, 2)), targets,
     )
-    steps = next(count for count in (4, 3, 2, 1) if rows % (count * d.row_tile) == 0 and d.PD % (count * 8) == 0)
+    steps = next(count for count in (2, 1) if rows % (count * d.row_tile) == 0 and d.PD % (count * 8) == 0)
     part = lambda height, width: pl.BlockSpec((height // steps, width), lambda i: (i, 0))
     all_of = lambda height, width: pl.BlockSpec((height, width), lambda i: (0, 0))
     rest = ((q, out_ch), (4, channels), (4, channels), (1, hidden), (1, out_ch))

time: 175 us -> 157 us (0.90)
  Pallas kernels: 174 us -> 156 us
    pallas_call x1, Pallas kernels: 169 us -> 152 us  [per_device(): pl.pallas_call(functools.partial(kernel, d), out_shape=[shape((d.PD, d.C)...]
where the time goes in v3:
time: 157 us
  Pallas kernels  156 us (99%)
    pallas_call x1, Pallas kernels, per_device(): pl.pallas_call(functools.partial(kernel, d), out_shape=[shape((d.PD, d.C)...  152 us
    pallas_call x1, Pallas kernels, per_device(): pl.pallas_call(finish, grid=(steps,), out_shape=[shape((d.PD, channels),...  4.15 us

profile of v3, /device:TPU:0, one launch (start us, length us, event | category | flops | bytes accessed | tf_op | source)
XLA Modules:
  0.0 157.3 jit_solution(7416295317188545839)
XLA Ops:
  0.7 152.3 %shard_map.239 = (f32[192,512]{1,0:T(8,128)}, bf16[576,512]{1,0:T(8,128)(2,1)}, bf16[576,512]{1,0:T(8,128)(2,1)}, bf16[576,512]{1,0:T(8,128)(2,1)}, bf16[576,512...) custom-call(bf16[192,512]{1,0:T(8,128)(2,1)} %bitcast.10, bf16[576,512]{1,0:T(8,128)(2,1)} %refs_1_.1, ...), custom_call_target="tpu_custom_call" | custom-call | tf_op jit(solution)/shard_map/pallas_call | solution.py:1044
  153.0 4.1 %shard_map.240 = (f32[192,512]{1,0:T(8,128)}, f32[576,512]{1,0:T(8,128)}, f32[576,512]{1,0:T(8,128)}, f32[576,512]{1,0:T(8,128)}, f32[576,512]{1,0:T(8,128)}, /*...) custom-call(f32[192,512]{1,0:T(8,128)} %get-tuple-element.30.gi, ...), custom_call_target="tpu_custom_call" | custom-call | tf_op jit(solution)/shard_map/pallas_call | solution.py:1063

commit v4 on v3

--- a/solution.py
+++ b/solution.py
@@ -26,8 +26,8 @@
     ]
     + [f"stat{i}" for i in range(8)]
     + [f"core{i}" for i in range(5)]
-    + [f"z{i}" for i in range(5)]
-    + [f"mid{i}" for i in range(5)]
+    + [f"z{i}.{h}" for i in range(5) for h in range(2)]
+    + [f"mid{i}.{h}" for i in range(5) for h in range(2)]
     + ["rows4"]
     + [f"own{i}" for i in range(5)]
     + [f"out{i}" for i in range(4)]
@@ -88,7 +88,6 @@
         "small_all": first_of(all_r, F - 1),
         "rows4": first_of(hr, R - 1),
         "core4": lambda: hcr,
-        "mid4": lambda: hzr.at[0],
     }
     for way in ("x", "y", "f"):
         for h in range(2):
@@ -106,7 +105,6 @@
         volume[f"stat{e}"] = first_of(st_r.at[e], F - 1)
     for l in range(4):
         volume[f"core{l}"] = lambda l=l: cr.at[l]
-        volume[f"mid{l}"] = lambda l=l: zr.at[l, 0]
 
     def wait_for(ref, sem):
         pltpu.make_async_copy(ref, ref, sem).wait()
@@ -162,79 +160,121 @@
     over(F, lambda k: pl.semaphore_signal(barrier, inc=1, device_id=(r, (f + k) % F), device_id_type=MESH), 1)
     pl.semaphore_wait(barrier, R + F - 2)
 
-    def w_block(l, owner):
-        return wf.at[l, block(owner)] if l < 4 else hp.at[owner]
-
-    def w_copy(l, src, owner, to, send_sem, recv_sem):
+    pieces = range(d.pieces)
+
+    def cut(l, h):
+        size = rows if l < 4 else half
+        first = -(-size // (d.pieces * d.row_tile)) * d.row_tile
+        return (0, first) if h == 0 else (first, size - first)
+
+    def cut_at(l, h):
+        first, size = cut(l, h)
+        return pl.ds(first, size)
+
+    near = sorted({1, Z - 1})
+    beyond = list(range(2, Z - 1))
+
+    def w_block(l, owner, h):
+        first, size = cut(l, h)
+        if l < 4:
+            return wf.at[l, pl.ds(pl.multiple_of(owner * rows + first, d.row_tile), size)]
+        return hp.at[owner, pl.ds(first, size)]
+
+    def w_copy(l, h, src, owner, to, send_sem, recv_sem):
         return pltpu.make_async_remote_copy(
-            src_ref=src, dst_ref=w_block(l, owner), send_sem=send_sem, recv_sem=recv_sem, device_id=to, device_id_type=MESH
+            src_ref=src, dst_ref=w_block(l, owner, h), send_sem=send_sem, recv_sem=recv_sem, device_id=to, device_id_type=MESH
         )
 
-    def w_src(l):
-        return w_in[l].at[:, my_lanes] if l < 4 else hw_s
-
-    def w_send(l, k):
-        arriving["near" if k in (1, Z - 1) else "rest", l, k] = lambda: direct(Z - k, lambda: w_wait(l, wrz.at[l, k]))
-        leaving["w", l, k] = lambda: direct(k, lambda: w_wait(l, wsz.at[l, k]))
-        direct(k, lambda: w_copy(l, w_src(l), f, z_peer(k), wsz.at[l, k], wrz.at[l, k]).start())
+    def w_src(l, h):
+        return w_in[l].at[cut_at(l, h), my_lanes] if l < 4 else hw_s.at[cut_at(l, h)]
+
+    def w_wait(l, h, sem):
+        wait_for(w_block(l, f, h), sem)
+
+    def w_send(l, h, k, who=lambda body: body()):
+        u = l * d.pieces + h
+        arriving["z", l, h, k] = lambda: direct(Z - k, lambda: w_wait(l, h, wrz.at[u, k]))
+        leaving["z", l, h, k] = lambda: direct(k, lambda: w_wait(l, h, wsz.at[u, k]))
+        start = lambda: w_copy(l, h, w_src(l, h), f, z_peer(k), wsz.at[u, k], wrz.at[u, k]).start()
+        who(lambda: direct(k, start))
+
+    def w_relayed(l, h, k):
+        u = l * d.pieces + h
+        arriving["core", l, h, k] = lambda: w_wait(l, h, wrf.at[u, k])
+        leaving["core", l, h, k] = lambda: w_wait(l, h, wsf.at[u, k])
 
     def w_push_near(l):
-        for k in sorted({1, Z - 1}):
-            w_send(l, k)
-        w_copy(l, w_src(l), f, sib, wsf.at[l, 0], wrf.at[l, 0]).start()
-        arriving["core", l, 0] = lambda: w_wait(l, wrf.at[l, 0])
-        leaving["core", l, 0] = lambda: w_wait(l, wsf.at[l, 0])
-        copy_here(w_src(l), w_block(l, f), f"own{l}")
-
-    def w_push_rest(l):
-        for k in range(2, Z - 1):
-            w_send(l, k)
-
-    def w_wait(l, sem):
-        pltpu.make_async_copy(w_block(l, f), w_block(l, f), sem).wait()
-
-    def w_arrived(l, k):
+        for h in pieces:
+            u = l * d.pieces + h
+            for k in near:
+                w_send(l, h, k)
+            w_copy(l, h, w_src(l, h), f, sib, wsf.at[u, 0], wrf.at[u, 0]).start()
+            w_relayed(l, h, 0)
+        copy_here(w_in[l].at[:, my_lanes] if l < 4 else hw_s, wf.at[l, block(f)] if l < 4 else hp.at[f], f"own{l}")
+
+    def w_push_rest(l, hs=pieces, who=lambda body: body()):
+        for h in hs:
+            for k in beyond:
+                w_send(l, h, k, who)
+
+    def at_ends(body):
+        if line:
+            when(is_end, body)
+        else:
+            body()
+
+    def between(body):
+        if line:
+            when(jnp.logical_not(is_end), body)
+
+    def w_arrived(l, h, k):
+        u = l * d.pieces + h
         owner = ((zc + Z - k) % Z) * 2 + core
-        w_wait(l, wrz.at[l, k])
-        w_copy(l, w_block(l, owner), owner, sib, wsf.at[l, k], wrf.at[l, k]).start()
-
-    def w_relayed(l, k):
-        arriving["core", l, k] = lambda: w_wait(l, wrf.at[l, k])
-        leaving["core", l, k] = lambda: w_wait(l, wsf.at[l, k])
-
-    def w_relay_rest(l):
-        for k in range(2, Z - 1):
-            arriving.pop(("rest", l, k))
-            w_arrived(l, k)
-            w_relayed(l, k)
-        if line:
-
-            def hand_on():
-                to = (Z - 1) * (zc - 1)
-                owner = (Z - 1 - to) * 2 + core
-                slot = jnp.where(zc == 1, 1, Z - 1)
-                w_copy(l, w_block(l, owner), owner, (r, to * 2 + core), wsz.at[l, 0], wrz.at[l, slot]).start()
-
-            when(jnp.logical_not(is_end), hand_on)
-            leaving["far", l] = lambda: when(jnp.logical_not(is_end), lambda: w_wait(l, wsz.at[l, 0]))
+        w_wait(l, h, wrz.at[u, k])
+        w_copy(l, h, w_block(l, owner, h), owner, sib, wsf.at[u, k], wrf.at[u, k]).start()
+
+    def w_relay_rest(l, hs=pieces):
+        for h in hs:
+            u = l * d.pieces + h
+            for k in beyond:
+                arriving.pop(("z", l, h, k))
+                w_arrived(l, h, k)
+                w_relayed(l, h, k)
+            if line:
+
+                def hand_on():
+                    to = (Z - 1) * (zc - 1)
+                    owner = (Z - 1 - to) * 2 + core
+                    slot = jnp.where(zc == 1, 1, Z - 1)
+                    w_copy(
+                        l, h, w_block(l, owner, h), owner, (r, to * 2 + core), wsz.at[u, 0], wrz.at[u, slot]
+                    ).start()
+
+                when(jnp.logical_not(is_end), hand_on)
+                leaving["far", l, h] = lambda u=u, h=h: when(
+                    jnp.logical_not(is_end), lambda: w_wait(l, h, wsz.at[u, 0])
+                )
 
     def w_relay_near(l):
-        for k in sorted({1, Z - 1}):
-            arriving.pop(("near", l, k))
-            direct(Z - k, lambda: w_arrived(l, k))
-            if not line:
-                w_relayed(l, k)
+        for h in pieces:
+            for k in near:
+                arriving.pop(("z", l, h, k))
+                direct(Z - k, lambda: w_arrived(l, h, k))
+                if not line:
+                    w_relayed(l, h, k)
 
     def w_far(l):
         if line:
-            for k in (1, Z - 1):
-                w_relayed(l, k)
-            when(zc == 0, lambda: w_arrived(l, 1))
-            when(zc == Z - 1, lambda: w_arrived(l, Z - 1))
+            for h in pieces:
+                for k in near:
+                    w_relayed(l, h, k)
+                when(zc == 0, lambda: w_arrived(l, h, 1))
+                when(zc == Z - 1, lambda: w_arrived(l, h, Z - 1))
 
     def w_finish(l):
-        for k in range(Z):
-            wait_recv(("core", l, k))
+        for h in pieces:
+            for k in range(Z):
+                wait_recv(("core", l, h, k))
         wait_recv(f"own{l}")
 
     w_push_rest(0)
@@ -439,8 +479,14 @@
     def from_core(l):
         return cr.at[l] if l < 4 else hcr
 
-    def from_z(l):
-        return zr.at[l] if l < 4 else hzr
+    def from_z(l, i, h):
+        return zr.at[l, i, cut_at(l, h)] if l < 4 else hzr.at[i, cut_at(l, h)]
+
+    def g_piece(l, owner, h):
+        first, size = cut(l, h)
+        if l < 4:
+            return gf.at[l, pl.ds(pl.multiple_of(owner * rows + first, d.row_tile), size)]
+        return hg.at[owner, pl.ds(first, size)]
 
     def weight_grad(l, src, height):
         for kx in range(3):
@@ -477,20 +523,30 @@
         over(Z, step)
 
     def z_push(l):
+        for h in pieces:
+            z_push_middle(l, h)
+        for h in pieces:
+            z_push_piece(l, h)
+
+    def z_push_middle(l, h):
+        if line:
+
+            def to_middle():
+                through, owner = jnp.where(zc == 0, 1, Z - 2), Z - 1 - zc
+                send(g_piece(l, 2 * owner + core, h), from_z(l, through, h), (r, 2 * through + core), f"mid{l}.{h}")
+
+            when(is_end, to_middle)
+            g = GROUP[f"mid{l}.{h}"]
+            arriving[f"mid{l}.{h}"] = lambda: when(
+                jnp.logical_not(is_end), lambda: wait_for(from_z(l, 0, h), rsem.at[g])
+            )
+            leaving[f"mid{l}.{h}"] = lambda: when(is_end, lambda: wait_for(from_z(l, 0, h), ssem.at[g]))
+
+    def z_push_piece(l, h):
         def push(k):
             to = (zc + k) % Z
-            send(g_block(l, 2 * to + core), from_z(l).at[zc], (r, 2 * to + core), f"z{l}")
-
-        if line:
-
-            def to_middle():
-                through, owner = jnp.where(zc == 0, 1, Z - 2), Z - 1 - zc
-                send(g_block(l, 2 * owner + core), from_z(l).at[through], (r, 2 * through + core), f"mid{l}")
-
-            when(is_end, to_middle)
-            middle, outside = arriving.pop(f"mid{l}"), leaving.pop(f"mid{l}")
-            arriving[f"mid{l}"] = lambda: when(jnp.logical_not(is_end), middle)
-            leaving[f"mid{l}"] = lambda: when(is_end, outside)
+            send(g_piece(l, 2 * to + core, h), from_z(l, zc, h), (r, 2 * to + core), f"z{l}.{h}")
+
         for k in range(1, Z) if Z <= 8 else ():
             if line and k == 2:
                 when(is_end, lambda: push(2))
@@ -498,47 +554,58 @@
                 direct(k, lambda: push(k))
         if Z > 8:
             over(Z, push, 1)
-        arriving[f"z{l}"] = lambda: z_wait(l, rsem.at[GROUP[f"z{l}"]])
-        leaving[f"z{l}"] = lambda: z_wait(l, ssem.at[GROUP[f"z{l}"]])
+        arriving[f"z{l}.{h}"] = lambda: z_wait(l, h, rsem.at[GROUP[f"z{l}.{h}"]])
+        leaving[f"z{l}.{h}"] = lambda: z_wait(l, h, ssem.at[GROUP[f"z{l}.{h}"]])
 
     def z_middle(l):
+        for h in pieces:
+            z_middle_piece(l, h)
+
+    def z_middle_piece(l, h):
         if line:
-            wait_recv(f"mid{l}")
+            wait_recv(f"mid{l}.{h}")
 
             def hand_on():
                 owner = (Z - 1) * (Z - 2 - zc)
-                ref = g_block(l, 2 * owner + core)
-                ref[...] = (ref[...].astype(F32) + from_z(l)[zc].astype(F32)).astype(ref.dtype)
-                send(ref, from_z(l).at[zc], (r, 2 * owner + core), f"z{l}")
+                ref = g_piece(l, 2 * owner + core, h)
+                ref[...] = (ref[...].astype(F32) + from_z(l, zc, h)[...].astype(F32)).astype(ref.dtype)
+                send(ref, from_z(l, zc, h), (r, 2 * owner + core), f"z{l}.{h}")
 
             when(jnp.logical_not(is_end), hand_on)
 
-    def z_wait(l, sem):
+    def z_wait(l, h, sem):
+        first, size = cut(l, h)
+        many = lambda count: (zr.at[l, pl.ds(0, count), cut_at(l, h)] if l < 4 else hzr.at[pl.ds(0, count), cut_at(l, h)])
         if line:
-            when(is_end, lambda: wait_for(from_z(l).at[pl.ds(0, Z - 2)], sem))
-            when(jnp.logical_not(is_end), lambda: wait_for(from_z(l).at[pl.ds(0, Z - 1)], sem))
+            when(is_end, lambda: wait_for(many(Z - 2), sem))
+            when(jnp.logical_not(is_end), lambda: wait_for(many(Z - 1), sem))
         else:
-            wait_for(from_z(l).at[pl.ds(0, Z - 1)], sem)
+            wait_for(many(Z - 1), sem)
 
     def z_sum(l):
-        wait_recv(f"z{l}")
-        summed = g_block(l, f)[...].astype(F32)
+        for h in pieces:
+            z_sum_piece(l, h)
+        if l < 4:
+            gather_start(f"rows{l}", rows_piece(l))
+        else:
+            over(R, lambda k: send(hr.at[r], hr.at[r], rep_peer(k), "rows4"), 1)
+
+    def z_sum_piece(l, h):
+        wait_recv(f"z{l}.{h}")
+        read = lambda i: from_z(l, i, h)[...].astype(F32)
+        summed = g_piece(l, f, h)[...].astype(F32)
         if line:
             one_side = jnp.where(zc == 0, 1, jnp.where(zc == Z - 1, Z - 2, zc - 1))
             other_side = jnp.where(zc == 0, 2, jnp.where(zc == Z - 1, 1, zc + 1))
-            summed = summed + from_z(l)[one_side].astype(F32) + from_z(l)[other_side].astype(F32)
             opposite = jnp.where(zc == 1, Z - 1, 0)
-            third = from_z(l)[opposite].astype(F32)
-            summed = summed + jnp.where(is_end, 0.0, third)
+            summed = summed + read(one_side) + read(other_side) + jnp.where(is_end, 0.0, read(opposite))
         else:
-            summed = lax.fori_loop(1, Z, lambda k, so_far: so_far + from_z(l)[(zc + k) % Z].astype(F32), summed)
+            summed = lax.fori_loop(1, Z, lambda k, so_far: so_far + read((zc + k) % Z), summed)
         summed = summed * (1.0 / root)
         if l < 4:
-            gather[l, :, my_lanes] = summed.astype(gather.dtype)
-            gather_start(f"rows{l}", rows_piece(l))
+            gather[l, cut_at(l, h), my_lanes] = summed.astype(gather.dtype)
         else:
-            hr[r] = summed.astype(hr.dtype)
-            over(R, lambda k: send(hr.at[r], hr.at[r], rep_peer(k), "rows4"), 1)
+            hr[r, cut_at(l, h)] = summed.astype(hr.dtype)
 
     def rows_done(l):
         if l < 4:
@@ -566,6 +633,7 @@
     w_relay_rest(0)
     w_relay_near(0)
     w_far(0)
+    w_push_rest(1, who=at_ends)
     wait_recv("images")
     wait_recv("own_image")
     wait_recv("start")
@@ -573,10 +641,6 @@
     rep_all = lambda src, dst, group: over(R, lambda k: send(src, dst, rep_peer(k), group), 1)
     images_here = M // PIX
     inverse_of, counts = [], None
-
-    def w_relay(l):
-        w_relay_rest(l)
-        w_relay_near(l)
 
     def widened(j, i, b):
         value = zg[j, image_rows(i), b * CR : (b + 1) * CR].astype(F32)
@@ -619,9 +683,17 @@
         if l == 0:
             st_s[l, 2:3, :] = sum(start_r[i, 0:1, :] for i in range(R))
         exchange(l)
-        if l != 1:
-            w_push_rest(l + 1)
-        w_push_near(l + 1)
+        if l == 0:
+            w_push_rest(1, who=between)
+            w_push_near(1)
+            w_relay_rest(1)
+        elif l < 3:
+            w_push_rest(l + 1, pieces[1:])
+            w_push_near(l + 1)
+            w_relay_rest(l + 1, pieces[:1])
+        else:
+            w_push_near(4)
+            w_relay_rest(4)
         if gathers:
             gather_forward(f"ag{l}", ag_piece(j))
         elif l == 1:
@@ -678,6 +750,7 @@
             pool_own[...] = pooled.astype(BF16)
             pool_all[:, my_lanes] = pooled.astype(BF16)
             rep_all(pool_own, pool_all.at[:, my_lanes], "pool")
+            w_relay_rest(2, pieces[1:])
             slopes_of(0)
         elif l == 3:
             over(R, lambda k: send(a2a_s.at[(r + k) % R], s4.at[:, my_lanes], rep_peer(k), "a2a"), 1)
@@ -685,15 +758,18 @@
         elif l == 0:
             pool_matrices()
         else:
+            w_relay_rest(3, pieces[1:])
             pack_head()
-        w_relay(l + 1)
-        if l == 0:
-            w_push_rest(2)
+        w_relay_near(l + 1)
+        if l < 2:
+            w_push_rest(l + 2, pieces[:1])
+        elif l == 2:
+            w_push_rest(4)
+        w_far(l + 1)
         if gathers:
             wait_recv(f"norm{j}")
             await_rest(f"ag{l}")
             per_image(images_here, activate_all, 0)
-        w_far(l + 1)
 
     w_finish(4)
     low_lanes = lax.broadcasted_iota(jnp.int32, (half, LANES), 1) < d.HC
@@ -862,12 +938,15 @@
         over(R, lambda k: send(sums_s.at[j, (r + k) % R], sums_r.at[j, r], rep_peer(k), f"sums{j}"), 1)
         scatter_start(f"rs{l}", rs_piece(j), rs_land(j))
         sums_r[j, r] = sums_s[j, r]
+        z_middle_piece(l + 1, 0)
         weight_grad(l, s.at[l], M)
         wait_recv(f"sums{j}")
         e = 7 - (l - 1)
         st_s[e, 0:2, :] = sum(sums_r[j, i, 0:2, :] for i in range(R))
         exchange(e)
         scatter_forward(f"rs{l}", rs_piece(j), rs_land(j))
+        for h in pieces[1:]:
+            z_middle_piece(l + 1, h)
 
     wait_recv("dh3")
     enter(3, lambda i, at: a2a_r[i].astype(F32))
@@ -876,7 +955,6 @@
     head_small()
     through_norm(3, from_zb(3))
     layer_down(3)
-    z_middle(4)
     core_sum(3)
     z_push(3)
 
@@ -887,11 +965,11 @@
         ps_s[2 * part_at] = chosen[:, 0:CR]
         ps_s[2 * part_at + 1] = chosen[:, CR : 2 * CR]
 
+    z_middle(3)
     data_grad(2, M, write_pooled)
     over(R, lambda k: send(ps_s.at[(r + k) % R], ps_r.at[r], rep_peer(k), "rs2"), 1)
     ps_r[r] = ps_s[r]
     weight_grad(2, s.at[2], M)
-    z_middle(3)
     wait_recv("rs2")
     pooled = sum(ps_r[i].astype(F32) for i in range(R))
     inside, unused = windows(True)
@@ -904,13 +982,13 @@
     through_norm(1, from_zb(1))
     gather_forward("rows3", rows_piece(3))
     layer_down(1)
-    z_middle(2)
     core_sum(1)
     z_push(1)
+    z_sum(2)
 
     through_norm(0, from_scatter(0))
     weight_grad(0, s.at[0], M)
-    z_sum(2)
+    gather_forward("rows2", rows_piece(2))
 
     def write_images(part_at, part):
         for i in range(R):
@@ -918,7 +996,6 @@
 
     data_grad(0, M, write_images)
     scatter_start("rs0", gi_piece, gi_land)
-    gather_forward("rows2", rows_piece(2))
     z_middle(1)
     core_sum(0)
     z_push(0)
@@ -938,10 +1015,24 @@
     for h in range(2):
         at = slice(h * (PD // 2), (h + 1) * (PD // 2))
         gi[at, :] = gi_s[r, at, :].astype(F32) + gi_l[1 + 2 * h].astype(F32) + gi_l[4 + h].astype(F32)
-    z_sum(0)
+    last = rows_piece(0)
+    if d.pieces == 2:
+        z_sum_piece(0, 0)
+        send(last(r, 0), last(r, 0), at_one, "rows0x0")
+        send(last(r, 0), last(r, 0), at_two, "rows0y0")
+        send(last(r, 0), last(r, 0), (both, f), "rows0f0")
+        rows_done(1)
+        z_sum_piece(0, 1)
+        send(last(r, 1), last(r, 1), at_one, "rows0x1")
+        send(last(r, 1), last(r, 1), at_two, "rows0y1")
+        send(last(r, 1), last(r, 1), (both, f), "rows0f1")
+        wait_recv("rows0x0")
+        wait_recv("rows0y1")
+    else:
+        z_sum(0)
+        rows_done(1)
+        gather_forward("rows0", last)
     wait_recv("norms")
-    rows_done(1)
-    gather_forward("rows0", rows_piece(0))
     rows_done(0)
 
     drain()
@@ -976,6 +1067,7 @@
         PD=n * height * breadth, HC=hidden, OC=out_ch, q=q,
     )
     d.M = R * d.PD
+    d.pieces = 2 if d.Z == 4 else 1
     d.PW = d.M // 4
     wire = BF16 if rows % 16 == 0 else F32
     d.row_tile = 16 if rows % 16 == 0 else 8
@@ -1034,10 +1126,10 @@
         vm((LANES, 2 * LANES), F32),
         pltpu.SemaphoreType.DMA((len(GROUPS),)),
         pltpu.SemaphoreType.DMA((len(GROUPS),)),
-        pltpu.SemaphoreType.DMA((5, d.Z)),
-        pltpu.SemaphoreType.DMA((5, d.Z)),
-        pltpu.SemaphoreType.DMA((5, d.Z)),
-        pltpu.SemaphoreType.DMA((5, d.Z)),
+        pltpu.SemaphoreType.DMA((5 * d.pieces, d.Z)),
+        pltpu.SemaphoreType.DMA((5 * d.pieces, d.Z)),
+        pltpu.SemaphoreType.DMA((5 * d.pieces, d.Z)),
+        pltpu.SemaphoreType.DMA((5 * d.pieces, d.Z)),
     ]
     here, there = pl.BlockSpec(memory_space=pltpu.VMEM), pl.BlockSpec(memory_space=pl.ANY)
     shape = jax.ShapeDtypeStruct

time: 157 us -> 152 us (0.968)
  Pallas kernels: 156 us -> 151 us
    pallas_call x1, Pallas kernels: 152 us -> 147 us  [per_device(): pl.pallas_call(functools.partial(kernel, d), out_shape=[shape((d.PD, d.C)...]
where the time goes in v4:
time: 152 us
  Pallas kernels  151 us (99%)
    pallas_call x1, Pallas kernels, per_device(): pl.pallas_call(functools.partial(kernel, d), out_shape=[shape((d.PD, d.C)...  147 us
    pallas_call x1, Pallas kernels, per_device(): pl.pallas_call(finish, grid=(steps,), out_shape=[shape((d.PD, channels),...  4.15 us

profile of v4, /device:TPU:0, one launch (start us, length us, event | category | flops | bytes accessed | tf_op | source)
XLA Modules:
  0.0 152.2 jit_solution(1714493590277627666)
XLA Ops:
  0.7 147.2 %shard_map.239 = (f32[192,512]{1,0:T(8,128)}, bf16[576,512]{1,0:T(8,128)(2,1)}, bf16[576,512]{1,0:T(8,128)(2,1)}, bf16[576,512]{1,0:T(8,128)(2,1)}, bf16[576,512...) custom-call(bf16[192,512]{1,0:T(8,128)(2,1)} %bitcast.10, bf16[576,512]{1,0:T(8,128)(2,1)} %refs_1_.1, ...), custom_call_target="tpu_custom_call" | custom-call | tf_op jit(solution)/shard_map/pallas_call | solution.py:1136
  147.9 4.1 %shard_map.240 = (f32[192,512]{1,0:T(8,128)}, f32[576,512]{1,0:T(8,128)}, f32[576,512]{1,0:T(8,128)}, f32[576,512]{1,0:T(8,128)}, f32[576,512]{1,0:T(8,128)}, /*...) custom-call(f32[192,512]{1,0:T(8,128)} %get-tuple-element.30.gi, ...), custom_call_target="tpu_custom_call" | custom-call | tf_op jit(solution)/shard_map/pallas_call | solution.py:1155

commit v5 on v4

--- a/solution.py
+++ b/solution.py
@@ -17,8 +17,9 @@
 
 GROUPS = (
     ["images", "start", "head_out", "a2a", "pool", "dh3", "rs2", "norms", "small_rep", "small_all"]
-    + [f"sums{i}" for i in range(2)]
-    + [f"norm{i}" for i in range(2)]
+    + [f"sums{i}" for i in range(4)]
+    + ["pool_slope"]
+    + [f"norm{i}" for i in range(3)]
     + [
         f"{name}{way}"
         for name in ("ag0", "ag2", "rs3", "rs1", "rs0", "rows0", "rows1", "rows2", "rows3")
@@ -31,7 +32,8 @@
     + ["rows4"]
     + [f"own{i}" for i in range(5)]
     + [f"out{i}" for i in range(4)]
-    + ["own_image"]
+    + [f"in{i}" for i in range(11)]
+    + ["own_image", "out_gi", "out_ghc", "out_gnorm", "out_gsmall"]
 )
 GROUP = {name: number for number, name in enumerate(GROUPS)}
 
@@ -39,11 +41,13 @@
 def kernel(d, *refs):
     it = iter(refs)
     take = lambda count: [next(it) for _ in range(count)]
-    images, w0, w1, w2, w3, hw, ho, gain, shift, hb, ob, tw, pidx, lab, msk, tgt = take(16)
-    gi, gw0, gw1, gw2, gw3, ghc, gnorm, gsmall = take(8)
+    images, w0, w1, w2, w3, *small_in = take(16)
+    gi_out, gw0, gw1, gw2, gw3, *small_out = take(8)
+    small = hw, ho, gain, shift, hb, ob, tw, pidx, lab, msk, tgt = take(11)
+    gi, ghc, gnorm, gsmall = take(4)
     gather, columns_s = take(2)
     (s, s4, wf, y, zb, zhat, d9, u_sel, ut_sel, a2a_s, a2a_r, rs_s, rs_l, pool_own, pool_all, ps_s, ps_r, gi_s, gi_l) = take(19)
-    (zg, slope, slope_z, nrm_s, nrm_r, sums_s, sums_r) = take(7)
+    (zg, slope, slope_z, nrm_s, nrm_r, sums_s, sums_r, z4, slope4, slope_z4, sp_own, sp_all) = take(12)
     (gf, cr, zr, hw_s, hp, hg, hcr, hzr, hr, st_s, st_r, start_s, start_r, ho_s, ho_r, rep_s, rep_r, all_s, all_r, norm_s, feat) = take(21)
     ssem, rsem, wsz, wrz, wsf, wrf = take(6)
     w_in, gw = (w0, w1, w2, w3, hw_s), (gw0, gw1, gw2, gw3)
@@ -79,7 +83,8 @@
         "own_image": first_of(s.at[0], PD),
         "start": first_of(start_r, R - 1),
         "head_out": first_of(ho_r, F - 1),
-        "a2a": lambda: s4.at[:, pl.ds(0, (R - 1) * CR)],
+        "a2a": lambda: z4.at[:, pl.ds(0, (R - 1) * CR)],
+        "pool_slope": lambda: sp_all.at[:, :, pl.ds(0, (R - 1) * CR)],
         "pool": lambda: pool_all.at[:, pl.ds(0, (R - 1) * CR)],
         "dh3": first_of(a2a_r, R - 1),
         "rs2": first_of(ps_r, R - 1),
@@ -98,8 +103,9 @@
             size = half if h == 0 else rows - half
             for l in range(4):
                 volume[f"rows{l}{way}{h}"] = lambda l=l, size=size: gather.at[l, pl.ds(0, size), pl.ds(0, CR)]
-    for j in range(2):
+    for j in range(4):
         volume[f"sums{j}"] = first_of(sums_r.at[j], R - 1)
+    for j in range(3):
         volume[f"norm{j}"] = first_of(nrm_r.at[j], R - 1)
     for e in range(8):
         volume[f"stat{e}"] = first_of(st_r.at[e], F - 1)
@@ -155,6 +161,9 @@
             for wait in list(waits.values()):
                 wait()
 
+    for i, (src, dst) in enumerate(zip(small_in, small)):
+        copy_here(src, dst, f"in{i}")
+
     barrier = pltpu.get_barrier_semaphore()
     over(R, lambda k: pl.semaphore_signal(barrier, inc=1, device_id=rep_peer(k), device_id_type=MESH), 1)
     over(F, lambda k: pl.semaphore_signal(barrier, inc=1, device_id=(r, (f + k) % F), device_id_type=MESH), 1)
@@ -283,6 +292,8 @@
     own_rows = s.at[0, pl.ds(pl.multiple_of(r * PD, PD), PD)]
     copy_here(images, own_rows, "own_image")
 
+    for i in range(len(small)):
+        wait_recv(f"in{i}")
     start_s[...] = jnp.zeros_like(start_s)
     masks = jnp.concatenate([msk[:, i, :] for i in range(d.n)], axis=1).astype(F32)
     labels = jnp.concatenate([lab[i : i + 1, :] for i in range(d.n)], axis=1).astype(F32)
@@ -659,6 +670,34 @@
 
         per_image(images_here, body, 0)
 
+    def rows_of(l):
+        return gain[l : l + 1, my_lanes], shift[l : l + 1, my_lanes]
+
+    def slope_here(l, at):
+        g_row, b_row = rows_of(l)
+        normed = zhat[l, at, :]
+        shaped = normed * g_row + b_row
+        squashed = sigmoid(shaped)
+        return normed, squashed + shaped * squashed * (1.0 - squashed)
+
+    def pool_slopes():
+        def body(i, carry):
+            at = image_rows(i)
+            normed, steep = slope_here(1, at)
+            y[at, 0:CR] = steep
+            y[at, CR : 2 * CR] = steep * normed
+            return carry
+
+        per_image(images_here, body, 0)
+        inside, unused = windows(False)
+        averaged = jnp.dot(
+            jnp.where(inside, 0.25, 0.0), y[:, 0 : 2 * CR], precision=EXACT, preferred_element_type=F32
+        ).astype(BF16)
+        for k in range(2):
+            sp_own[k] = averaged[:, k * CR : (k + 1) * CR]
+            sp_all[k, :, my_lanes] = averaged[:, k * CR : (k + 1) * CR]
+        rep_all(sp_own, sp_all.at[:, :, my_lanes], "pool_slope")
+
     for l in range(4):
         w_finish(l)
         if l == 2:
@@ -666,18 +705,24 @@
             s[2] = jnp.dot(u_sel[...], pool_all[...], preferred_element_type=F32).astype(BF16)
         first = conv(s.at[l], images_here, l, zb)
         mean_here = first * (1.0 / M)
-        j = l // 2
         gathers = l in (0, 2)
+        ahead = l != 1
+        j = 2 if l == 3 else l // 2
 
         def squares(i, so_far):
             apart = zb[image_rows(i), :] - mean_here
             if gathers:
                 zg[j, image_rows(i), my_lanes] = apart.astype(BF16)
+            elif l == 3:
+                a2a_s[i] = apart.astype(BF16)
             return so_far + jnp.sum(jnp.square(apart), axis=0, keepdims=True)
 
         squared = per_image(images_here, squares, jnp.zeros((1, CR), F32))
         if gathers:
             gather_start(f"ag{l}", ag_piece(j))
+        elif l == 3:
+            over(R, lambda k: send(a2a_s.at[(r + k) % R], z4.at[:, my_lanes], rep_peer(k), "a2a"), 1)
+            z4[:, my_lanes] = a2a_s[r]
         st_s[l, 0:1, :] = first
         st_s[l, 1:2, :] = squared
         if l == 0:
@@ -709,7 +754,7 @@
         if l == 0:
             counts = tot[2:3]
         g_row, b_row = gain[l : l + 1, my_lanes], shift[l : l + 1, my_lanes]
-        if gathers:
+        if ahead:
             off = (mean_here - mean) * inverse
             nrm_s[j, 0:1, :] = inverse * g_row
             nrm_s[j, 1:2, :] = off * g_row + b_row
@@ -724,10 +769,7 @@
             zhat[l, at, :] = normed
             shaped = normed * g_row + b_row
             hidden = shaped * sigmoid(shaped)
-            if l == 1:
-                zb[at, :] = hidden
-            else:
-                a2a_s[i] = hidden.astype(BF16)
+            zb[at, :] = hidden
             return carry
 
         def keep_normed(i, carry):
@@ -741,7 +783,7 @@
                 s[l + 1, image_rows(i), b * CR : (b + 1) * CR] = (shaped * sigmoid(shaped)).astype(BF16)
             return carry
 
-        per_image(images_here, keep_normed if gathers else activate, 0)
+        per_image(images_here, keep_normed if ahead else activate, 0)
         if l == 1:
             inside, unused = windows(False)
             pooled = jnp.dot(
@@ -751,13 +793,11 @@
             pool_all[:, my_lanes] = pooled.astype(BF16)
             rep_all(pool_own, pool_all.at[:, my_lanes], "pool")
             w_relay_rest(2, pieces[1:])
+            pool_slopes()
             slopes_of(0)
-        elif l == 3:
-            over(R, lambda k: send(a2a_s.at[(r + k) % R], s4.at[:, my_lanes], rep_peer(k), "a2a"), 1)
-            s4[:, my_lanes] = a2a_s[r]
         elif l == 0:
             pool_matrices()
-        else:
+        elif l == 2:
             w_relay_rest(3, pieces[1:])
             pack_head()
         w_relay_near(l + 1)
@@ -783,7 +823,24 @@
         return carry
 
     lax.fori_loop(0, F, unpack, 0)
+    wait_recv("norm2")
     wait_recv("a2a")
+
+    def activate_own(i, carry):
+        at = image_rows(i)
+        for b in range(R):
+            lanes = slice(b * CR, (b + 1) * CR)
+            value = z4[at, lanes].astype(F32)
+            a, o, inverse, off = [nrm_r[2, b, k : k + 1, :] for k in range(4)]
+            shaped = value * a + o
+            squashed = sigmoid(shaped)
+            s4[at, lanes] = (shaped * squashed).astype(BF16)
+            steep = squashed + shaped * squashed * (1.0 - squashed)
+            slope4[at, lanes] = steep.astype(BF16)
+            slope_z4[at, lanes] = (steep * (value * inverse + off)).astype(BF16)
+        return carry
+
+    per_image(PD // PIX, activate_own, 0)
     wait_recv("head_out")
     conv(s4, PD // PIX, 4, zb)
     head_bias = jnp.concatenate([hb[...], jnp.zeros((1, CR - d.HC), F32)], axis=1)
@@ -828,12 +885,30 @@
 
     per_image(PD // PIX, spread_head, 0)
 
-    def write_dh3(half, part):
-        a2a_s[2 * half] = part[:, 0:CR].astype(BF16)
-        a2a_s[2 * half + 1] = part[:, CR : 2 * CR].astype(BF16)
+    def put_sums(j, n, grad, steep, steep_z):
+        sums_s[j, n, 0:1, :] = jnp.sum(grad * steep.astype(F32), axis=0, keepdims=True)
+        sums_s[j, n, 1:2, :] = jnp.sum(grad * steep_z.astype(F32), axis=0, keepdims=True)
+
+    def send_sums(j):
+        over(R, lambda k: send(sums_s.at[j, (r + k) % R], sums_r.at[j, r], rep_peer(k), f"sums{j}"), 1)
+        sums_r[j, r] = sums_s[j, r]
+
+    def pass_sums(j, e):
+        wait_recv(f"sums{j}")
+        st_s[e, 0:2, :] = sum(sums_r[j, i, 0:2, :] for i in range(R))
+        exchange(e)
+
+    def write_dh3(part_at, part):
+        for b in range(2):
+            n = 2 * part_at + b
+            grad = part[:, b * CR : (b + 1) * CR]
+            cols = slice(n * CR, (n + 1) * CR)
+            a2a_s[n] = grad.astype(BF16)
+            put_sums(2, n, grad, slope4[:, cols], slope_z4[:, cols])
 
     wait_send("a2a")
     data_grad(4, PD, write_dh3)
+    send_sums(2)
     over(R, lambda k: send(a2a_s.at[(r + k) % R], a2a_r.at[r], rep_peer(k), "dh3"), 1)
     a2a_r[r] = a2a_s[r]
     weight_grad(4, s4, PD)
@@ -858,33 +933,6 @@
         over(F, lambda k: send(all_s.at[(f + k) % F], all_r.at[f], (r, (f + k) % F), "small_all"), 1)
         all_r[f] = all_s[f]
 
-    def rows_of(l):
-        return gain[l : l + 1, my_lanes], shift[l : l + 1, my_lanes]
-
-    def slope_here(l, at):
-        g_row, b_row = rows_of(l)
-        normed = zhat[l, at, :]
-        shaped = normed * g_row + b_row
-        squashed = sigmoid(shaped)
-        return normed, squashed + shaped * squashed * (1.0 - squashed)
-
-    def enter(l, entering):
-        def body(i, so_far):
-            at = image_rows(i)
-            normed, steep = slope_here(l, at)
-            grad = entering(i, at) * steep
-            zb[at, :] = grad
-            return (
-                so_far[0] + jnp.sum(grad, axis=0, keepdims=True),
-                so_far[1] + jnp.sum(grad * normed, axis=0, keepdims=True),
-            )
-
-        none = jnp.zeros((1, CR), F32)
-        part_bias, part_gain = per_image(images_here, body, (none, none))
-        st_s[7 - l, 0:1, :] = part_bias
-        st_s[7 - l, 1:2, :] = part_gain
-        exchange(7 - l)
-
     def through_norm(l, grad_of):
         tot = jnp.sum(exchanged(7 - l), axis=0)
         bias_sum, gain_sum = tot[0:1], tot[1:2]
@@ -893,6 +941,8 @@
         scale = inverse_of[l] * rows_of(l)[0]
         if l in (0, 2):
             await_rest(f"rs{l + 1}")
+        elif l == 3:
+            wait_recv("dh3")
 
         def body(i, carry):
             at = image_rows(i)
@@ -901,9 +951,6 @@
             return carry
 
         per_image(images_here, body, 0)
-
-    def from_zb(l):
-        return lambda i, at: (zhat[l, at, :], zb[at, :])
 
     def from_scatter(l):
         j = l // 2
@@ -931,71 +978,79 @@
                 grad = part[:, b * CR : (b + 1) * CR]
                 rs_s[j, n] = grad.astype(BF16)
                 cols = slice(n * CR, (n + 1) * CR)
-                sums_s[j, n, 0:1, :] = jnp.sum(grad * slope[j, :, cols].astype(F32), axis=0, keepdims=True)
-                sums_s[j, n, 1:2, :] = jnp.sum(grad * slope_z[j, :, cols].astype(F32), axis=0, keepdims=True)
+                put_sums(j, n, grad, slope[j, :, cols], slope_z[j, :, cols])
 
         data_grad(l, M, write)
-        over(R, lambda k: send(sums_s.at[j, (r + k) % R], sums_r.at[j, r], rep_peer(k), f"sums{j}"), 1)
+        send_sums(j)
         scatter_start(f"rs{l}", rs_piece(j), rs_land(j))
-        sums_r[j, r] = sums_s[j, r]
         z_middle_piece(l + 1, 0)
         weight_grad(l, s.at[l], M)
-        wait_recv(f"sums{j}")
-        e = 7 - (l - 1)
-        st_s[e, 0:2, :] = sum(sums_r[j, i, 0:2, :] for i in range(R))
-        exchange(e)
+        pass_sums(j, 7 - (l - 1))
         scatter_forward(f"rs{l}", rs_piece(j), rs_land(j))
         for h in pieces[1:]:
             z_middle_piece(l + 1, h)
 
-    wait_recv("dh3")
-    enter(3, lambda i, at: a2a_r[i].astype(F32))
+    def from_head(i, at):
+        normed, steep = slope_here(3, at)
+        return normed, a2a_r[i].astype(F32) * steep
+
+    pass_sums(2, 4)
     core_sum(4)
     z_push(4)
     head_small()
-    through_norm(3, from_zb(3))
+    through_norm(3, from_head)
     layer_down(3)
     core_sum(3)
     z_push(3)
+    z_sum(4)
 
     through_norm(2, from_scatter(2))
 
     def write_pooled(part_at, part):
-        chosen = jnp.dot(ut_sel[...], part.astype(BF16), preferred_element_type=F32).astype(BF16)
-        ps_s[2 * part_at] = chosen[:, 0:CR]
-        ps_s[2 * part_at + 1] = chosen[:, CR : 2 * CR]
+        chosen = jnp.dot(ut_sel[...], part.astype(BF16), preferred_element_type=F32)
+        for b in range(2):
+            n = 2 * part_at + b
+            grad = chosen[:, b * CR : (b + 1) * CR]
+            cols = slice(n * CR, (n + 1) * CR)
+            ps_s[n] = grad.astype(BF16)
+            put_sums(3, n, grad, sp_all[0, :, cols], sp_all[1, :, cols])
 
     z_middle(3)
+    wait_recv("pool_slope")
     data_grad(2, M, write_pooled)
+    send_sums(3)
     over(R, lambda k: send(ps_s.at[(r + k) % R], ps_r.at[r], rep_peer(k), "rs2"), 1)
     ps_r[r] = ps_s[r]
     weight_grad(2, s.at[2], M)
+    pass_sums(3, 6)
+    core_sum(2)
+    z_push(2)
     wait_recv("rs2")
     pooled = sum(ps_r[i].astype(F32) for i in range(R))
     inside, unused = windows(True)
     zb[...] = jnp.dot(jnp.where(inside, 0.25, 0.0), pooled, precision=EXACT, preferred_element_type=F32)
-    enter(1, lambda i, at: zb[at, :])
-    core_sum(2)
-    z_push(2)
-    z_sum(4)
+
+    def from_pool(i, at):
+        normed, steep = slope_here(1, at)
+        return normed, zb[at, :] * steep
+
+    through_norm(1, from_pool)
+    layer_down(1)
     z_sum(3)
-    through_norm(1, from_zb(1))
-    gather_forward("rows3", rows_piece(3))
-    layer_down(1)
     core_sum(1)
     z_push(1)
+    gather_forward("rows3", rows_piece(3))
     z_sum(2)
 
     through_norm(0, from_scatter(0))
-    weight_grad(0, s.at[0], M)
-    gather_forward("rows2", rows_piece(2))
-
     def write_images(part_at, part):
         for i in range(R):
             gi_s[i, :, part_at * 2 * CR : (part_at + 1) * 2 * CR] = part[i * PD : (i + 1) * PD].astype(BF16)
 
     data_grad(0, M, write_images)
     scatter_start("rs0", gi_piece, gi_land)
+    weight_grad(0, s.at[0], M)
+    gather_forward("rows2", rows_piece(2))
     z_middle(1)
     core_sum(0)
     z_push(0)
@@ -1008,6 +1063,8 @@
     wait_recv("small_all")
     gsmall[...] = jnp.sum(all_r[...], axis=0) * (1.0 / root)
     rows_done(4)
+    copy_here(ghc, small_out[0], "out_ghc")
+    copy_here(gsmall, small_out[2], "out_gsmall")
     rows_done(3)
     gather_forward("rows1", rows_piece(1))
     rows_done(2)
@@ -1015,6 +1072,9 @@
     for h in range(2):
         at = slice(h * (PD // 2), (h + 1) * (PD // 2))
         gi[at, :] = gi_s[r, at, :].astype(F32) + gi_l[1 + 2 * h].astype(F32) + gi_l[4 + h].astype(F32)
+    copy_here(gi, gi_out, "out_gi")
+    wait_recv("norms")
+    copy_here(gnorm, small_out[1], "out_gnorm")
     last = rows_piece(0)
     if d.pieces == 2:
         z_sum_piece(0, 0)
@@ -1032,7 +1092,6 @@
         z_sum(0)
         rows_done(1)
         gather_forward("rows0", last)
-    wait_recv("norms")
     rows_done(0)
 
     drain()
@@ -1074,7 +1133,16 @@
     d.half = -(-rows // (2 * d.row_tile)) * d.row_tile
     vm = pltpu.VMEM
     patch = 9 * channels
-    scratch = [
+    smalls = (
+        head_conv.T, head_out, norm_gain, norm_bias, head_bias.reshape(1, hidden), out_bias.reshape(1, out_ch),
+        task_weights.reshape(1, 3), pool_index, labels, jnp.transpose(task_masks, (1, 0, 2)), targets,
+    )
+    smalls = (smalls[0].astype(wire),) + smalls[1:]
+    scratch = [vm(value.shape, value.dtype) for value in smalls] + [
+        vm((d.PD, d.C), F32),
+        vm((hidden, rows), F32),
+        vm((8, d.C), F32),
+        vm((16, LANES), F32),
         vm((4, rows, d.C), wire),
         vm((d.PD, LANES), F32),
         vm((4, d.M, d.C), BF16),
@@ -1099,10 +1167,15 @@
         vm((2, d.M, d.C), BF16),
         vm((2, d.M, d.C), BF16),
         vm((2, d.M, d.C), BF16),
-        vm((2, 8, LANES), F32),
-        vm((2, R, 8, LANES), F32),
-        vm((2, R, 8, LANES), F32),
-        vm((2, R, 8, LANES), F32),
+        vm((3, 8, LANES), F32),
+        vm((3, R, 8, LANES), F32),
+        vm((4, R, 8, LANES), F32),
+        vm((4, R, 8, LANES), F32),
+        vm((d.PD, d.C), BF16),
+        vm((d.PD, d.C), BF16),
+        vm((d.PD, d.C), BF16),
+        vm((2, d.PW, d.CR), BF16),
+        vm((2, d.PW, d.C), BF16),
         vm((4, patch, d.CR), wire),
         vm((4, d.Z, rows, d.CR), wire),
         vm((4, d.Z, rows, d.CR), wire),
@@ -1131,22 +1204,21 @@
         pltpu.SemaphoreType.DMA((5 * d.pieces, d.Z)),
         pltpu.SemaphoreType.DMA((5 * d.pieces, d.Z)),
     ]
-    here, there = pl.BlockSpec(memory_space=pltpu.VMEM), pl.BlockSpec(memory_space=pl.ANY)
+    there = pl.BlockSpec(memory_space=pl.ANY)
     shape = jax.ShapeDtypeStruct
     kept = pl.pallas_call(
         functools.partial(kernel, d),
         out_shape=[shape((d.PD, d.C), F32)]
         + [shape((rows, d.C), wire)] * 4
         + [shape((hidden, rows), F32), shape((8, d.C), F32), shape((16, LANES), F32)],
-        in_specs=[there] * 5 + [here] * 11,
-        out_specs=[here] + [there] * 4 + [here] * 3,
+        in_specs=[there] * 16,
+        out_specs=[there] * 8,
         scratch_shapes=scratch,
-        compiler_params=pltpu.CompilerParams(collective_id=0, has_side_effects=True, vmem_limit_bytes=60 * 2**20),
+        compiler_params=pltpu.CompilerParams(collective_id=0, has_side_effects=True, vmem_limit_bytes=63 * 2**20),
     )(
         images.reshape(d.PD, channels),
         *(w.astype(wire) for w in (enc_first, enc_second, dec_first, dec_second)),
-        head_conv.T, head_out, norm_gain, norm_bias, head_bias.reshape(1, hidden), out_bias.reshape(1, out_ch),
-        task_weights.reshape(1, 3), pool_index, labels, jnp.transpose(task_masks, (1, 0, 2)), targets,
+        *smalls,
     )
     steps = next(count for count in (2, 1) if rows % (count * d.row_tile) == 0 and d.PD % (count * 8) == 0)
     part = lambda height, width: pl.BlockSpec((height // steps, width), lambda i: (i, 0))

time: 152 us -> 145 us (0.954)
  Pallas kernels: 151 us -> 144 us
    pallas_call x1, Pallas kernels: 147 us -> 140 us  [per_device(): pl.pallas_call(functools.partial(kernel, d), out_shape=[shape((d.PD, d.C)...]
where the time goes in v5:
time: 145 us
  Pallas kernels  144 us (99%)
    pallas_call x1, Pallas kernels, per_device(): pl.pallas_call(functools.partial(kernel, d), out_shape=[shape((d.PD, d.C)...  140 us
    pallas_call x1, Pallas kernels, per_device(): pl.pallas_call(finish, grid=(steps,), out_shape=[shape((d.PD, channels),...  4.15 us

profile of v5, /device:TPU:0, one launch (start us, length us, event | category | flops | bytes accessed | tf_op | source)
XLA Modules:
  0.0 144.8 jit_solution(565211114464370599)
XLA Ops:
  0.7 139.8 %shard_map.239 = (f32[192,512]{1,0:T(8,128)}, bf16[576,512]{1,0:T(8,128)(2,1)}, bf16[576,512]{1,0:T(8,128)(2,1)}, bf16[576,512]{1,0:T(8,128)(2,1)}, bf16[576,512...) custom-call(bf16[192,512]{1,0:T(8,128)(2,1)} %bitcast.10, bf16[576,512]{1,0:T(8,128)(2,1)} %refs_1_.1, ...), custom_call_target="tpu_custom_call" | custom-call | tf_op jit(solution)/shard_map/pallas_call | solution.py:1209
  140.5 4.1 %shard_map.240 = (f32[192,512]{1,0:T(8,128)}, f32[576,512]{1,0:T(8,128)}, f32[576,512]{1,0:T(8,128)}, f32[576,512]{1,0:T(8,128)}, f32[576,512]{1,0:T(8,128)}, /*...) custom-call(f32[192,512]{1,0:T(8,128)} %get-tuple-element.30.gi, ...), custom_call_target="tpu_custom_call" | custom-call | tf_op jit(solution)/shard_map/pallas_call | solution.py:1227

commit v6 on v5

--- a/solution.py
+++ b/solution.py
@@ -23,10 +23,11 @@
     + [
         f"{name}{way}"
         for name in ("ag0", "ag2", "rs3", "rs1", "rs0", "rows0", "rows1", "rows2", "rows3")
-        for way in ("x0", "x1", "y0", "y1", "f0", "f1")
+        for way in ("x0", "y1", "r")
     ]
     + [f"stat{i}" for i in range(8)]
     + [f"core{i}" for i in range(5)]
+    + [f"weights{i}" for i in range(5)]
     + [f"z{i}.{h}" for i in range(5) for h in range(2)]
     + [f"mid{i}.{h}" for i in range(5) for h in range(2)]
     + ["rows4"]
@@ -36,6 +37,24 @@
     + ["own_image", "out_gi", "out_ghc", "out_gnorm", "out_gsmall"]
 )
 GROUP = {name: number for number, name in enumerate(GROUPS)}
+
+CLASSES = [
+    "images", "start", "head_out", "a2a", "pool", "dh3", "rs2", "norms", "small_rep", "small_all", "pool_slope",
+    "rows4", "weights", "weights4", "core", "core4", "z", "z4", "ag", "rs", "rs0", "rows", "sums", "norm", "stat",
+]
+CLASS = {name: number for number, name in enumerate(CLASSES)}
+
+
+def class_of(group):
+    if group in CLASS:
+        return CLASS[group]
+    if group.startswith("rs0"):
+        return CLASS["rs0"]
+    name = group.rstrip("xyr0123456789.")
+    if name in ("mid", "z"):
+        name = "z"
+        return CLASS["z4" if group[len(group.split(".")[0]) - 1] == "4" else "z"]
+    return CLASS[name]
 
 
 def kernel(d, *refs):
@@ -49,7 +68,7 @@
     (s, s4, wf, y, zb, zhat, d9, u_sel, ut_sel, a2a_s, a2a_r, rs_s, rs_l, pool_own, pool_all, ps_s, ps_r, gi_s, gi_l) = take(19)
     (zg, slope, slope_z, nrm_s, nrm_r, sums_s, sums_r, z4, slope4, slope_z4, sp_own, sp_all) = take(12)
     (gf, cr, zr, hw_s, hp, hg, hcr, hzr, hr, st_s, st_r, start_s, start_r, ho_s, ho_r, rep_s, rep_r, all_s, all_r, norm_s, feat) = take(21)
-    ssem, rsem, wsz, wrz, wsf, wrf = take(6)
+    ssem, rsem, wrz = take(3)
     w_in, gw = (w0, w1, w2, w3, hw_s), (gw0, gw1, gw2, gw3)
     R, F, Z, rows, half, C, CR, W, PIX, PD, M, PW = d.R, d.F, d.Z, d.rows, d.half, d.C, d.CR, d.W, d.PIX, d.PD, d.M, d.PW
     total = float(M * F)
@@ -94,15 +113,18 @@
         "rows4": first_of(hr, R - 1),
         "core4": lambda: hcr,
     }
-    for way in ("x", "y", "f"):
-        for h in range(2):
-            for j in range(2):
-                volume[f"ag{2 * j}{way}{h}"] = lambda j=j: zg.at[j, pl.ds(0, M // 2), pl.ds(0, CR)]
-                volume[f"rs{2 * j + 1}{way}{h}"] = lambda j=j: rs_l.at[j, 0]
-            volume[f"rs0{way}{h}"] = lambda: gi_l.at[0]
-            size = half if h == 0 else rows - half
-            for l in range(4):
-                volume[f"rows{l}{way}{h}"] = lambda l=l, size=size: gather.at[l, pl.ds(0, size), pl.ds(0, CR)]
+    for j in range(2):
+        for way in ("x0", "y1"):
+            volume[f"ag{2 * j}{way}"] = lambda j=j: zg.at[j, pl.ds(0, M // 2), pl.ds(0, CR)]
+            volume[f"rs{2 * j + 1}{way}"] = lambda j=j: rs_l.at[j, 0]
+        volume[f"ag{2 * j}r"] = lambda j=j: zg.at[j, :, pl.ds(0, 2 * CR)]
+        volume[f"rs{2 * j + 1}r"] = lambda j=j: rs_l.at[j, pl.ds(0, 4)]
+    volume["rs0x0"] = volume["rs0y1"] = lambda: gi_l.at[0]
+    volume["rs0r"] = lambda: gi_l.at[pl.ds(0, 4)]
+    for l in range(4):
+        volume[f"rows{l}x0"] = lambda l=l: gather.at[l, pl.ds(0, half), pl.ds(0, CR)]
+        volume[f"rows{l}y1"] = lambda l=l: gather.at[l, pl.ds(half, rows - half), pl.ds(0, CR)]
+        volume[f"rows{l}r"] = lambda l=l: gather.at[l, :, pl.ds(0, (3 if l == 0 and line else 2) * CR)]
     for j in range(4):
         volume[f"sums{j}"] = first_of(sums_r.at[j], R - 1)
     for j in range(3):
@@ -119,7 +141,39 @@
         arriving.pop(group)()
 
     def wait_send(group):
-        leaving.pop(group)()
+        leaving.pop(CLASS[group])()
+
+    def when_line(at_end, inside, otherwise):
+        if line:
+            when(is_end, at_end)
+            when(jnp.logical_not(is_end), inside)
+        else:
+            otherwise()
+
+    def departed(number):
+        name = CLASSES[number]
+        whole = {
+            "core": lambda: cr,
+            "core4": lambda: hcr,
+            "z": lambda: zr.at[:, pl.ds(0, Z - 1)],
+            "z4": lambda: hzr.at[pl.ds(0, Z - 1)],
+            "ag": lambda: zg.at[:, :, pl.ds(0, 3 * CR)],
+            "rs": lambda: rs_l,
+            "rs0": lambda: gi_l,
+            "rows": lambda: gather.at[:, :, pl.ds(0, 3 * CR)],
+            "sums": lambda: sums_r.at[:, pl.ds(0, R - 1)],
+            "norm": lambda: nrm_r.at[:, pl.ds(0, R - 1)],
+            "stat": lambda: st_r.at[:, pl.ds(0, F - 1)],
+        }
+        sem = ssem.at[number]
+        if name == "weights":
+            many = lambda count: lambda: wait_for(wf.at[pl.ds(0, 4), pl.ds(0, count * rows)], sem)
+            when_line(many(6), many(8), many(2 * Z - 1))
+        elif name == "weights4":
+            many = lambda count: lambda: wait_for(hp.at[pl.ds(0, count)], sem)
+            when_line(many(6), many(8), many(2 * Z - 1))
+        else:
+            wait_for((whole[name] if name in whole else volume[name])(), sem)
 
     def copy_here(src, dst, group):
         g = GROUP[group]
@@ -127,12 +181,12 @@
         pltpu.make_async_copy(src, dst, rsem.at[g]).start()
 
     def send(src, dst, to, group):
-        g = GROUP[group]
+        g, out = GROUP[group], class_of(group)
         if group in volume:
             arriving[group] = lambda: wait_for(volume[group](), rsem.at[g])
-            leaving[group] = lambda: wait_for(volume[group](), ssem.at[g])
+        leaving[out] = lambda: departed(out)
         pltpu.make_async_remote_copy(
-            src_ref=src, dst_ref=dst, send_sem=ssem.at[g], recv_sem=rsem.at[g], device_id=to, device_id_type=MESH
+            src_ref=src, dst_ref=dst, send_sem=ssem.at[out], recv_sem=rsem.at[g], device_id=to, device_id_type=MESH
         ).start()
 
     def over(count, body, first=0):
@@ -189,10 +243,16 @@
             return wf.at[l, pl.ds(pl.multiple_of(owner * rows + first, d.row_tile), size)]
         return hp.at[owner, pl.ds(first, size)]
 
-    def w_copy(l, h, src, owner, to, send_sem, recv_sem):
+    def w_copy(l, h, src, owner, to, recv_sem):
+        out = CLASS["weights" if l < 4 else "weights4"]
+        leaving[out] = lambda: departed(out)
         return pltpu.make_async_remote_copy(
-            src_ref=src, dst_ref=w_block(l, owner, h), send_sem=send_sem, recv_sem=recv_sem, device_id=to, device_id_type=MESH
+            src_ref=src, dst_ref=w_block(l, owner, h), send_sem=ssem.at[out], recv_sem=recv_sem, device_id=to,
+            device_id_type=MESH,
         )
+
+    def w_to_core(l, h, src, owner):
+        w_copy(l, h, src, owner, sib, rsem.at[GROUP[f"weights{l}"]]).start()
 
     def w_src(l, h):
         return w_in[l].at[cut_at(l, h), my_lanes] if l < 4 else hw_s.at[cut_at(l, h)]
@@ -203,22 +263,14 @@
     def w_send(l, h, k, who=lambda body: body()):
         u = l * d.pieces + h
         arriving["z", l, h, k] = lambda: direct(Z - k, lambda: w_wait(l, h, wrz.at[u, k]))
-        leaving["z", l, h, k] = lambda: direct(k, lambda: w_wait(l, h, wsz.at[u, k]))
-        start = lambda: w_copy(l, h, w_src(l, h), f, z_peer(k), wsz.at[u, k], wrz.at[u, k]).start()
+        start = lambda: w_copy(l, h, w_src(l, h), f, z_peer(k), wrz.at[u, k]).start()
         who(lambda: direct(k, start))
-
-    def w_relayed(l, h, k):
-        u = l * d.pieces + h
-        arriving["core", l, h, k] = lambda: w_wait(l, h, wrf.at[u, k])
-        leaving["core", l, h, k] = lambda: w_wait(l, h, wsf.at[u, k])
 
     def w_push_near(l):
         for h in pieces:
-            u = l * d.pieces + h
             for k in near:
                 w_send(l, h, k)
-            w_copy(l, h, w_src(l, h), f, sib, wsf.at[u, 0], wrf.at[u, 0]).start()
-            w_relayed(l, h, 0)
+            w_to_core(l, h, w_src(l, h), f)
         copy_here(w_in[l].at[:, my_lanes] if l < 4 else hw_s, wf.at[l, block(f)] if l < 4 else hp.at[f], f"own{l}")
 
     def w_push_rest(l, hs=pieces, who=lambda body: body()):
@@ -240,7 +292,7 @@
         u = l * d.pieces + h
         owner = ((zc + Z - k) % Z) * 2 + core
         w_wait(l, h, wrz.at[u, k])
-        w_copy(l, h, w_block(l, owner, h), owner, sib, wsf.at[u, k], wrf.at[u, k]).start()
+        w_to_core(l, h, w_block(l, owner, h), owner)
 
     def w_relay_rest(l, hs=pieces):
         for h in hs:
@@ -248,42 +300,31 @@
             for k in beyond:
                 arriving.pop(("z", l, h, k))
                 w_arrived(l, h, k)
-                w_relayed(l, h, k)
             if line:
 
                 def hand_on():
                     to = (Z - 1) * (zc - 1)
                     owner = (Z - 1 - to) * 2 + core
                     slot = jnp.where(zc == 1, 1, Z - 1)
-                    w_copy(
-                        l, h, w_block(l, owner, h), owner, (r, to * 2 + core), wsz.at[u, 0], wrz.at[u, slot]
-                    ).start()
+                    w_copy(l, h, w_block(l, owner, h), owner, (r, to * 2 + core), wrz.at[u, slot]).start()
 
                 when(jnp.logical_not(is_end), hand_on)
-                leaving["far", l, h] = lambda u=u, h=h: when(
-                    jnp.logical_not(is_end), lambda: w_wait(l, h, wsz.at[u, 0])
-                )
 
     def w_relay_near(l):
         for h in pieces:
             for k in near:
                 arriving.pop(("z", l, h, k))
                 direct(Z - k, lambda: w_arrived(l, h, k))
-                if not line:
-                    w_relayed(l, h, k)
 
     def w_far(l):
         if line:
             for h in pieces:
-                for k in near:
-                    w_relayed(l, h, k)
                 when(zc == 0, lambda: w_arrived(l, h, 1))
                 when(zc == Z - 1, lambda: w_arrived(l, h, Z - 1))
 
     def w_finish(l):
-        for h in pieces:
-            for k in range(Z):
-                wait_recv(("core", l, h, k))
+        one = GROUP[f"weights{l}"]
+        wait_for(wf.at[l, pl.ds(0, Z * rows)] if l < 4 else hp.at[pl.ds(0, Z)], rsem.at[one])
         wait_recv(f"own{l}")
 
     w_push_rest(0)
@@ -435,33 +476,32 @@
     def gather_start(name, piece):
         send(piece(r, 0), piece(r, 0), at_one, f"{name}x0")
         send(piece(r, 1), piece(r, 1), at_two, f"{name}y1")
-        send(piece(r, 1), piece(r, 1), at_one, f"{name}x1")
-        send(piece(r, 0), piece(r, 0), at_two, f"{name}y0")
+        send(piece(r, 1), piece(r, 1), at_one, f"{name}r")
+        send(piece(r, 0), piece(r, 0), at_two, f"{name}r")
 
     def gather_forward(name, piece):
         wait_recv(f"{name}x0")
-        send(piece(one, 0), piece(one, 0), at_two, f"{name}f0")
+        send(piece(one, 0), piece(one, 0), at_two, f"{name}r")
         wait_recv(f"{name}y1")
-        send(piece(two, 1), piece(two, 1), at_one, f"{name}f1")
+        send(piece(two, 1), piece(two, 1), at_one, f"{name}r")
 
     def await_rest(name):
-        for way in ("x1", "y0", "f0", "f1"):
-            wait_recv(f"{name}{way}")
+        wait_recv(f"{name}r")
 
     def scatter_start(name, piece, land):
         send(piece(both, 0), land(0), at_one, f"{name}x0")
         send(piece(both, 1), land(2), at_two, f"{name}y1")
-        send(piece(one, 0), land(1), at_one, f"{name}x1")
-        send(piece(two, 1), land(3), at_two, f"{name}y0")
+        send(piece(one, 0), land(1), at_one, f"{name}r")
+        send(piece(two, 1), land(3), at_two, f"{name}r")
 
     def scatter_forward(name, piece, land):
-        for way, ref, came, dst, to, group in (
-            ("x0", piece(two, 0), land(0), land(4), at_two, "f0"),
-            ("y1", piece(one, 1), land(2), land(5), at_one, "f1"),
+        for way, ref, came, dst, to in (
+            ("x0", piece(two, 0), land(0), land(4), at_two),
+            ("y1", piece(one, 1), land(2), land(5), at_one),
         ):
             wait_recv(f"{name}{way}")
             ref[...] = (ref[...].astype(F32) + came[...].astype(F32)).astype(ref.dtype)
-            send(ref, dst, to, f"{name}{group}")
+            send(ref, dst, to, f"{name}r")
 
     def ag_piece(j):
         return lambda owner, h: zg.at[j, pl.ds(h * (M // 2), M // 2), lanes_of(owner)]
@@ -551,7 +591,6 @@
             arriving[f"mid{l}.{h}"] = lambda: when(
                 jnp.logical_not(is_end), lambda: wait_for(from_z(l, 0, h), rsem.at[g])
             )
-            leaving[f"mid{l}.{h}"] = lambda: when(is_end, lambda: wait_for(from_z(l, 0, h), ssem.at[g]))
 
     def z_push_piece(l, h):
         def push(k):
@@ -566,7 +605,6 @@
         if Z > 8:
             over(Z, push, 1)
         arriving[f"z{l}.{h}"] = lambda: z_wait(l, h, rsem.at[GROUP[f"z{l}.{h}"]])
-        leaving[f"z{l}.{h}"] = lambda: z_wait(l, h, ssem.at[GROUP[f"z{l}.{h}"]])
 
     def z_middle(l):
         for h in pieces:
@@ -1078,16 +1116,14 @@
     last = rows_piece(0)
     if d.pieces == 2:
         z_sum_piece(0, 0)
-        send(last(r, 0), last(r, 0), at_one, "rows0x0")
-        send(last(r, 0), last(r, 0), at_two, "rows0y0")
-        send(last(r, 0), last(r, 0), (both, f), "rows0f0")
+        send(last(r, 0), last(r, 0), at_one, "rows0r")
+        send(last(r, 0), last(r, 0), at_two, "rows0r")
+        send(last(r, 0), last(r, 0), (both, f), "rows0r")
         rows_done(1)
         z_sum_piece(0, 1)
-        send(last(r, 1), last(r, 1), at_one, "rows0x1")
-        send(last(r, 1), last(r, 1), at_two, "rows0y1")
-        send(last(r, 1), last(r, 1), (both, f), "rows0f1")
-        wait_recv("rows0x0")
-        wait_recv("rows0y1")
+        send(last(r, 1), last(r, 1), at_one, "rows0r")
+        send(last(r, 1), last(r, 1), at_two, "rows0r")
+        send(last(r, 1), last(r, 1), (both, f), "rows0r")
     else:
         z_sum(0)
         rows_done(1)
@@ -1197,11 +1233,8 @@
         vm((F, 16, LANES), F32),
         vm((8, LANES), F32),
         vm((LANES, 2 * LANES), F32),
+        pltpu.SemaphoreType.DMA((len(CLASSES),)),
         pltpu.SemaphoreType.DMA((len(GROUPS),)),
-        pltpu.SemaphoreType.DMA((len(GROUPS),)),
-        pltpu.SemaphoreType.DMA((5 * d.pieces, d.Z)),
-        pltpu.SemaphoreType.DMA((5 * d.pieces, d.Z)),
-        pltpu.SemaphoreType.DMA((5 * d.pieces, d.Z)),
         pltpu.SemaphoreType.DMA((5 * d.pieces, d.Z)),
     ]
     there = pl.BlockSpec(memory_space=pl.ANY)

time: 145 us -> 143 us (0.986)
  Pallas kernels: 144 us -> 142 us
    pallas_call x1, Pallas kernels: 140 us -> 138 us  [per_device(): pl.pallas_call(functools.partial(kernel, d), out_shape=[shape((d.PD, d.C)...]
where the time goes in v6:
time: 143 us
  Pallas kernels  142 us (99%)
    pallas_call x1, Pallas kernels, per_device(): pl.pallas_call(functools.partial(kernel, d), out_shape=[shape((d.PD, d.C)...  138 us
    pallas_call x1, Pallas kernels, per_device(): pl.pallas_call(finish, grid=(steps,), out_shape=[shape((d.PD, channels),...  4.15 us

profile of v6, /device:TPU:0, one launch (start us, length us, event | category | flops | bytes accessed | tf_op | source)
XLA Modules:
  0.0 142.6 jit_solution(80483281382104465)
XLA Ops:
  0.7 137.6 %shard_map.239 = (f32[192,512]{1,0:T(8,128)}, bf16[576,512]{1,0:T(8,128)(2,1)}, bf16[576,512]{1,0:T(8,128)(2,1)}, bf16[576,512]{1,0:T(8,128)(2,1)}, bf16[576,512...) custom-call(bf16[192,512]{1,0:T(8,128)(2,1)} %bitcast.10, bf16[576,512]{1,0:T(8,128)(2,1)} %refs_1_.1, ...), custom_call_target="tpu_custom_call" | custom-call | tf_op jit(solution)/shard_map/pallas_call | solution.py:1242
  138.3 4.1 %shard_map.240 = (f32[192,512]{1,0:T(8,128)}, f32[576,512]{1,0:T(8,128)}, f32[576,512]{1,0:T(8,128)}, f32[576,512]{1,0:T(8,128)}, f32[576,512]{1,0:T(8,128)}, /*...) custom-call(f32[192,512]{1,0:T(8,128)} %get-tuple-element.30.gi, ...), custom_call_target="tpu_custom_call" | custom-call | tf_op jit(solution)/shard_map/pallas_call | solution.py:1260

commit v7 on v6

--- a/solution.py
+++ b/solution.py
@@ -453,14 +453,14 @@
                 jnp.concatenate([low_blank, low[: PIX - W]], axis=0),
             )
             for ky in range(3):
-                d9[at, (kx * 3 + ky) * CR : (kx * 3 + ky + 1) * CR] = nine[ky]
+                d9[at, (ky * 3 + kx) * CR : (ky * 3 + kx + 1) * CR] = nine[ky]
 
     def data_grad(l, height, write):
         step = 2 * CR
         for half in range(C // step):
             taps = [
                 wf[l, t * C + half * step : t * C + (half + 1) * step, :].astype(BF16)
-                for t in (3 * ky + kx for kx in range(3) for ky in range(3))
+                for t in range(9)
             ]
             part = lax.dot_general(
                 d9[0:height, :],
@@ -540,16 +540,21 @@
         return hg.at[owner, pl.ds(first, size)]
 
     def weight_grad(l, src, height):
-        for kx in range(3):
+        to_core = lambda k: send(g_block(l, 2 * k + 1 - core), from_core(l).at[k], sib, f"core{l}")
+        sent = 0
+        for ky in range(3):
             part = lax.dot_general(
                 src[...],
-                d9[0:height, kx * 3 * CR : (kx + 1) * 3 * CR],
+                d9[0:height, ky * 3 * CR : (ky + 1) * 3 * CR],
                 (((0,), (0,)), ((), ())),
                 preferred_element_type=F32,
             )
-            for ky in range(3):
+            for kx in range(3):
                 t = 3 * ky + kx
-                gf[l % 4, t * C : (t + 1) * C, :] = part[:, ky * CR : (ky + 1) * CR].astype(gf.dtype)
+                gf[l % 4, t * C : (t + 1) * C, :] = part[:, kx * CR : (kx + 1) * CR].astype(gf.dtype)
+            while l < 4 and sent < Z and 2 * (sent + 1) * rows <= (ky + 1) * 3 * C:
+                to_core(sent)
+                sent += 1
         if l == 4:
 
             def pack(i, carry):
@@ -562,7 +567,7 @@
                 return carry
 
             lax.fori_loop(0, F, pack, 0)
-        over(Z, lambda k: send(g_block(l, 2 * k + 1 - core), from_core(l).at[k], sib, f"core{l}"))
+            over(Z, to_core)
 
     def core_sum(l):
         wait_recv(f"core{l}")
@@ -1053,10 +1058,10 @@
             ps_s[n] = grad.astype(BF16)
             put_sums(3, n, grad, sp_all[0, :, cols], sp_all[1, :, cols])
 
-    z_middle(3)
     wait_recv("pool_slope")
     data_grad(2, M, write_pooled)
     send_sums(3)
+    z_middle(3)
     over(R, lambda k: send(ps_s.at[(r + k) % R], ps_r.at[r], rep_peer(k), "rs2"), 1)
     ps_r[r] = ps_s[r]
     weight_grad(2, s.at[2], M)

time: 143 us -> 142 us (level)
  no operation moved by 1% of the time
where the time goes in v7:
time: 142 us; the launch traced here: 141 us
  Pallas kernels  141 us (99%)
    pallas_call x1, Pallas kernels, per_device(): pl.pallas_call(functools.partial(kernel, d), out_shape=[shape((d.PD, d.C)...  136 us
    pallas_call x1, Pallas kernels, per_device(): pl.pallas_call(finish, grid=(steps,), out_shape=[shape((d.PD, channels),...  4.15 us

profile of v7, /device:TPU:0, one launch (start us, length us, event | category | flops | bytes accessed | tf_op | source)
XLA Modules:
  0.0 141.4 jit_solution(9508867356963308287)
XLA Ops:
  0.7 136.4 %shard_map.239 = (f32[192,512]{1,0:T(8,128)}, bf16[576,512]{1,0:T(8,128)(2,1)}, bf16[576,512]{1,0:T(8,128)(2,1)}, bf16[576,512]{1,0:T(8,128)(2,1)}, bf16[576,512...) custom-call(bf16[192,512]{1,0:T(8,128)(2,1)} %bitcast.10, bf16[576,512]{1,0:T(8,128)(2,1)} %refs_1_.1, ...), custom_call_target="tpu_custom_call" | custom-call | tf_op jit(solution)/shard_map/pallas_call | solution.py:1247
  137.1 4.1 %shard_map.240 = (f32[192,512]{1,0:T(8,128)}, f32[576,512]{1,0:T(8,128)}, f32[576,512]{1,0:T(8,128)}, f32[576,512]{1,0:T(8,128)}, f32[576,512]{1,0:T(8,128)}, /*...) custom-call(f32[192,512]{1,0:T(8,128)} %get-tuple-element.30.gi, ...), custom_call_target="tpu_custom_call" | custom-call | tf_op jit(solution)/shard_map/pallas_call | solution.py:1265

commit v8 on v7

--- a/solution.py
+++ b/solution.py
@@ -16,31 +16,31 @@
 EXACT = lax.Precision.HIGHEST
 
 GROUPS = (
-    ["images", "start", "head_out", "a2a", "pool", "dh3", "rs2", "norms", "small_rep", "small_all"]
-    + [f"sums{i}" for i in range(4)]
-    + ["pool_slope"]
-    + [f"norm{i}" for i in range(3)]
+    ["im", "st", "ho", "a2a", "pl", "d3", "rs2", "ns", "sp", "sa"]
+    + [f"s{i}" for i in range(4)]
+    + ["ps"]
+    + [f"n{i}" for i in range(3)]
     + [
         f"{name}{way}"
-        for name in ("ag0", "ag2", "rs3", "rs1", "rs0", "rows0", "rows1", "rows2", "rows3")
+        for name in ("ag0", "ag2", "rs3", "rs1", "rs0", "w0", "w1", "w2", "w3")
         for way in ("x0", "y1", "r")
     ]
-    + [f"stat{i}" for i in range(8)]
-    + [f"core{i}" for i in range(5)]
-    + [f"weights{i}" for i in range(5)]
+    + [f"t{i}" for i in range(8)]
+    + [f"c{i}" for i in range(5)]
+    + [f"k{i}" for i in range(5)]
     + [f"z{i}.{h}" for i in range(5) for h in range(2)]
-    + [f"mid{i}.{h}" for i in range(5) for h in range(2)]
-    + ["rows4"]
-    + [f"own{i}" for i in range(5)]
-    + [f"out{i}" for i in range(4)]
+    + [f"m{i}.{h}" for i in range(5) for h in range(2)]
+    + ["w4"]
+    + [f"o{i}" for i in range(5)]
+    + [f"u{i}" for i in range(4)]
     + [f"in{i}" for i in range(11)]
-    + ["own_image", "out_gi", "out_ghc", "out_gnorm", "out_gsmall"]
+    + ["oi", "og", "oh", "on", "os"]
 )
 GROUP = {name: number for number, name in enumerate(GROUPS)}
 
 CLASSES = [
-    "images", "start", "head_out", "a2a", "pool", "dh3", "rs2", "norms", "small_rep", "small_all", "pool_slope",
-    "rows4", "weights", "weights4", "core", "core4", "z", "z4", "ag", "rs", "rs0", "rows", "sums", "norm", "stat",
+    "im", "st", "ho", "a2a", "pl", "d3", "rs2", "ns", "sp", "sa", "ps",
+    "w4", "k", "k4", "c", "c4", "z", "z4", "ag", "rs", "rs0", "w", "s", "n", "t",
 ]
 CLASS = {name: number for number, name in enumerate(CLASSES)}
 
@@ -51,7 +51,7 @@
     if group.startswith("rs0"):
         return CLASS["rs0"]
     name = group.rstrip("xyr0123456789.")
-    if name in ("mid", "z"):
+    if name in ("m", "z"):
         name = "z"
         return CLASS["z4" if group[len(group.split(".")[0]) - 1] == "4" else "z"]
     return CLASS[name]
@@ -98,20 +98,20 @@
         return lambda: ref.at[pl.ds(0, count)]
 
     volume = {
-        "images": first_of(s.at[0], (R - 1) * PD),
-        "own_image": first_of(s.at[0], PD),
-        "start": first_of(start_r, R - 1),
-        "head_out": first_of(ho_r, F - 1),
+        "im": first_of(s.at[0], (R - 1) * PD),
+        "oi": first_of(s.at[0], PD),
+        "st": first_of(start_r, R - 1),
+        "ho": first_of(ho_r, F - 1),
         "a2a": lambda: z4.at[:, pl.ds(0, (R - 1) * CR)],
-        "pool_slope": lambda: sp_all.at[:, :, pl.ds(0, (R - 1) * CR)],
-        "pool": lambda: pool_all.at[:, pl.ds(0, (R - 1) * CR)],
-        "dh3": first_of(a2a_r, R - 1),
+        "ps": lambda: sp_all.at[:, :, pl.ds(0, (R - 1) * CR)],
+        "pl": lambda: pool_all.at[:, pl.ds(0, (R - 1) * CR)],
+        "d3": first_of(a2a_r, R - 1),
         "rs2": first_of(ps_r, R - 1),
-        "norms": lambda: gnorm.at[:, pl.ds(0, (R - 1) * CR)],
-        "small_rep": first_of(rep_r, R - 1),
-        "small_all": first_of(all_r, F - 1),
-        "rows4": first_of(hr, R - 1),
-        "core4": lambda: hcr,
+        "ns": lambda: gnorm.at[:, pl.ds(0, (R - 1) * CR)],
+        "sp": first_of(rep_r, R - 1),
+        "sa": first_of(all_r, F - 1),
+        "w4": first_of(hr, R - 1),
+        "c4": lambda: hcr,
     }
     for j in range(2):
         for way in ("x0", "y1"):
@@ -122,17 +122,17 @@
     volume["rs0x0"] = volume["rs0y1"] = lambda: gi_l.at[0]
     volume["rs0r"] = lambda: gi_l.at[pl.ds(0, 4)]
     for l in range(4):
-        volume[f"rows{l}x0"] = lambda l=l: gather.at[l, pl.ds(0, half), pl.ds(0, CR)]
-        volume[f"rows{l}y1"] = lambda l=l: gather.at[l, pl.ds(half, rows - half), pl.ds(0, CR)]
-        volume[f"rows{l}r"] = lambda l=l: gather.at[l, :, pl.ds(0, (3 if l == 0 and line else 2) * CR)]
+        volume[f"w{l}x0"] = lambda l=l: gather.at[l, pl.ds(0, half), pl.ds(0, CR)]
+        volume[f"w{l}y1"] = lambda l=l: gather.at[l, pl.ds(half, rows - half), pl.ds(0, CR)]
+        volume[f"w{l}r"] = lambda l=l: gather.at[l, :, pl.ds(0, (3 if l == 0 and line else 2) * CR)]
     for j in range(4):
-        volume[f"sums{j}"] = first_of(sums_r.at[j], R - 1)
+        volume[f"s{j}"] = first_of(sums_r.at[j], R - 1)
     for j in range(3):
-        volume[f"norm{j}"] = first_of(nrm_r.at[j], R - 1)
+        volume[f"n{j}"] = first_of(nrm_r.at[j], R - 1)
     for e in range(8):
-        volume[f"stat{e}"] = first_of(st_r.at[e], F - 1)
+        volume[f"t{e}"] = first_of(st_r.at[e], F - 1)
     for l in range(4):
-        volume[f"core{l}"] = lambda l=l: cr.at[l]
+        volume[f"c{l}"] = lambda l=l: cr.at[l]
 
     def wait_for(ref, sem):
         pltpu.make_async_copy(ref, ref, sem).wait()
@@ -153,23 +153,23 @@
     def departed(number):
         name = CLASSES[number]
         whole = {
-            "core": lambda: cr,
-            "core4": lambda: hcr,
+            "c": lambda: cr,
+            "c4": lambda: hcr,
             "z": lambda: zr.at[:, pl.ds(0, Z - 1)],
             "z4": lambda: hzr.at[pl.ds(0, Z - 1)],
             "ag": lambda: zg.at[:, :, pl.ds(0, 3 * CR)],
             "rs": lambda: rs_l,
             "rs0": lambda: gi_l,
-            "rows": lambda: gather.at[:, :, pl.ds(0, 3 * CR)],
-            "sums": lambda: sums_r.at[:, pl.ds(0, R - 1)],
-            "norm": lambda: nrm_r.at[:, pl.ds(0, R - 1)],
-            "stat": lambda: st_r.at[:, pl.ds(0, F - 1)],
+            "w": lambda: gather.at[:, :, pl.ds(0, 3 * CR)],
+            "s": lambda: sums_r.at[:, pl.ds(0, R - 1)],
+            "n": lambda: nrm_r.at[:, pl.ds(0, R - 1)],
+            "t": lambda: st_r.at[:, pl.ds(0, F - 1)],
         }
         sem = ssem.at[number]
-        if name == "weights":
+        if name == "k":
             many = lambda count: lambda: wait_for(wf.at[pl.ds(0, 4), pl.ds(0, count * rows)], sem)
             when_line(many(6), many(8), many(2 * Z - 1))
-        elif name == "weights4":
+        elif name == "k4":
             many = lambda count: lambda: wait_for(hp.at[pl.ds(0, count)], sem)
             when_line(many(6), many(8), many(2 * Z - 1))
         else:
@@ -244,7 +244,7 @@
         return hp.at[owner, pl.ds(first, size)]
 
     def w_copy(l, h, src, owner, to, recv_sem):
-        out = CLASS["weights" if l < 4 else "weights4"]
+        out = CLASS["k" if l < 4 else "k4"]
         leaving[out] = lambda: departed(out)
         return pltpu.make_async_remote_copy(
             src_ref=src, dst_ref=w_block(l, owner, h), send_sem=ssem.at[out], recv_sem=recv_sem, device_id=to,
@@ -252,7 +252,7 @@
         )
 
     def w_to_core(l, h, src, owner):
-        w_copy(l, h, src, owner, sib, rsem.at[GROUP[f"weights{l}"]]).start()
+        w_copy(l, h, src, owner, sib, rsem.at[GROUP[f"k{l}"]]).start()
 
     def w_src(l, h):
         return w_in[l].at[cut_at(l, h), my_lanes] if l < 4 else hw_s.at[cut_at(l, h)]
@@ -271,7 +271,7 @@
             for k in near:
                 w_send(l, h, k)
             w_to_core(l, h, w_src(l, h), f)
-        copy_here(w_in[l].at[:, my_lanes] if l < 4 else hw_s, wf.at[l, block(f)] if l < 4 else hp.at[f], f"own{l}")
+        copy_here(w_in[l].at[:, my_lanes] if l < 4 else hw_s, wf.at[l, block(f)] if l < 4 else hp.at[f], f"o{l}")
 
     def w_push_rest(l, hs=pieces, who=lambda body: body()):
         for h in hs:
@@ -323,15 +323,15 @@
                 when(zc == Z - 1, lambda: w_arrived(l, h, Z - 1))
 
     def w_finish(l):
-        one = GROUP[f"weights{l}"]
+        one = GROUP[f"k{l}"]
         wait_for(wf.at[l, pl.ds(0, Z * rows)] if l < 4 else hp.at[pl.ds(0, Z)], rsem.at[one])
-        wait_recv(f"own{l}")
+        wait_recv(f"o{l}")
 
     w_push_rest(0)
     w_push_near(0)
-    over(R, lambda k: send(images, s.at[0, pl.ds(pl.multiple_of(r * PD, PD), PD)], rep_peer(k), "images"), 1)
+    over(R, lambda k: send(images, s.at[0, pl.ds(pl.multiple_of(r * PD, PD), PD)], rep_peer(k), "im"), 1)
     own_rows = s.at[0, pl.ds(pl.multiple_of(r * PD, PD), PD)]
-    copy_here(images, own_rows, "own_image")
+    copy_here(images, own_rows, "oi")
 
     for i in range(len(small)):
         wait_recv(f"in{i}")
@@ -344,11 +344,11 @@
     lane = lax.broadcasted_iota(jnp.int32, (1, LANES), 1)
     start_s[0:1, :] = sum(jnp.where(lane == t, counted[t : t + 1, :], 0.0) for t in range(3))
     start_s[1:2, 0 : PW // R] = pools
-    over(R, lambda k: send(start_s, start_r.at[r], rep_peer(k), "start"), 1)
+    over(R, lambda k: send(start_s, start_r.at[r], rep_peer(k), "st"), 1)
     start_r[r] = start_s[...]
     ho_s[...] = jnp.zeros_like(ho_s)
     ho_s[0 : d.q, 0 : d.OC] = ho[...].astype(F32)
-    over(F, lambda k: send(ho_s, ho_r.at[f], (r, (f + k) % F), "head_out"), 1)
+    over(F, lambda k: send(ho_s, ho_r.at[f], (r, (f + k) % F), "ho"), 1)
     ho_r[f] = ho_s[...]
     def pack_head():
         wide = -(-rows // LANES) * LANES
@@ -400,7 +400,7 @@
         return pl.ds(pl.multiple_of(i * PIX, PIX), PIX)
 
     def per_image(count, body, init):
-        return lax.fori_loop(0, count, body, init)
+        return lax.fori_loop(0, count, body, init, unroll=True)
 
     def column_of(shape):
         return lax.broadcasted_iota(jnp.int32, shape, 0) & (W - 1)
@@ -540,7 +540,7 @@
         return hg.at[owner, pl.ds(first, size)]
 
     def weight_grad(l, src, height):
-        to_core = lambda k: send(g_block(l, 2 * k + 1 - core), from_core(l).at[k], sib, f"core{l}")
+        to_core = lambda k: send(g_block(l, 2 * k + 1 - core), from_core(l).at[k], sib, f"c{l}")
         sent = 0
         for ky in range(3):
             part = lax.dot_general(
@@ -570,7 +570,7 @@
             over(Z, to_core)
 
     def core_sum(l):
-        wait_recv(f"core{l}")
+        wait_recv(f"c{l}")
 
         def step(k):
             ref = g_block(l, 2 * k + core)
@@ -589,11 +589,11 @@
 
             def to_middle():
                 through, owner = jnp.where(zc == 0, 1, Z - 2), Z - 1 - zc
-                send(g_piece(l, 2 * owner + core, h), from_z(l, through, h), (r, 2 * through + core), f"mid{l}.{h}")
+                send(g_piece(l, 2 * owner + core, h), from_z(l, through, h), (r, 2 * through + core), f"m{l}.{h}")
 
             when(is_end, to_middle)
-            g = GROUP[f"mid{l}.{h}"]
-            arriving[f"mid{l}.{h}"] = lambda: when(
+            g = GROUP[f"m{l}.{h}"]
+            arriving[f"m{l}.{h}"] = lambda: when(
                 jnp.logical_not(is_end), lambda: wait_for(from_z(l, 0, h), rsem.at[g])
             )
 
@@ -617,7 +617,7 @@
 
     def z_middle_piece(l, h):
         if line:
-            wait_recv(f"mid{l}.{h}")
+            wait_recv(f"m{l}.{h}")
 
             def hand_on():
                 owner = (Z - 1) * (Z - 2 - zc)
@@ -640,9 +640,9 @@
         for h in pieces:
             z_sum_piece(l, h)
         if l < 4:
-            gather_start(f"rows{l}", rows_piece(l))
+            gather_start(f"w{l}", rows_piece(l))
         else:
-            over(R, lambda k: send(hr.at[r], hr.at[r], rep_peer(k), "rows4"), 1)
+            over(R, lambda k: send(hr.at[r], hr.at[r], rep_peer(k), "w4"), 1)
 
     def z_sum_piece(l, h):
         wait_recv(f"z{l}.{h}")
@@ -663,10 +663,10 @@
 
     def rows_done(l):
         if l < 4:
-            await_rest(f"rows{l}")
-            copy_here(gather.at[l], gw[l], f"out{l}")
+            await_rest(f"w{l}")
+            copy_here(gather.at[l], gw[l], f"u{l}")
         else:
-            wait_recv("rows4")
+            wait_recv("w4")
             summed = sum(hr[i].astype(F32) for i in range(R))
             wide = -(-half // LANES) * LANES
             if wide > half:
@@ -676,11 +676,11 @@
             ghc[:, half:rows] = summed[d.HC : 2 * d.HC, 0 : rows - half]
 
     def exchange(e):
-        over(F, lambda k: send(st_s.at[e], st_r.at[e, f], (r, (f + k) % F), f"stat{e}"), 1)
+        over(F, lambda k: send(st_s.at[e], st_r.at[e, f], (r, (f + k) % F), f"t{e}"), 1)
         st_r[e, f] = st_s[e]
 
     def exchanged(e):
-        wait_recv(f"stat{e}")
+        wait_recv(f"t{e}")
         return st_r[e]
 
     st_s[...] = jnp.zeros_like(st_s)
@@ -688,9 +688,9 @@
     w_relay_near(0)
     w_far(0)
     w_push_rest(1, who=at_ends)
-    wait_recv("images")
-    wait_recv("own_image")
-    wait_recv("start")
+    wait_recv("im")
+    wait_recv("oi")
+    wait_recv("st")
 
     rep_all = lambda src, dst, group: over(R, lambda k: send(src, dst, rep_peer(k), group), 1)
     images_here = M // PIX
@@ -739,12 +739,12 @@
         for k in range(2):
             sp_own[k] = averaged[:, k * CR : (k + 1) * CR]
             sp_all[k, :, my_lanes] = averaged[:, k * CR : (k + 1) * CR]
-        rep_all(sp_own, sp_all.at[:, :, my_lanes], "pool_slope")
+        rep_all(sp_own, sp_all.at[:, :, my_lanes], "ps")
 
     for l in range(4):
         w_finish(l)
         if l == 2:
-            wait_recv("pool")
+            wait_recv("pl")
             s[2] = jnp.dot(u_sel[...], pool_all[...], preferred_element_type=F32).astype(BF16)
         first = conv(s.at[l], images_here, l, zb)
         mean_here = first * (1.0 / M)
@@ -803,7 +803,7 @@
             nrm_s[j, 1:2, :] = off * g_row + b_row
             nrm_s[j, 2:3, :] = inverse
             nrm_s[j, 3:4, :] = off
-            rep_all(nrm_s.at[j], nrm_r.at[j, r], f"norm{j}")
+            rep_all(nrm_s.at[j], nrm_r.at[j, r], f"n{j}")
             nrm_r[j, r] = nrm_s[j]
 
         def activate(i, carry):
@@ -834,7 +834,7 @@
             )
             pool_own[...] = pooled.astype(BF16)
             pool_all[:, my_lanes] = pooled.astype(BF16)
-            rep_all(pool_own, pool_all.at[:, my_lanes], "pool")
+            rep_all(pool_own, pool_all.at[:, my_lanes], "pl")
             w_relay_rest(2, pieces[1:])
             pool_slopes()
             slopes_of(0)
@@ -850,7 +850,7 @@
             w_push_rest(4)
         w_far(l + 1)
         if gathers:
-            wait_recv(f"norm{j}")
+            wait_recv(f"n{j}")
             await_rest(f"ag{l}")
             per_image(images_here, activate_all, 0)
 
@@ -866,7 +866,7 @@
         return carry
 
     lax.fori_loop(0, F, unpack, 0)
-    wait_recv("norm2")
+    wait_recv("n2")
     wait_recv("a2a")
 
     def activate_own(i, carry):
@@ -884,7 +884,7 @@
         return carry
 
     per_image(PD // PIX, activate_own, 0)
-    wait_recv("head_out")
+    wait_recv("ho")
     conv(s4, PD // PIX, 4, zb)
     head_bias = jnp.concatenate([hb[...], jnp.zeros((1, CR - d.HC), F32)], axis=1)
     out_bias = jnp.concatenate([ob[...], jnp.zeros((1, CR - d.OC), F32)], axis=1)
@@ -933,11 +933,11 @@
         sums_s[j, n, 1:2, :] = jnp.sum(grad * steep_z.astype(F32), axis=0, keepdims=True)
 
     def send_sums(j):
-        over(R, lambda k: send(sums_s.at[j, (r + k) % R], sums_r.at[j, r], rep_peer(k), f"sums{j}"), 1)
+        over(R, lambda k: send(sums_s.at[j, (r + k) % R], sums_r.at[j, r], rep_peer(k), f"s{j}"), 1)
         sums_r[j, r] = sums_s[j, r]
 
     def pass_sums(j, e):
-        wait_recv(f"sums{j}")
+        wait_recv(f"s{j}")
         st_s[e, 0:2, :] = sum(sums_r[j, i, 0:2, :] for i in range(R))
         exchange(e)
 
@@ -952,7 +952,7 @@
     wait_send("a2a")
     data_grad(4, PD, write_dh3)
     send_sums(2)
-    over(R, lambda k: send(a2a_s.at[(r + k) % R], a2a_r.at[r], rep_peer(k), "dh3"), 1)
+    over(R, lambda k: send(a2a_s.at[(r + k) % R], a2a_r.at[r], rep_peer(k), "d3"), 1)
     a2a_r[r] = a2a_s[r]
     weight_grad(4, s4, PD)
     head_act, grad_out = y[0:PD, 0:CR], y[0:PD, CR : 2 * CR]
@@ -962,18 +962,18 @@
     rep_s[d.HC : d.HC + 8, :] = jnp.zeros((8, LANES), F32)
     rep_s[d.HC : d.HC + 1, :] = jnp.sum(zb[0:PD, :], axis=0, keepdims=True)
     rep_s[d.HC + 1 : d.HC + 2, :] = jnp.sum(grad_out, axis=0, keepdims=True)
-    over(R, lambda k: send(rep_s, rep_r.at[r], rep_peer(k), "small_rep"), 1)
+    over(R, lambda k: send(rep_s, rep_r.at[r], rep_peer(k), "sp"), 1)
     rep_r[r] = rep_s[...]
 
     def head_small():
-        wait_recv("small_rep")
+        wait_recv("sp")
         summed = sum(rep_r[i] for i in range(R))
         for i in range(F):
             all_s[i, 0 : d.q, :] = summed[i * d.q : (i + 1) * d.q]
             if d.q < 8:
                 all_s[i, d.q : 8, :] = jnp.zeros((8 - d.q, LANES), F32)
             all_s[i, 8:16, :] = summed[d.HC : d.HC + 8]
-        over(F, lambda k: send(all_s.at[(f + k) % F], all_r.at[f], (r, (f + k) % F), "small_all"), 1)
+        over(F, lambda k: send(all_s.at[(f + k) % F], all_r.at[f], (r, (f + k) % F), "sa"), 1)
         all_r[f] = all_s[f]
 
     def through_norm(l, grad_of):
@@ -985,7 +985,7 @@
         if l in (0, 2):
             await_rest(f"rs{l + 1}")
         elif l == 3:
-            wait_recv("dh3")
+            wait_recv("d3")
 
         def body(i, carry):
             at = image_rows(i)
@@ -1058,7 +1058,7 @@
             ps_s[n] = grad.astype(BF16)
             put_sums(3, n, grad, sp_all[0, :, cols], sp_all[1, :, cols])
 
-    wait_recv("pool_slope")
+    wait_recv("ps")
     data_grad(2, M, write_pooled)
     send_sums(3)
     z_middle(3)
@@ -1082,7 +1082,7 @@
     z_sum(3)
     core_sum(1)
     z_push(1)
-    gather_forward("rows3", rows_piece(3))
+    gather_forward("w3", rows_piece(3))
     z_sum(2)
 
     through_norm(0, from_scatter(0))
@@ -1093,46 +1093,46 @@
     data_grad(0, M, write_images)
     scatter_start("rs0", gi_piece, gi_land)
     weight_grad(0, s.at[0], M)
-    gather_forward("rows2", rows_piece(2))
+    gather_forward("w2", rows_piece(2))
     z_middle(1)
     core_sum(0)
     z_push(0)
 
     gnorm[:, my_lanes] = norm_s[...]
-    rep_all(norm_s, gnorm.at[:, my_lanes], "norms")
+    rep_all(norm_s, gnorm.at[:, my_lanes], "ns")
     z_middle(0)
     scatter_forward("rs0", gi_piece, gi_land)
     z_sum(1)
-    wait_recv("small_all")
+    wait_recv("sa")
     gsmall[...] = jnp.sum(all_r[...], axis=0) * (1.0 / root)
     rows_done(4)
-    copy_here(ghc, small_out[0], "out_ghc")
-    copy_here(gsmall, small_out[2], "out_gsmall")
+    copy_here(ghc, small_out[0], "oh")
+    copy_here(gsmall, small_out[2], "os")
     rows_done(3)
-    gather_forward("rows1", rows_piece(1))
+    gather_forward("w1", rows_piece(1))
     rows_done(2)
     await_rest("rs0")
     for h in range(2):
         at = slice(h * (PD // 2), (h + 1) * (PD // 2))
         gi[at, :] = gi_s[r, at, :].astype(F32) + gi_l[1 + 2 * h].astype(F32) + gi_l[4 + h].astype(F32)
-    copy_here(gi, gi_out, "out_gi")
-    wait_recv("norms")
-    copy_here(gnorm, small_out[1], "out_gnorm")
+    copy_here(gi, gi_out, "og")
+    wait_recv("ns")
+    copy_here(gnorm, small_out[1], "on")
     last = rows_piece(0)
     if d.pieces == 2:
         z_sum_piece(0, 0)
-        send(last(r, 0), last(r, 0), at_one, "rows0r")
-        send(last(r, 0), last(r, 0), at_two, "rows0r")
-        send(last(r, 0), last(r, 0), (both, f), "rows0r")
+        send(last(r, 0), last(r, 0), at_one, "w0r")
+        send(last(r, 0), last(r, 0), at_two, "w0r")
+        send(last(r, 0), last(r, 0), (both, f), "w0r")
         rows_done(1)
         z_sum_piece(0, 1)
-        send(last(r, 1), last(r, 1), at_one, "rows0r")
-        send(last(r, 1), last(r, 1), at_two, "rows0r")
-        send(last(r, 1), last(r, 1), (both, f), "rows0r")
+        send(last(r, 1), last(r, 1), at_one, "w0r")
+        send(last(r, 1), last(r, 1), at_two, "w0r")
+        send(last(r, 1), last(r, 1), (both, f), "w0r")
     else:
         z_sum(0)
         rows_done(1)
-        gather_forward("rows0", last)
+        gather_forward("w0", last)
     rows_done(0)
 
     drain()

time: 142 us -> 140 us (0.986)
  Pallas kernels: 141 us -> 139 us
    pallas_call x1, Pallas kernels: 136 us -> 135 us  [per_device(): pl.pallas_call(functools.partial(kernel, d), out_shape=[shape((d.PD, d.C)...]
where the time goes in v8:
time: 140 us
  Pallas kernels  139 us (99%)
    pallas_call x1, Pallas kernels, per_device(): pl.pallas_call(functools.partial(kernel, d), out_shape=[shape((d.PD, d.C)...  135 us
    pallas_call x1, Pallas kernels, per_device(): pl.pallas_call(finish, grid=(steps,), out_shape=[shape((d.PD, channels),...  4.15 us

profile of v8, /device:TPU:0, one launch (start us, length us, event | category | flops | bytes accessed | tf_op | source)
XLA Modules:
  0.0 139.8 jit_solution(9355867840872375673)
XLA Ops:
  0.7 134.8 %shard_map.239 = (f32[192,512]{1,0:T(8,128)}, bf16[576,512]{1,0:T(8,128)(2,1)}, bf16[576,512]{1,0:T(8,128)(2,1)}, bf16[576,512]{1,0:T(8,128)(2,1)}, bf16[576,512...) custom-call(bf16[192,512]{1,0:T(8,128)(2,1)} %bitcast.10, bf16[576,512]{1,0:T(8,128)(2,1)} %refs_1_.1, ...), custom_call_target="tpu_custom_call" | custom-call | tf_op jit(solution)/shard_map/pallas_call | solution.py:1247
  135.5 4.1 %shard_map.240 = (f32[192,512]{1,0:T(8,128)}, f32[576,512]{1,0:T(8,128)}, f32[576,512]{1,0:T(8,128)}, f32[576,512]{1,0:T(8,128)}, f32[576,512]{1,0:T(8,128)}, /*...) custom-call(f32[192,512]{1,0:T(8,128)} %get-tuple-element.30.gi, ...), custom_call_target="tpu_custom_call" | custom-call | tf_op jit(solution)/shard_map/pallas_call | solution.py:1265
